TPU v7x, 128 devices: a whole 4x4x4 slice. The times are simulated.
128 devices in a mesh: gx: 4 (over x), gy: 32 (over z, y, core).
Axes of the slice: x: 4, y: 4, z: 4, core: 2. Of those that a mesh axis runs over, the one named last changes fastest.
Arguments:
- a_tiles: float32 [6144, 3, 128, 128], P(('gx', 'gy')), may hold values from -0.5 to 0.5
- a_cols: int32 [6144, 3], P(('gx', 'gy')), may hold values from 0 to 6143, as said below
- a_len: int32 [6144], P(('gx', 'gy')), may hold values from 1 to 3, as said below
- p_tiles: float32 [6144, 2, 128, 128], P(('gx', 'gy')), may hold values from -1 to 1
- aggregate: int32 [6144], replicated, may hold values from 0 to 2047, as said below
- owner: int32 [2048], replicated, may hold values from 0 to 127, as said below
Outputs:
- coarse_operator: float32 [2048, 7, 128, 128], P(('gx', 'gy'))
Inputs may be any that keep to these rules, and one draw needn't show every extreme that they name: For k < a_len[i] the a_cols[i, k] are distinct among i - 1, i, i + 1 modulo 6144, the first being i; the later slots hold the remaining ones of these and belong to no operator. a_len[i] = 3 where i mod 48 is 0 or 47. aggregate[i] is i // 3 or i // 3 - 1, modulo 2048. The owner of row r of the 16 coarse rows of the device at (x, y) is the device at ((x + u[r]) mod 4, (v[y] + t[r]) mod 32), where u takes each value 16 // 4 times, v is a permutation and t takes no value more than 1 times, that many in every draw; each device owns exactly 16 coarse rows.
All inputs are finite; a program needn't handle non-finite values.
Results may differ from a plain program's by a relative error of at most 0.0003.
Values sent between devices are 32-bit elements; how exact they have to be, the bound alone decides.
No kernel may reach another device: no remote copies, remote signals or barrier semaphores. Data moves between devices by JAX's collectives and lax.ppermute only.
A program may use at most 192 MiB of HBM per device.

v0:
```python
import functools

import jax
import jax.numpy as jnp
from jax import lax
from jax.experimental import pallas as pl
from jax.experimental.pallas import tpu as pltpu
from jax.sharding import PartitionSpec as P

B = 128
KP = 2
LANES = 128
CWIN = 7
W = 6
BF = jnp.bfloat16
F32 = jnp.float32
SMEM = pltpu.SMEM
ANYWHERE = pl.BlockSpec(memory_space=pl.ANY)
VMEM = pltpu.VMEM


LEFT, OUT_LEFT, OUT_RIGHT, CODE, PLAN = 64, 128, 192, 256, 384


def split(x):
    high = x.astype(BF)
    return high, (x - high.astype(F32)).astype(BF)


def left_operand(x):
    high, low = split(x)
    return jnp.concatenate([high, low, high], axis=1)


def right_operand(x):
    high, low = split(x)
    return jnp.concatenate([high, high, low], axis=0)


def matmul(left, right):
    return jnp.dot(left, right, preferred_element_type=F32)


def spread(total, flag, base, pair, slots):
    first, second = pair
    values = {
        base - 1: jnp.where(flag, first, 0.0),
        base: jnp.where(flag, second, first),
        base + 1: jnp.where(flag, 0.0, second),
    }
    for s, value in values.items():
        if s in slots:
            total[s] = value if total.get(s) is None else total[s] + value


def row_product(p_pair, tiles):
    turned = jnp.concatenate([p_pair[0].T, p_pair[1].T], axis=0)
    return matmul(left_operand(turned), right_operand(jnp.concatenate(tiles, axis=1)))


SLOTS = {0: (0, 1, 2, 3), 1: (1, 2, 3), 2: (1, 2, 3, 4)}


def main_kernel(
    plan,
    a_ref, p_ref, before_ref, after_ref,
    out,
    stage, carry, sems,
):
    step = pl.program_id(0)
    steps = pl.num_programs(0) - 1
    buf = lax.rem(step, 2)

    def copy_out(at, which, row):
        c = 2 * at - 1 + row
        return pltpu.make_async_copy(stage.at[which, row], out.at[c], sems.at[which, row])

    def drain(at):
        which = lax.rem(at, 2)
        for row in range(2):
            @pl.when((2 * at - 1 + row >= 0) & (2 * at - 1 + row < 2 * steps))
            def _():
                copy_out(at, which, row).wait()

    @pl.when(step >= 2)
    def _():
        drain(step - 2)

    @pl.when(step == 0)
    def _():
        carry[...] = jnp.zeros_like(carry)

    stage[buf, 0] = carry[0]
    stage[buf, 1] = carry[1]

    @pl.when(step < steps)
    def _():
        carry[...] = jnp.zeros_like(carry)
        first = step * W
        flags = {q: plan[first + q + 4] > 0 for q in range(-1, W + 1)}

        def p_tile(q, m):
            if q < 0:
                return before_ref[0, m]
            if q >= W:
                return after_ref[0, m]
            return p_ref[q, m]

        lefts = {}
        for r in range(W):
            tiles = {
                0: jnp.where(plan[OUT_LEFT + first + r] > 0, a_ref[r, plan[LEFT + first + r]], 0.0),
                1: a_ref[r, 0],
                2: jnp.where(plan[OUT_RIGHT + first + r] > 0, a_ref[r, 3 - plan[LEFT + first + r]], 0.0),
            }
            for k in range(3):
                lefts[r, r + k - 1] = left_operand(tiles[k])
        total = {r: {} for r in range(W)}
        for q in range(-1, W + 1):
            rows = [r for r in (q - 1, q, q + 1) if 0 <= r < W]
            right = right_operand(jnp.concatenate([p_tile(q, 0), p_tile(q, 1)], axis=1))
            product = matmul(jnp.concatenate([lefts[r, q] for r in rows], axis=0), right)
            for n, r in enumerate(rows):
                pair = (product[n * B : (n + 1) * B, :B], product[n * B : (n + 1) * B, B:])
                spread(total[r], flags[q], q // 3 - r // 3 + 2, pair, SLOTS[r % 3])
        for r in range(W):
            slots = SLOTS[r % 3]
            product = row_product((p_ref[r, 0], p_ref[r, 1]), [total[r][s] for s in slots])
            g = r // 3
            for n, s in enumerate(slots):
                one = product[:B, n * B : (n + 1) * B]
                two = product[B:, n * B : (n + 1) * B]
                for delta, value in (
                    (-1, jnp.where(flags[r], one, 0.0)),
                    (0, jnp.where(flags[r], two, one)),
                    (1, jnp.where(flags[r], 0.0, two)),
                ):
                    place = g + delta + 1
                    if place < 2:
                        stage[buf, place, s + 1 - delta] += value
                    else:
                        carry[place - 2, s + 1 - delta] += value

    for row in range(2):
        @pl.when((2 * step - 1 + row >= 0) & (2 * step - 1 + row < 2 * steps))
        def _():
            copy_out(step, buf, row).start()

    @pl.when(step == steps)
    def _():
        drain(step - 1)
        drain(step)


def main_product(plan, a_tiles, p_tiles):
    rows = a_tiles.shape[0]
    steps = rows // W
    coarse = rows // 3
    last = steps - 1

    def spec(shape, index):
        return pl.BlockSpec(shape, index)

    return pl.pallas_call(
        main_kernel,
        grid_spec=pltpu.PrefetchScalarGridSpec(
            num_scalar_prefetch=1,
            grid=(steps + 1,),
            in_specs=[
                spec((W, 3, B, B), lambda s, *_: (jnp.minimum(s, last), 0, 0, 0)),
                spec((W, KP, B, B), lambda s, *_: (jnp.minimum(s, last), 0, 0, 0)),
                spec((1, KP, B, B), lambda s, *_: (jnp.maximum(jnp.minimum(s, last) * W - 1, 0), 0, 0, 0)),
                spec((1, KP, B, B), lambda s, *_: (jnp.minimum(s * W + W, rows - 1), 0, 0, 0)),
            ],
            out_specs=pl.BlockSpec(memory_space=pl.ANY),
            scratch_shapes=[
                VMEM((2, 2, CWIN, B, B), F32),
                VMEM((2, CWIN, B, B), F32),
                pltpu.SemaphoreType.DMA((2, 2)),
            ],
        ),
        out_shape=jax.ShapeDtypeStruct((coarse, CWIN, B, B), F32),
        compiler_params=pltpu.CompilerParams(
            dimension_semantics=("arbitrary",), vmem_limit_bytes=56 << 20
        ),
        cost_estimate=pl.CostEstimate(
            flops=16_000_000_000, bytes_accessed=24_000_000, transcendentals=0
        ),
        name="triple_product",
    )(plan, a_tiles, p_tiles, p_tiles, p_tiles)


def edge_kernel(
    plan,
    before, after, a_first, a_last, p_first, p_last, in_rows,
    out_rows,
    rows_ref, sems,
):
    coarse = out_rows.shape[0]
    held = (0, 1, coarse - 2, coarse - 1)

    def copy(n, back):
        there, here = out_rows.at[held[n]], rows_ref.at[n]
        if back:
            return pltpu.make_async_copy(here, there, sems.at[n])
        return pltpu.make_async_copy(there, here, sems.at[n])

    for n in range(4):
        copy(n, False).start()

    sums = []
    for side in range(2):
        halo = (before, after)[side]
        a_edge = (a_first, a_last)[side]
        own_p = (p_first, p_last)[side]
        own_flag = plan[(4, 3 * coarse + 3)[side]] > 0
        flags, tiles, p_at = {}, {}, {}
        for n in range(4):
            q = n - 1 if side == 0 else n
            flags[q] = plan[(0, 3 * coarse + 4)[side] + n] > 0
            p_at[q] = (halo[9 + 2 * n], halo[10 + 2 * n])
        near = 3 if side == 0 else -1
        flags[near] = own_flag
        p_at[near] = (own_p[0, 0], own_p[0, 1])
        total = {r: {} for r in range(3)}
        total[near] = {}
        for q in range(-1, 4):
            rows = [r for r in (q - 1, q, q + 1) if 0 <= r < 3]
            lefts = [left_operand(halo[3 * r + q - r + 1]) for r in rows]
            if q == (2 if side == 0 else 0):
                rows.append(near)
                lefts.append(left_operand(a_edge[0]))
            right = right_operand(jnp.concatenate(p_at[q], axis=1))
            product = matmul(jnp.concatenate(lefts, axis=0), right)
            for n, r in enumerate(rows):
                pair = (product[n * B : (n + 1) * B, :B], product[n * B : (n + 1) * B, B:])
                base = q // 3 - r // 3 + 2
                slots = SLOTS[r % 3] if r != near else (base - 1, base, base + 1)
                spread(total[r], flags[q], base, pair, slots)
        outer, inner = {}, {}

        def put(target, w, value):
            target[w] = value if w not in target else target[w] + value

        for r in range(3):
            slots = sorted(total[r])
            pick = 1 if side == 0 else 0
            turned = left_operand(p_at[r][pick].T)
            product = matmul(turned, right_operand(jnp.concatenate([total[r][s] for s in slots], axis=1)))
            for n, s in enumerate(slots):
                value = product[:, n * B : (n + 1) * B]
                if side == 0:
                    put(outer, s, jnp.where(flags[r], 0.0, value))
                else:
                    put(outer, s + 2, jnp.where(flags[r], value, 0.0))
        slots = sorted(total[near])
        product = row_product(p_at[near], [total[near][s] for s in slots])
        for n, s in enumerate(slots):
            one = product[:B, n * B : (n + 1) * B]
            two = product[B:, n * B : (n + 1) * B]
            put(outer, s + 1, jnp.where(own_flag, two, one))
            if side == 0:
                put(inner, s, jnp.where(own_flag, 0.0, two))
            else:
                put(inner, s + 2, jnp.where(own_flag, one, 0.0))
        sums.append((outer, inner))

    for n in range(4):
        copy(n, False).wait()
    for n, target in ((0, sums[0][0]), (1, sums[0][1]), (2, sums[1][1]), (3, sums[1][0])):
        for w, value in target.items():
            rows_ref[n, w] += value
    for n in range(4):
        copy(n, True).start()
    for n in range(4):
        copy(n, True).wait()


def edge_product(plan, before, after, up, down, p_tiles, out_rows):
    rows = p_tiles.shape[0]

    def whole(x):
        return pl.BlockSpec(x.shape, lambda *_: (0,) * x.ndim)

    anywhere = pl.BlockSpec(memory_space=pl.ANY)
    return pl.pallas_call(
        edge_kernel,
        grid_spec=pltpu.PrefetchScalarGridSpec(
            num_scalar_prefetch=1,
            grid=(1,),
            in_specs=[whole(before), whole(after)]
            + [
                pl.BlockSpec((1, B, B), lambda *_: (0, 0, 0)),
                pl.BlockSpec((1, B, B), lambda *_: (8, 0, 0)),
                pl.BlockSpec((1, KP, B, B), lambda *_: (0, 0, 0, 0)),
                pl.BlockSpec((1, KP, B, B), lambda *_: (rows - 1, 0, 0, 0)),
                anywhere,
            ],
            out_specs=anywhere,
            scratch_shapes=[VMEM((4, CWIN, B, B), F32), pltpu.SemaphoreType.DMA((4,))],
        ),
        out_shape=jax.ShapeDtypeStruct(out_rows.shape, F32),
        input_output_aliases={7: 0},
        compiler_params=pltpu.CompilerParams(
            dimension_semantics=("arbitrary",), vmem_limit_bytes=56 << 20
        ),
        cost_estimate=pl.CostEstimate(flops=2_000_000_000, bytes_accessed=10_000_000, transcendentals=0),
        name="edge_rows",
    )(plan, before, after, down, up, p_tiles, p_tiles, out_rows)


def plan_kernel(place, cols, length, a_tiles, p_tiles, aggregate, owners, owners_all, plan, counts, up, down, low, high, near, mine_ref, sem):
    fine, coarse = length.shape[0], counts.shape[0]
    wide = aggregate.shape[0]
    fine_total = wide * LANES
    first = place[0] * fine
    line = jnp.where(first < 4, wide - 1, (first - 4) >> 7)
    begin = jnp.where(first < 4, LANES - 4, (first - 4) & (LANES - 1))
    lines = (line, jnp.where(line == wide - 1, 0, line + 1))
    index_loads = [
        pltpu.make_async_copy(aggregate.at[pl.ds(at, 1)], near.at[pl.ds(n, 1)], sem.at[n]) for n, at in enumerate(lines)
    ]
    index_loads.append(
        pltpu.make_async_copy(owners.at[pl.ds((place[0] * coarse) >> 7, 1)], mine_ref, sem.at[2])
    )
    for load in index_loads:
        load.start()

    def entry(i):
        before = first + i - 1
        before = jnp.where(before < 0, fine_total - 1, before)
        left = jnp.where(cols[1, i] == before, 1, 2)
        return left, length[i] > left, length[i] > 3 - left

    sends = []
    for out, row, p_row in ((up, fine - 3, fine - 4), (down, 0, 0)):
        for r in range(3):
            left, on_left, on_right = entry(row + r)
            for k, slot, on in ((0, left, on_left), (2, 3 - left, on_right)):
                sends.append((a_tiles.at[row + r, slot], out.at[3 * r + k], on))
            sends.append((a_tiles.at[row + r, 0], out.at[3 * r + 1], None))
        for n in range(4):
            for m in range(KP):
                sends.append((p_tiles.at[p_row + n, m], out.at[9 + 2 * n + m], None))
    for k, (here, there, on) in enumerate(sends):
        if on is None:
            pltpu.make_async_copy(here, there, sem.at[3 + k]).start()
        else:

            @pl.when(on)
            def _():
                pltpu.make_async_copy(here, there, sem.at[3 + k]).start()

            @pl.when(jnp.logical_not(on))
            def _():
                there[...] = jnp.zeros(there.shape, F32)

    def flag(k, carry):
        row = first + k - 4
        row = jnp.where(row < 0, row + fine_total, jnp.where(row >= fine_total, row - fine_total, row))
        at = begin + k
        plan[k] = jnp.where(near[at >> 7, at & (LANES - 1)] != lax.div(row, 3), 1, 0)
        return carry

    for load in index_loads:
        load.wait()
    lax.fori_loop(0, fine + 8, flag, 0, unroll=8)

    def bounds(k, mod, on_left, on_right):
        here = 2 - plan[k + 1]
        left = jnp.where(on_left, (1 if mod == 0 else 2) - plan[k], here)
        right = jnp.where(on_right, (3 if mod == 2 else 2) - plan[k + 2], here)
        low[k] = jnp.minimum(here, jnp.minimum(left, right))
        high[k] = 1 + jnp.maximum(here, jnp.maximum(left, right))

    for mod in range(3):
        bounds(mod, mod, True, True)
        bounds(fine + 3 + mod, mod, True, True)

    def group(g, carry):
        for mod in range(3):
            i = 3 * g + mod
            left, on_left, on_right = entry(i)
            plan[LEFT + i] = left
            plan[OUT_LEFT + i] = jnp.where(on_left & (i > 0), 1, 0)
            plan[OUT_RIGHT + i] = jnp.where(on_right & (i < fine - 1), 1, 0)
            bounds(i + 3, mod, on_left, on_right)
        return carry

    lax.fori_loop(0, coarse, group, 0, unroll=4)
    ids = lax.broadcasted_iota(jnp.int32, counts.shape, 0) * LANES + lax.broadcasted_iota(
        jnp.int32, counts.shape, 1
    )
    everyone = owners_all[...]

    def code(c, carry):
        least, most = jnp.int32(9), jnp.int32(-9)
        for mod in range(3):
            at = 3 * c + mod
            past, next_ = plan[at + 1] == 0, plan[at + 7] == 1
            least = jnp.minimum(least, low[at + 3] + 1)
            most = jnp.maximum(most, high[at + 3] + 1)
            least = jnp.minimum(least, jnp.where(past, low[at], 9))
            most = jnp.maximum(most, jnp.where(past, high[at], -9))
            least = jnp.minimum(least, jnp.where(next_, low[at + 6] + 2, 9))
            most = jnp.maximum(most, jnp.where(next_, high[at + 6] + 2, -9))
        row = place[0] * coarse + c
        mine = mine_ref[0, row & (LANES - 1)]
        spot = jnp.sum(jnp.where((everyone == mine) & (ids < row), 1, 0))
        tiles = most - least + 1
        plan[CODE + c] = mine * 1024 + spot * 64 + least * 8 + tiles
        return jnp.where(ids == row, tiles, carry)

    tiles = lax.fori_loop(0, coarse, code, jnp.zeros(counts.shape, jnp.int32), unroll=4)
    counts[...] = tiles.astype(F32)
    for k, (here, there, on) in enumerate(sends):
        if on is None:
            pltpu.make_async_copy(here, there, sem.at[3 + k]).wait()
        else:

            @pl.when(on)
            def _():
                pltpu.make_async_copy(here, there, sem.at[3 + k]).wait()


def make_plan(place, a_cols, a_len, aggregate, owner, a_tiles, p_tiles):
    fine = a_len.shape[0]
    coarse = fine // 3
    owners = owner.reshape(-1, LANES)

    def whole(shape):
        return pl.BlockSpec(shape, lambda *_: (0,) * len(shape))

    halo = (9 + 4 * KP, B, B)
    return pl.pallas_call(
        plan_kernel,
        grid_spec=pltpu.PrefetchScalarGridSpec(
            num_scalar_prefetch=3,
            grid=(1,),
            in_specs=[ANYWHERE] * 4 + [whole(owners.shape)],
            out_specs=[
                pl.BlockSpec(memory_space=SMEM),
                whole((coarse, LANES)),
                whole(halo),
                whole(halo),
            ],
            scratch_shapes=[
                SMEM((fine + 6,), jnp.int32),
                SMEM((fine + 6,), jnp.int32),
                SMEM((2, LANES), jnp.int32),
                SMEM((1, LANES), jnp.int32),
                pltpu.SemaphoreType.DMA((3 + 2 * halo[0],)),
            ],
        ),
        out_shape=[
            jax.ShapeDtypeStruct((PLAN,), jnp.int32),
            jax.ShapeDtypeStruct((coarse, LANES), F32),
            jax.ShapeDtypeStruct(halo, F32),
            jax.ShapeDtypeStruct(halo, F32),
        ],
        compiler_params=pltpu.CompilerParams(vmem_limit_bytes=32 << 20),
        cost_estimate=pl.CostEstimate(flops=0, bytes_accessed=5_000_000, transcendentals=0),
        name="plan",
    )(place, a_cols.T, a_len, a_tiles, p_tiles, aggregate.reshape(-1, LANES), owners, owners)


PARTS = (
    (0, 48, "xyz", ((37, 14, 48), (46, 24, 48), (54, 24, 48))),
    (48, 40, "yzx", ((49, 24, 48), (54, 24, 48), (50, 24, 48))),
    (88, 40, "zxy", ((47, 24, 48), (64, 32, 64), (53, 24, 48))),
)
SWAP = 67
SHIFT = {"x": 5, "z": 3, "y": 1}
FRONTS, BACKS = LANES - 2, LANES - 1
TABLE = pl.ds(8, 16)


def fields(code):
    return code >> 10, (code >> 6) & 15, (code >> 3) & 7, code & 7


def start_tiles(count, source, target, sem):
    for size in (4, 2, 1):
        first = count & (8 - 2 * size)

        @pl.when((count & size) != 0)
        def _():
            pltpu.make_async_copy(source(first, size), target(first, size), sem).start()


def wait_tiles(count, one, sem):
    def step(_, carry):
        pltpu.make_async_copy(one, one, sem).wait()
        return carry

    lax.fori_loop(0, count, step, 0)


class Rows:
    def __init__(self, codes, ref, first, height):
        self.codes, self.ref, self.first, self.height = codes, ref, first, height

    def walk(self, body):
        def step(k, carry):
            code = self.codes[CODE + k]
            tile = fields(code)[2]
            part = pl.ds(self.first, self.height)
            body(code, lambda at, size: self.ref.at[k, pl.ds(tile + at, size), part])
            return carry

        lax.fori_loop(0, self.ref.shape[0], step, 0)


class Slots:
    def __init__(self, header, ref, back):
        self.header, self.ref, self.back = header, ref, back

    def walk(self, body):
        def step(k, at):
            lane = FRONTS - 1 - k if self.back else k
            code = self.header[0, lane].astype(jnp.int32)
            count = code & 7
            slot = at - count if self.back else at
            body(code, lambda first, size: self.ref.at[pl.ds(slot + first, size)])
            return slot if self.back else slot + count

        entries = self.header[0, BACKS if self.back else FRONTS].astype(jnp.int32)
        lax.fori_loop(0, entries, step, self.ref.shape[0] if self.back else 1)


def read_headers(pairs, sem):
    copies = [pltpu.make_async_copy(ref.at[0, pl.ds(0, 1)], header, sem.at[k]) for k, (ref, header) in enumerate(pairs)]
    for copy in copies:
        copy.start()
    for copy in copies:
        copy.wait()


def read_table(arrivals, table_in, sem):
    copies = [pltpu.make_async_copy(x.at[0, TABLE], table_in.at[k], sem.at[k]) for k, x in enumerate(arrivals)]
    for copy in copies:
        copy.start()

    def finish():
        for copy in copies:
            copy.wait()
        table = table_in[0]
        for k in range(1, len(copies)):
            table = jnp.maximum(table, table_in[k])
        return table

    return finish


def route_kernel(stage, plan, place, *refs):
    refs = list(refs)
    parts = len(PARTS)
    if stage == 0:
        arrivals = [[refs.pop(0)]] * parts
        counts = refs.pop(0)
    else:
        arrivals = [[refs.pop(0) for _ in range(5)] for _ in range(parts)]
    outs_of = [[refs.pop(0) for _ in range(3)] for _ in range(parts)]
    bufs = [refs.pop(0) for _ in range(parts)]
    state, copy_sem, head_sem, out_sem, table_in, table_out, table_sem = [refs.pop(0) for _ in range(7)]
    heads = [[refs.pop(0) for _ in range(3)] for _ in range(parts)]
    odd = (place[0] & 1) == 1
    if stage > 0:
        came = [[refs.pop(0) for _ in range(5)] for _ in range(parts)]
        finish = read_table(arrivals[0], table_in, table_sem)
        read_headers([(arrivals[p][k], came[p][k]) for p in range(parts) for k in range(5)], head_sem)
        table_out[...] = finish()
    else:
        load = pltpu.make_async_copy(counts, table_out, head_sem.at[0])
        load.start()
        load.wait()
    tables = [
        pltpu.make_async_copy(table_out, outs_of[0][way].at[0, TABLE], out_sem.at[9 * parts + way]) for way in range(3)
    ]
    for table in tables:
        table.start()
    writes, kept = [], []

    def write_out(p):
        send, _, stay = PARTS[p][3][stage]
        buf, head, outs, zero = bufs[p], heads[p], outs_of[p], 16 * p
        wait_tiles(state[zero + 15], buf.at[0], copy_sem.at[p])
        fresh = [
            pltpu.make_async_copy(head[way], outs[way].at[0, pl.ds(0, 1)], out_sem.at[9 * p + way]) for way in range(3)
        ]
        for way in range(2):
            fresh.append(
                pltpu.make_async_copy(
                    buf.at[pl.ds(way * (send + 1) + 1, send)],
                    outs[way].at[pl.ds(1, send)],
                    out_sem.at[9 * p + 3 + way],
                )
            )
        for write in fresh:
            write.start()
        writes.extend(fresh)
        chunk = stay // 4
        for k in range(4):
            first = 1 + k * chunk
            write = pltpu.make_async_copy(
                buf.at[pl.ds(2 * (send + 1) + first, chunk)], outs[2].at[pl.ds(first, chunk)], out_sem.at[9 * p + 5 + k]
            )
            used = state[zero + 6] > first
            pl.when(used)(write.start)
            kept.append((used, write))

    for p, (first_row, height, order, sizes) in enumerate(PARTS):
        send, on, stay = sizes[stage]
        shift = SHIFT[order[stage]]
        buf, sem, head, zero = bufs[p], copy_sem.at[p], heads[p], 16 * p
        if stage == 0:
            sources = [Rows(plan, arrivals[p][0], first_row, height)]
        else:
            sources = [
                Slots(h, g, back)
                for h, g, back in zip(came[p], arrivals[p], (False, True, True, False, False))
            ]
        mine = (place[0] >> shift) & 3
        base = (0, send + 1, 2 * (send + 1))

        def turn(code):
            by = (code >> (10 + shift)) - mine
            return jnp.where(odd, -by, by) & 3

        for k in range(4):
            state[zero + k] = 0

        def count(code, source):
            where = turn(code)
            state[zero + where] = state[zero + where] + (code & 7)

        for source in sources:
            source.walk(count)
        ahead, behind, across = state[zero + 1], state[zero + 3], state[zero + 2]
        big, small = jnp.maximum(ahead, behind), jnp.minimum(ahead, behind)
        lesser = jnp.minimum(jnp.minimum(across, (across + big - small + 1) >> 1), on)
        forward = jnp.where(ahead <= behind, lesser, across - lesser)
        for k, value in ((4, 1), (5, 1), (6, 1), (7, send + 1), (8, send + 1), (14, forward)):
            state[zero + k] = value
        for k in (9, 10, 11, 12, 13, 15):
            state[zero + k] = 0

        def put(code, source, skip, tiles, slot):
            start_tiles(
                tiles,
                lambda at, size: source(skip + at, size),
                lambda at, size: buf.at[pl.ds(slot + at, size)],
                sem,
            )
            state[zero + 15] = state[zero + 15] + tiles

        def front(way, code, source, skip, tiles, limit):
            slot = state[zero + 4 + way]
            fits = slot + tiles <= limit
            if way < 2:
                fits = fits & (slot + tiles <= state[zero + 7 + way])

            @pl.when((tiles > 0) & fits)
            def _():
                state[zero + 4 + way] = slot + tiles
                entry = state[zero + 9 + way]
                state[zero + 9 + way] = entry + 1
                sent = (code & ~63) | ((((code >> 3) & 7) + skip) << 3) | tiles
                head[way][0, entry] = sent.astype(F32)
                put(code, source, skip, tiles, base[way] + slot)

        def back(way, code, source):
            tiles = code & 7
            slot = state[zero + 7 + way] - tiles

            @pl.when(slot >= state[zero + 4 + way])
            def _():
                state[zero + 7 + way] = slot
                entry = state[zero + 12 + way]
                state[zero + 12 + way] = entry + 1
                head[way][0, FRONTS - 1 - entry] = code.astype(F32)
                put(code, source, 0, tiles, base[way] + slot)

        def assign(code, source):
            where = turn(code)
            tiles = code & 7

            @pl.when(where == 0)
            def _():
                front(2, code, source, 0, tiles, stay + 1)

            @pl.when(where == 1)
            def _():
                back(0, code, source)

            @pl.when(where == 3)
            def _():
                back(1, code, source)

            @pl.when(where == 2)
            def _():
                take = jnp.minimum(tiles, state[zero + 14])
                state[zero + 14] = state[zero + 14] - take
                front(0, code, source, 0, take, on + 1)
                front(1, code, source, take, tiles - take, on + 1)

        for source in sources:
            source.walk(assign)
        for way in range(3):
            head[way][0, FRONTS] = state[zero + 9 + way].astype(F32)
            head[way][0, BACKS] = (state[zero + 12 + way] if way < 2 else jnp.int32(0)).astype(F32)
        if p > 0:
            write_out(p - 1)
    write_out(parts - 1)


    for used, write in kept:
        pl.when(used)(write.wait)
    for write in writes + tables:
        write.wait()


def table_scratch():
    return [VMEM((5, 16, LANES), F32), VMEM((16, LANES), F32), pltpu.SemaphoreType.DMA((5,))]


def head_scratch(count):
    return [SMEM((1, LANES), F32)] * count


def route(stage, plan, place, got):
    parts = len(PARTS)
    sizes = [(size[stage], height) for _, height, _, size in PARTS]
    result = pl.pallas_call(
        functools.partial(route_kernel, stage),
        grid_spec=pltpu.PrefetchScalarGridSpec(
            num_scalar_prefetch=2,
            grid=(1,),
            in_specs=[ANYWHERE] * len(got),
            out_specs=[ANYWHERE] * (3 * parts),
            scratch_shapes=[VMEM((2 * (send + 1) + stay + 1, height, LANES), F32) for (send, _, stay), height in sizes]
            + [
                SMEM((16 * parts,), jnp.int32),
                pltpu.SemaphoreType.DMA((parts,)),
                pltpu.SemaphoreType.DMA((5 * parts,)),
                pltpu.SemaphoreType.DMA((9 * parts + 3,)),
            ]
            + table_scratch()
            + head_scratch(3 * parts)
            + ([] if stage == 0 else head_scratch(5 * parts)),
        ),
        out_shape=[
            jax.ShapeDtypeStruct((size + 1, height, LANES), F32)
            for (send, _, stay), height in sizes
            for size in (send, send, stay)
        ],
        compiler_params=pltpu.CompilerParams(vmem_limit_bytes=48 << 20),
        cost_estimate=pl.CostEstimate(flops=0, bytes_accessed=24_000_000, transcendentals=0),
        name="route",
    )(plan, place, *got)
    return [result[3 * p : 3 * p + 3] for p in range(parts)]


def swap_kernel(place, *refs):
    refs = list(refs)
    parts = len(PARTS)
    got = [[refs.pop(0) for _ in range(5)] for _ in range(parts)]
    outs = [refs.pop(0) for _ in range(parts)]
    bufs = [refs.pop(0) for _ in range(parts)]
    state, copy_sem, head_sem, out_sem, table_in, table_out, table_sem = [refs.pop(0) for _ in range(7)]
    out_heads = [refs.pop(0) for _ in range(parts)]
    heads = [[refs.pop(0) for _ in range(5)] for _ in range(parts)]
    finish = read_table(got[0], table_in, table_sem)
    read_headers([(got[p][k], heads[p][k]) for p in range(parts) for k in range(5)], head_sem)
    core = place[0] & 1
    table_out[...] = finish()
    writes = [pltpu.make_async_copy(table_out, outs[0].at[0, TABLE], out_sem.at[2 * parts])]
    writes[0].start()

    def write_out(p):
        wait_tiles(state[4 * p + 2], bufs[p].at[0], copy_sem.at[p])
        fresh = [
            pltpu.make_async_copy(bufs[p].at[pl.ds(1, SWAP)], outs[p].at[pl.ds(1, SWAP)], out_sem.at[2 * p]),
            pltpu.make_async_copy(out_heads[p], outs[p].at[0, pl.ds(0, 1)], out_sem.at[2 * p + 1]),
        ]
        for write in fresh:
            write.start()
        writes.extend(fresh)

    for p in range(parts):
        buf, sem, head, zero = bufs[p], copy_sem.at[p], out_heads[p], 4 * p
        for k, value in ((0, 1), (1, 0), (2, 0)):
            state[zero + k] = value

        def assign(code, source):
            tiles = code & 7
            slot = state[zero]

            @pl.when((((code >> 10) & 1) != core) & (slot + tiles <= SWAP + 1))
            def _():
                state[zero] = slot + tiles
                entry = state[zero + 1]
                state[zero + 1] = entry + 1
                head[0, entry] = code.astype(F32)
                start_tiles(tiles, source, lambda at, size: buf.at[pl.ds(slot + at, size)], sem)
                state[zero + 2] = state[zero + 2] + tiles

        for h, g, back in zip(heads[p], got[p], (False, True, True, False, False)):
            Slots(h, g, back).walk(assign)
        head[0, FRONTS] = state[zero + 1].astype(F32)
        if p > 0:
            write_out(p - 1)
    write_out(parts - 1)
    for write in writes:
        write.wait()


def swap_out(place, got):
    parts = len(PARTS)
    heights = [height for _, height, _, _ in PARTS]
    inputs = [x for part in got for x in part]
    return pl.pallas_call(
        swap_kernel,
        grid_spec=pltpu.PrefetchScalarGridSpec(
            num_scalar_prefetch=1,
            grid=(1,),
            in_specs=[ANYWHERE] * len(inputs),
            out_specs=[ANYWHERE] * parts,
            scratch_shapes=[VMEM((SWAP + 1, height, LANES), F32) for height in heights]
            + [
                SMEM((4 * parts,), jnp.int32),
                pltpu.SemaphoreType.DMA((parts,)),
                pltpu.SemaphoreType.DMA((5 * parts,)),
                pltpu.SemaphoreType.DMA((2 * parts + 1,)),
            ]
            + table_scratch()
            + head_scratch(6 * parts),
        ),
        out_shape=[jax.ShapeDtypeStruct((SWAP + 1, height, LANES), F32) for height in heights],
        compiler_params=pltpu.CompilerParams(vmem_limit_bytes=48 << 20),
        cost_estimate=pl.CostEstimate(flops=0, bytes_accessed=16_000_000, transcendentals=0),
        name="swap_out",
    )(place, *inputs)


def gather_kernel(firsts, heights, place, *refs):
    refs = list(refs)
    parts = len(heights)
    got = [[refs.pop(0) for _ in range(6)] for _ in range(parts)]
    out, state, copy_sem, head_sem = [refs.pop(0) for _ in range(4)]
    heads = [[refs.pop(0) for _ in range(6)] for _ in range(parts)]
    copies = [
        pltpu.make_async_copy(got[p][k].at[0, pl.ds(0, 1)], heads[p][k], head_sem.at[6 * p + k])
        for p in range(parts)
        for k in range(6)
    ]
    for copy in copies:
        copy.start()

    def clear(k, carry):
        out[k] = jnp.zeros(out.shape[1:], F32)
        return carry

    lax.fori_loop(0, out.shape[0], clear, 0)
    for copy in copies:
        copy.wait()
    core = place[0] & 1
    for p in range(parts):
        sem = copy_sem.at[p]
        part = pl.ds(firsts[p], heights[p])
        state[p] = 0

        def assign(code, source):
            owner, row, tile, tiles = fields(code)

            @pl.when((owner & 1) == core)
            def _():
                start_tiles(tiles, source, lambda at, size: out.at[row, pl.ds(tile + at, size), part], sem)
                state[p] = state[p] + tiles

        for k, back in enumerate((False, True, True, False, False, False)):
            Slots(heads[p][k], got[p][k], back).walk(assign)
    for p in range(parts):
        wait_tiles(state[p], out.at[0, 0, pl.ds(firsts[p], heights[p])], copy_sem.at[p])


def gather_rows(place, got, coarse):
    firsts = tuple(first for first, _, _, _ in PARTS)
    heights = tuple(height for _, height, _, _ in PARTS)
    parts = len(PARTS)
    inputs = [x for part in got for x in part]
    return pl.pallas_call(
        functools.partial(gather_kernel, firsts, heights),
        grid_spec=pltpu.PrefetchScalarGridSpec(
            num_scalar_prefetch=1,
            grid=(1,),
            in_specs=[ANYWHERE] * len(inputs),
            out_specs=pl.BlockSpec((coarse, CWIN, B, B), lambda *_: (0, 0, 0, 0)),
            scratch_shapes=[
                SMEM((4,), jnp.int32),
                pltpu.SemaphoreType.DMA((parts,)),
                pltpu.SemaphoreType.DMA((6 * parts,)),
            ]
            + head_scratch(6 * parts),
        ),
        out_shape=jax.ShapeDtypeStruct((coarse, CWIN, B, B), F32),
        compiler_params=pltpu.CompilerParams(vmem_limit_bytes=56 << 20),
        cost_estimate=pl.CostEstimate(flops=0, bytes_accessed=16_000_000, transcendentals=0),
        name="gather_rows",
    )(place, *inputs)


def fits_kernel(owner_ref, one_ref, two_ref, out_ref):
    units = owner_ref.shape[1]
    devices = LANES
    owner = owner_ref[...]
    turned = jnp.maximum(one_ref[0, TABLE], two_ref[0, TABLE])
    tiles = jnp.concatenate([turned[r : r + 1] for r in range(units // devices)], axis=1)
    source = lax.broadcasted_iota(jnp.int32, (1, units), 1) // (units // devices)
    index = lax.broadcasted_iota(jnp.int32, (devices, units), 0)
    kinds = lax.broadcasted_iota(jnp.int32, (8, units), 0)

    def tally(holder, kind):
        left = jnp.where(holder == index, 1.0, 0.0).astype(BF)
        right = jnp.where(kinds == kind, tiles, 0.0).astype(BF)
        return lax.dot_general(left, right, (((1,), (1,)), ((), ())), preferred_element_type=F32)

    def step(holder, shift):
        return holder + ((((owner >> shift) & 3) - ((holder >> shift) & 3)) << shift)

    excess = jnp.full((devices, 1), -1.0, F32)
    holder = source
    for _, _, order, sizes in PARTS:
        holder = source
        for axis, (send, on, stay) in zip(order, sizes):
            shift = SHIFT[axis]
            table = tally(holder, ((owner >> shift) - (holder >> shift)) & 3)
            here, ahead, across, behind = (table[:, k : k + 1] for k in range(4))
            big, small = jnp.maximum(ahead, behind), jnp.minimum(ahead, behind)
            lesser = jnp.minimum(jnp.minimum(across, jnp.floor((across + big - small + 1.0) * 0.5)), float(on))
            greater = across - lesser
            for value, limit in ((small + lesser, send), (big + greater, send), (greater, on), (here, stay)):
                excess = jnp.maximum(excess, value - float(limit))
            holder = step(holder, shift)
    table = tally(holder, (owner ^ holder) & 1)
    excess = jnp.maximum(excess, table[:, 1:2] - float(SWAP))
    out_ref[...] = jnp.broadcast_to(jnp.max(excess, axis=0, keepdims=True), out_ref.shape)


def ring_fits(owner, one, two):
    turned = owner.reshape(1, -1)
    head = pl.BlockSpec((1,) + one.shape[1:], lambda *_: (0, 0, 0))
    return pl.pallas_call(
        fits_kernel,
        grid=(1,),
        in_specs=[pl.BlockSpec(turned.shape, lambda *_: (0, 0)), head, head],
        out_specs=pl.BlockSpec((8, LANES), lambda *_: (0, 0)),
        out_shape=jax.ShapeDtypeStruct((8, LANES), F32),
        compiler_params=pltpu.CompilerParams(vmem_limit_bytes=32 << 20),
        cost_estimate=pl.CostEstimate(flops=100_000_000, bytes_accessed=100_000, transcendentals=0),
        name="ring_fits",
    )(turned, one, two)[0, 0] <= 0.0


AXES = ("gx", "gy")


def neighbours(axis, way):
    shift, size = SHIFT[axis], lax.axis_size(AXES)
    pairs = []
    for i in range(size):
        by = way if i % 2 == 0 else -way
        pairs.append((i, (i & ~(3 << shift)) | ((((i >> shift) + by) & 3) << shift)))
    return pairs


def by_ring(plan, place, rows, counts):
    got = [[rows, counts]]
    for stage in range(3):
        sent = route(stage, plan, place, [x for part in got for x in part])
        got = []
        for (one, two, stay), (_, _, order, sizes) in zip(sent, PARTS):
            on = sizes[stage][1] + 1
            ways = neighbours(order[stage], 1), neighbours(order[stage], -1)
            came = [lax.ppermute(x, AXES, way) for x, way in zip((one, two), ways)]
            came += [lax.ppermute(x[:on], AXES, way) for x, way in zip(came, ways)]
            got.append([stay] + came)
    size = lax.axis_size(AXES)
    pairs = [(i, i ^ 1) for i in range(size)]
    other = swap_out(place, got)
    swapped = [lax.ppermute(x, AXES, pairs) for x in other]
    return [part + [x] for part, x in zip(got, swapped)], other[0], swapped[0]


def shards(a_tiles, a_cols, a_len, p_tiles, aggregate, owner):
    device = lax.axis_index(AXES)
    size = lax.axis_size(AXES)
    coarse = a_tiles.shape[0] // 3
    place = jnp.reshape(device, (1,)).astype(jnp.int32)
    plan, counts, up, down = make_plan(place, a_cols, a_len, aggregate, owner, a_tiles, p_tiles)
    before = lax.ppermute(up, AXES, [(i, (i + 1) % size) for i in range(size)])
    behind = lax.ppermute(down, AXES, [((i + 1) % size, i) for i in range(size)])
    coarse_rows = main_product(plan, a_tiles, p_tiles)
    coarse_rows = edge_product(plan, before, behind, up, down, p_tiles, coarse_rows)
    got, one, two = by_ring(plan, place, coarse_rows, counts)
    fits = ring_fits(owner, one, two)
    return lax.cond(
        fits,
        lambda kept, parts: gather_rows(place, parts, coarse),
        lambda kept, parts: by_slots(kept, owner, device),
        coarse_rows,
        got,
    )


def by_slots(complete, owner, device):
    count_x, count_y = lax.axis_size("gx"), lax.axis_size("gy")
    index_x, index_y = device // count_y, device % count_y
    coarse = complete.shape[0]
    depth = coarse // count_x
    table = owner.reshape(count_x, count_y, coarse)
    order = jnp.arange(coarse)
    shift = table[0, 0] // count_y
    same = shift[None, :] == shift[:, None]
    rank = jnp.sum((same & (order[None, :] < order[:, None])).astype(jnp.int32), axis=1)
    mine = table[index_x, index_y]
    slot = (mine // count_y) * depth + rank
    hits = slot[None, :] == order[:, None]
    packed = complete[jnp.sum(jnp.where(hits, order[None, :], 0), axis=1)]
    moved = lax.all_to_all(packed, "gx", split_axis=0, concat_axis=0, tiled=True)
    from_x = (index_x - shift) % count_x
    column = table[:, index_y] % count_y
    target = jnp.sum(jnp.where(jnp.arange(count_x)[:, None] == from_x[None, :], column, 0), axis=0)
    hits = target[None, :] == jnp.arange(count_y)[:, None]
    packed = moved[jnp.sum(jnp.where(hits, (from_x * depth + rank)[None, :], 0), axis=1)]
    moved = lax.all_to_all(packed, "gy", split_axis=0, concat_axis=0, tiled=True)
    found = table.reshape(-1, coarse) == device
    sender = jnp.sum(jnp.where(found, jnp.arange(count_x * count_y)[:, None], 0), axis=0)
    ids = sender * coarse + order
    spot = jnp.sum((ids[None, :] < ids[:, None]).astype(jnp.int32), axis=1)
    hits = spot[None, :] == order[:, None]
    return moved[jnp.sum(jnp.where(hits, (sender % count_y)[None, :], 0), axis=1)]


def solution(mesh):
    in_specs = (
        P(("gx", "gy"), None, None, None),
        P(("gx", "gy"), None),
        P(("gx", "gy")),
        P(("gx", "gy"), None, None, None),
        P(),
        P(),
    )
    out_specs = P(("gx", "gy"), None, None, None)
    return jax.shard_map(shards, mesh=mesh, in_specs=in_specs, out_specs=out_specs, check_vma=False)
```

profile of v0, /device:TPU:0, one launch (start us, length us, event | category | flops | bytes accessed | tf_op | source)
XLA Modules:
  0.0 261.3 jit_solution(5681940537002660215)
XLA Ops:
  2.8 3.7 %copy-done.1 = f32[48,3,128,128]{3,2,1,0:T(8,128)S(1)} copy-done((f32[48,3,128,128]{3,2,1,0:T(8,128)S(1)}, f32[48,3,128,128]{3,2,1,0:T(8,128)}, u32[]{:S(2)}) %copy-start.1) | copy-done | bytes 9437208
  8.5 7.5 %plan.1 = (s32[384]{0:T(512)S(1)}, f32[16,128]{1,0:T(8,128)S(1)}, f32[17,128,128]{2,1,0:T(8,128)S(1)}, f32[17,128,128]{2,1,0:T(8,128)S(1)}) custom-call(s32[1]{0:T(128)} %bitcast.10.place, s32[3,48]{1,0:T(4,128)S(1)} %bitcast.34, s32[48]{0:T(128)S(1)} %copy-done.11, f32[48,3,128,128]{3,2,1,0:T(8,128)S(1)} %copy-done.1, f32[48,2,128,128]{3,2,1,0:T(8,128)S(1)} %copy-done, ...), custom_call_target="tpu_custom_call" | custom-call | bytes 5000000 | tf_op jit(solution)/shard_map/plan/pallas_call | solution.py:435
  16.6 8.1 %collective-permute-start.1 = (f32[17,128,128]{2,1,0:T(8,128)S(1)}, f32[17,128,128]{2,1,0:T(8,128)S(1)}, u32[]{:S(2)}, u32[]{:S(2)}) collective-permute-start(f32[17,128,128]{2,1,0:T(8,128)S(1)} %get-tuple-element.110.a_first), channel_id=1, source_target_pairs={{1,0},{2,1},{3,2},{4,3},{5,4},{6,5},{7,6},{8,7},{9,8},{10,9},{11,1... | collective-permute-start | bytes 3342344 | tf_op jit(solution)/shard_map/ppermute | solution.py:1002
  24.8 18.2 %triple_product.1.in_rows = f32[16,7,128,128]{3,2,1,0:T(8,128)} custom-call(s32[384]{0:T(512)} %copy-done.7, f32[48,3,128,128]{3,2,1,0:T(8,128)} %a_ref.1, f32[48,2,128,128]{3,2,1,0:T(8,128)} %p_last.1, f32[48,2,128,128]{3,2,1,0:T(8,128)} %p_last.1, f32[48,2,128,128]{3,2,1,0:T(8,128)} %p_last.1), custom_call_target="tpu_custom_call" | custom-call | flops 16000000000 | bytes 24000000 | tf_op jit(solution)/shard_map/triple_product/pallas_call | solution.py:164
  45.0 5.8 %edge_rows.1.refs_0_ = f32[16,7,128,128]{3,2,1,0:T(8,128)} custom-call(s32[384]{0:T(512)} %copy-done.7, f32[17,128,128]{2,1,0:T(8,128)} %copy-done.21, f32[17,128,128]{2,1,0:T(8,128)} %copy-done.22, f32[17,128,128]{2,1,0:T(8,128)} %copy-done.3, f32[17,128,128]{2,1,0:T(8,128)} %copy-done.2, ...), custom_call_target="tpu_custom_call", output_to_operand_aliasing={{}: (7, {})} | custom-call | flops 2000000000 | bytes 10000000 | tf_op jit(solution)/shard_map/edge_rows/pallas_call | solution.py:286
  50.9 9.0 %route.3 = (f32[38,48,128]{2,1,0:T(8,128)S(1)}, f32[38,48,128]{2,1,0:T(8,128)S(1)}, f32[49,48,128]{2,1,0:T(8,128)}, f32[50,40,128]{2,1,0:T(8,128)}, f32[50,40,12...) custom-call(s32[384]{0:T(512)S(1)} %copy-done.8, ...), custom_call_target="tpu_custom_call" | custom-call | bytes 24000000 | tf_op jit(solution)/shard_map/route/pallas_call | solution.py:734
  60.9 3.2 %collective-permute-start.7 = (f32[50,40,128]{2,1,0:T(8,128)}, f32[50,40,128]{2,1,0:T(8,128)S(1)}, u32[]{:S(2)}, u32[]{:S(2)}) collective-permute-start(f32[50,40,128]{2,1,0:T(8,128)} %get-tuple-element.117), channel_id=1, source_target_pairs={{0,6},{1,3},{2,0},{3,5},{4,2},{5,7},{6,4},{7,1},{8,14},{9,11},{10,... | collective-permute-start | bytes 3072008 | tf_op jit(solution)/shard_map/ppermute | solution.py:985
  64.1 3.2 %collective-permute-start.11 = (f32[48,40,128]{2,1,0:T(8,128)S(1)}, f32[48,40,128]{2,1,0:T(8,128)S(1)}, u32[]{:S(2)}, u32[]{:S(2)}) collective-permute-start(f32[48,40,128]{2,1,0:T(8,128)S(1)} %get-tuple-element.120), channel_id=1, source_target_pairs={{0,24},{1,9},{2,26},{3,11},{4,28},{5,13},{6,30},{7,15},{8,0},{9,17... | collective-permute-start | bytes 2949128 | tf_op jit(solution)/shard_map/ppermute | solution.py:985
  67.3 12.0 %collective-permute-done.2.refs_1_ = f32[38,48,128]{2,1,0:T(8,128)S(1)} collective-permute-done((f32[38,48,128]{2,1,0:T(8,128)S(1)}, f32[38,48,128]{2,1,0:T(8,128)S(1)}, u32[]{:S(2)}, u32[]{:S(2)}) %collective-permute-start.2) | collective-permute-done | bytes 933920 | tf_op jit(solution)/shard_map/ppermute | solution.py:985
  79.3 6.3 %collective-permute-done.10.refs_11_ = f32[48,40,128]{2,1,0:T(8,128)S(1)} collective-permute-done((f32[48,40,128]{2,1,0:T(8,128)S(1)}, f32[48,40,128]{2,1,0:T(8,128)S(1)}, u32[]{:S(2)}, u32[]{:S(2)}) %collective-permute-start.10) | collective-permute-done | bytes 983072 | tf_op jit(solution)/shard_map/ppermute | solution.py:985
  87.0 3.3 %collective-permute-start.13 = (f32[25,40,128]{2,1,0:T(8,128)S(1)}, f32[25,40,128]{2,1,0:T(8,128)S(1)}, u32[]{:S(2)}, u32[]{:S(2)}) collective-permute-start(f32[25,40,128]{2,1,0:T(8,128)S(1)} %slice.91), channel_id=1, source_target_pairs={{0,24},{1,9},{2,26},{3,11},{4,28},{5,13},{6,30},{7,15},{8,0},{9,17... | collective-permute-start | bytes 1536008 | tf_op jit(solution)/shard_map/ppermute | solution.py:986
  94.5 4.2 %collective-permute-start.5 = (f32[15,48,128]{2,1,0:T(8,128)S(1)}, f32[15,48,128]{2,1,0:T(8,128)S(1)}, u32[]{:S(2)}, u32[]{:S(2)}) collective-permute-start(f32[15,48,128]{2,1,0:T(8,128)S(1)} %slice.87), channel_id=1, source_target_pairs={{0,96},{1,33},{2,98},{3,35},{4,100},{5,37},{6,102},{7,39},{8,104},... | collective-permute-start | bytes 1105928 | tf_op jit(solution)/shard_map/ppermute | solution.py:986
  98.7 5.0 %collective-permute-done.5.refs_4_ = f32[15,48,128]{2,1,0:T(8,128)S(1)} collective-permute-done((f32[15,48,128]{2,1,0:T(8,128)S(1)}, f32[15,48,128]{2,1,0:T(8,128)S(1)}, u32[]{:S(2)}, u32[]{:S(2)}) %collective-permute-start.5) | collective-permute-done | bytes 368672 | tf_op jit(solution)/shard_map/ppermute | solution.py:986
  103.7 13.1 %route.4 = (f32[47,48,128]{2,1,0:T(8,128)}, f32[47,48,128]{2,1,0:T(8,128)}, f32[49,48,128]{2,1,0:T(8,128)}, f32[55,40,128]{2,1,0:T(8,128)}, f32[55,40,128]{2,1,0...) custom-call(s32[384]{0:T(512)S(1)} %copy-done.8, ...), custom_call_target="tpu_custom_call" | custom-call | bytes 24000000 | tf_op jit(solution)/shard_map/route/pallas_call | solution.py:734
  117.0 3.9 %collective-permute-start.23 = (f32[65,40,128]{2,1,0:T(8,128)}, f32[65,40,128]{2,1,0:T(8,128)S(1)}, u32[]{:S(2)}, u32[]{:S(2)}) collective-permute-start(f32[65,40,128]{2,1,0:T(8,128)} %get-tuple-element.129), channel_id=1, source_target_pairs={{0,96},{1,33},{2,98},{3,35},{4,100},{5,37},{6,102},{7,39},{8,104},... | collective-permute-start | bytes 3993608 | tf_op jit(solution)/shard_map/ppermute | solution.py:985
  120.9 3.2 %collective-permute-start.15 = (f32[47,48,128]{2,1,0:T(8,128)}, f32[47,48,128]{2,1,0:T(8,128)S(1)}, u32[]{:S(2)}, u32[]{:S(2)}) collective-permute-start(f32[47,48,128]{2,1,0:T(8,128)} %get-tuple-element.123), channel_id=1, source_target_pairs={{0,6},{1,3},{2,0},{3,5},{4,2},{5,7},{6,4},{7,1},{8,14},{9,11},{10,... | collective-permute-start | bytes 3465224 | tf_op jit(solution)/shard_map/ppermute | solution.py:985
  124.1 9.8 %collective-permute-done.18.refs_6_ = f32[55,40,128]{2,1,0:T(8,128)S(1)} collective-permute-done((f32[55,40,128]{2,1,0:T(8,128)}, f32[55,40,128]{2,1,0:T(8,128)S(1)}, u32[]{:S(2)}, u32[]{:S(2)}) %collective-permute-start.18) | collective-permute-done | bytes 1126432 | tf_op jit(solution)/shard_map/ppermute | solution.py:985
  134.3 15.7 %collective-permute-done.22.refs_11_ = f32[65,40,128]{2,1,0:T(8,128)S(1)} collective-permute-done((f32[65,40,128]{2,1,0:T(8,128)}, f32[65,40,128]{2,1,0:T(8,128)S(1)}, u32[]{:S(2)}, u32[]{:S(2)}) %collective-permute-start.22) | collective-permute-done | bytes 1331232 | tf_op jit(solution)/shard_map/ppermute | solution.py:985
  157.1 3.2 %collective-permute-done.20.refs_8_ = f32[25,40,128]{2,1,0:T(8,128)S(1)} collective-permute-done((f32[25,40,128]{2,1,0:T(8,128)S(1)}, f32[25,40,128]{2,1,0:T(8,128)S(1)}, u32[]{:S(2)}, u32[]{:S(2)}) %collective-permute-start.20) | collective-permute-done | bytes 512032 | tf_op jit(solution)/shard_map/ppermute | solution.py:986
  163.0 6.6 %collective-permute-done.21.refs_9_ = f32[25,40,128]{2,1,0:T(8,128)S(1)} collective-permute-done((f32[25,40,128]{2,1,0:T(8,128)S(1)}, f32[25,40,128]{2,1,0:T(8,128)S(1)}, u32[]{:S(2)}, u32[]{:S(2)}) %collective-permute-start.21) | collective-permute-done | bytes 512032 | tf_op jit(solution)/shard_map/ppermute | solution.py:986
  169.8 11.9 %route.5 = (f32[55,48,128]{2,1,0:T(8,128)}, f32[55,48,128]{2,1,0:T(8,128)}, f32[49,48,128]{2,1,0:T(8,128)}, f32[51,40,128]{2,1,0:T(8,128)S(1)}, f32[51,40,128]{2...) custom-call(s32[384]{0:T(512)S(1)} %copy-done.8, ...), custom_call_target="tpu_custom_call" | custom-call | bytes 24000000 | tf_op jit(solution)/shard_map/route/pallas_call | solution.py:734
  182.0 4.2 %collective-permute-start.27 = (f32[55,48,128]{2,1,0:T(8,128)}, f32[55,48,128]{2,1,0:T(8,128)S(1)}, u32[]{:S(2)}, u32[]{:S(2)}) collective-permute-start(f32[55,48,128]{2,1,0:T(8,128)} %get-tuple-element.132), channel_id=1, source_target_pairs={{0,24},{1,9},{2,26},{3,11},{4,28},{5,13},{6,30},{7,15},{8,0},{9,17... | collective-permute-start | bytes 4055048 | tf_op jit(solution)/shard_map/ppermute | solution.py:985
  189.3 17.6 %collective-permute-done.30.refs_6_ = f32[51,40,128]{2,1,0:T(8,128)} collective-permute-done((f32[51,40,128]{2,1,0:T(8,128)S(1)}, f32[51,40,128]{2,1,0:T(8,128)}, u32[]{:S(2)}, u32[]{:S(2)}) %collective-permute-start.30) | collective-permute-done | bytes 1044512 | tf_op jit(solution)/shard_map/ppermute | solution.py:985
  206.9 3.5 %collective-permute-start.35 = (f32[54,40,128]{2,1,0:T(8,128)}, f32[54,40,128]{2,1,0:T(8,128)}, u32[]{:S(2)}, u32[]{:S(2)}) collective-permute-start(f32[54,40,128]{2,1,0:T(8,128)} %get-tuple-element.138), channel_id=1, source_target_pairs={{0,6},{1,3},{2,0},{3,5},{4,2},{5,7},{6,4},{7,1},{8,14},{9,11},{10,... | collective-permute-start | bytes 3317768 | tf_op jit(solution)/shard_map/ppermute | solution.py:985
  211.5 4.6 %collective-permute-done.26.refs_1_ = f32[55,48,128]{2,1,0:T(8,128)S(1)} collective-permute-done((f32[55,48,128]{2,1,0:T(8,128)}, f32[55,48,128]{2,1,0:T(8,128)S(1)}, u32[]{:S(2)}, u32[]{:S(2)}) %collective-permute-start.26) | collective-permute-done | bytes 1351712 | tf_op jit(solution)/shard_map/ppermute | solution.py:985
  216.3 3.3 %collective-permute-start.29 = (f32[25,48,128]{2,1,0:T(8,128)S(1)}, f32[25,48,128]{2,1,0:T(8,128)}, u32[]{:S(2)}, u32[]{:S(2)}) collective-permute-start(f32[25,48,128]{2,1,0:T(8,128)S(1)} %slice.99), channel_id=1, source_target_pairs={{0,24},{1,9},{2,26},{3,11},{4,28},{5,13},{6,30},{7,15},{8,0},{9,17... | collective-permute-start | bytes 1843208 | tf_op jit(solution)/shard_map/ppermute | solution.py:986
  220.7 3.3 %collective-permute-start.33 = (f32[25,40,128]{2,1,0:T(8,128)S(1)}, f32[25,40,128]{2,1,0:T(8,128)}, u32[]{:S(2)}, u32[]{:S(2)}) collective-permute-start(f32[25,40,128]{2,1,0:T(8,128)S(1)} %slice.101), channel_id=1, source_target_pairs={{0,96},{1,33},{2,98},{3,35},{4,100},{5,37},{6,102},{7,39},{8,104},... | collective-permute-start | bytes 1536008 | tf_op jit(solution)/shard_map/ppermute | solution.py:986
  227.4 3.4 %collective-permute-done.32.refs_8_ = f32[25,40,128]{2,1,0:T(8,128)} collective-permute-done((f32[25,40,128]{2,1,0:T(8,128)S(1)}, f32[25,40,128]{2,1,0:T(8,128)}, u32[]{:S(2)}, u32[]{:S(2)}) %collective-permute-start.32) | collective-permute-done | bytes 512032 | tf_op jit(solution)/shard_map/ppermute | solution.py:986
  231.2 7.0 %collective-permute-done.36.refs_13_ = f32[25,40,128]{2,1,0:T(8,128)} collective-permute-done((f32[25,40,128]{2,1,0:T(8,128)S(1)}, f32[25,40,128]{2,1,0:T(8,128)}, u32[]{:S(2)}, u32[]{:S(2)}) %collective-permute-start.36) | collective-permute-done | bytes 512032 | tf_op jit(solution)/shard_map/ppermute | solution.py:986
  239.9 5.6 %swap_out.1 = (f32[68,48,128]{2,1,0:T(8,128)S(1)}, f32[68,40,128]{2,1,0:T(8,128)S(1)}, f32[68,40,128]{2,1,0:T(8,128)S(1)}) custom-call(s32[1]{0:T(128)} %bitcast.10.place, f32[49,48,128]{2,1,0:T(8,128)} %get-tuple-element.130.refs_0_, f32[55,48,128]{2,1,0:T(8,128)S(1)} %collective-permute-done.26.refs_1_, ...), custom_call_target="tpu_custom_call" | custom-call | bytes 16000000 | tf_op jit(solution)/shard_map/swap_out/pallas_call | solution.py:822
  253.3 7.9 %conditional.1 = (f32[16,7,128,128]{3,2,1,0:T(8,128)}) conditional(s32[]{:T(128)} %bitcast.14, (s32[2048]{0:T(1024)S(1)}, s32[]{:T(128)}, f32[16,7,128,128]{3,2,1,0:T(8,128)}) %tuple.21, (s32[1]{0:T(128)}, f32[49,48,128]{2,1,0:T(8,128)}, f32[55,48,128]{2,1,0:T(8,128)S(1)}, f32[55,48,128]{2,1,0:T(8,128)S(1)}, f32[25,48,128]{2,1,0:T(8,128)S(1)}, ...), branch_computations={%region_0.8_spmd, %region_8.9_spmd} | conditional | flops 16265 | bytes 124829464 | solution.py:1007
  253.3 7.9 %gather_rows.1 = f32[16,7,128,128]{3,2,1,0:T(8,128)} custom-call(s32[1]{0:T(128)} %get-tuple-element.55.place, f32[49,48,128]{2,1,0:T(8,128)} %get-tuple-element.56.refs_0_, f32[55,48,128]{2,1,0:T(8,128)S(1)} %get-tuple-element.57.refs_1_, f32[55,48,128]{2,1,0:T(8,128)S(1)} %get-tuple-element.58.refs_2_, f32[25,48,128]{2,1,0:T(8,128)S(1)} %get-tuple-element.59.refs_3_, ...), custom_call_target="tpu_custom_call" | custom-call | bytes 16000000 | tf_op jit(solution)/shard_map/cond/branch_1_fun/gather_rows/pallas_call | solution.py:892
  (127 shorter events, 42.9 us)
Async XLA Ops:
  16.6 26.3 %collective-permute-start = (f32[17,128,128]{2,1,0:T(8,128)S(1)}, f32[17,128,128]{2,1,0:T(8,128)S(1)}, u32[]{:S(2)}, u32[]{:S(2)}) collective-permute-start(f32[17,128,128]{2,1,0:T(8,128)S(1)} %get-tuple-element.109.a_last), channel_id=1, source_target_pairs={{0,1},{1,2},{2,3},{3,4},{4,5},{5,6},{6,7},{7,8},{8,9},{9,10},{10,1... | collective-permute-start | bytes 3342344 | tf_op jit(solution)/shard_map/ppermute | solution.py:1001
  16.6 26.3 %collective-permute-start.1 = (f32[17,128,128]{2,1,0:T(8,128)S(1)}, f32[17,128,128]{2,1,0:T(8,128)S(1)}, u32[]{:S(2)}, u32[]{:S(2)}) collective-permute-start(f32[17,128,128]{2,1,0:T(8,128)S(1)} %get-tuple-element.110.a_first), channel_id=1, source_target_pairs={{1,0},{2,1},{3,2},{4,3},{5,4},{6,5},{7,6},{8,7},{9,8},{10,9},{11,1... | collective-permute-start | bytes 3342344 | tf_op jit(solution)/shard_map/ppermute | solution.py:1002
  60.8 18.5 %collective-permute-start.2 = (f32[38,48,128]{2,1,0:T(8,128)S(1)}, f32[38,48,128]{2,1,0:T(8,128)S(1)}, u32[]{:S(2)}, u32[]{:S(2)}) collective-permute-start(f32[38,48,128]{2,1,0:T(8,128)S(1)} %get-tuple-element.113), channel_id=1, source_target_pairs={{0,32},{1,97},{2,34},{3,99},{4,36},{5,101},{6,38},{7,103},{8,40},{... | collective-permute-start | bytes 2801672 | tf_op jit(solution)/shard_map/ppermute | solution.py:985
  60.8 24.7 %collective-permute-start.10 = (f32[48,40,128]{2,1,0:T(8,128)S(1)}, f32[48,40,128]{2,1,0:T(8,128)S(1)}, u32[]{:S(2)}, u32[]{:S(2)}) collective-permute-start(f32[48,40,128]{2,1,0:T(8,128)S(1)} %get-tuple-element.119), channel_id=1, source_target_pairs={{0,8},{1,25},{2,10},{3,27},{4,12},{5,29},{6,14},{7,31},{8,16},{9,1... | collective-permute-start | bytes 2949128 | tf_op jit(solution)/shard_map/ppermute | solution.py:985
  60.8 26.2 %collective-permute-start.6 = (f32[50,40,128]{2,1,0:T(8,128)}, f32[50,40,128]{2,1,0:T(8,128)S(1)}, u32[]{:S(2)}, u32[]{:S(2)}) collective-permute-start(f32[50,40,128]{2,1,0:T(8,128)} %get-tuple-element.116), channel_id=1, source_target_pairs={{0,2},{1,7},{2,4},{3,1},{4,6},{5,3},{6,0},{7,5},{8,10},{9,15},{10,... | collective-permute-start | bytes 3072008 | tf_op jit(solution)/shard_map/ppermute | solution.py:985
  60.9 29.5 %collective-permute-start.7 = (f32[50,40,128]{2,1,0:T(8,128)}, f32[50,40,128]{2,1,0:T(8,128)S(1)}, u32[]{:S(2)}, u32[]{:S(2)}) collective-permute-start(f32[50,40,128]{2,1,0:T(8,128)} %get-tuple-element.117), channel_id=1, source_target_pairs={{0,6},{1,3},{2,0},{3,5},{4,2},{5,7},{6,4},{7,1},{8,14},{9,11},{10,... | collective-permute-start | bytes 3072008 | tf_op jit(solution)/shard_map/ppermute | solution.py:985
  64.1 22.7 %collective-permute-start.11 = (f32[48,40,128]{2,1,0:T(8,128)S(1)}, f32[48,40,128]{2,1,0:T(8,128)S(1)}, u32[]{:S(2)}, u32[]{:S(2)}) collective-permute-start(f32[48,40,128]{2,1,0:T(8,128)S(1)} %get-tuple-element.120), channel_id=1, source_target_pairs={{0,24},{1,9},{2,26},{3,11},{4,28},{5,13},{6,30},{7,15},{8,0},{9,17... | collective-permute-start | bytes 2949128 | tf_op jit(solution)/shard_map/ppermute | solution.py:985
  79.2 13.6 %collective-permute-start.3 = (f32[38,48,128]{2,1,0:T(8,128)S(1)}, f32[38,48,128]{2,1,0:T(8,128)S(1)}, u32[]{:S(2)}, u32[]{:S(2)}) collective-permute-start(f32[38,48,128]{2,1,0:T(8,128)S(1)} %get-tuple-element.114), channel_id=1, source_target_pairs={{0,96},{1,33},{2,98},{3,35},{4,100},{5,37},{6,102},{7,39},{8,104},... | collective-permute-start | bytes 2801672 | tf_op jit(solution)/shard_map/ppermute | solution.py:985
  86.9 16.8 %collective-permute-start.12 = (f32[25,40,128]{2,1,0:T(8,128)S(1)}, f32[25,40,128]{2,1,0:T(8,128)S(1)}, u32[]{:S(2)}, u32[]{:S(2)}) collective-permute-start(f32[25,40,128]{2,1,0:T(8,128)S(1)} %slice.90), channel_id=1, source_target_pairs={{0,8},{1,25},{2,10},{3,27},{4,12},{5,29},{6,14},{7,31},{8,16},{9,1... | collective-permute-start | bytes 1536008 | tf_op jit(solution)/shard_map/ppermute | solution.py:986
  87.0 16.7 %collective-permute-start.13 = (f32[25,40,128]{2,1,0:T(8,128)S(1)}, f32[25,40,128]{2,1,0:T(8,128)S(1)}, u32[]{:S(2)}, u32[]{:S(2)}) collective-permute-start(f32[25,40,128]{2,1,0:T(8,128)S(1)} %slice.91), channel_id=1, source_target_pairs={{0,24},{1,9},{2,26},{3,11},{4,28},{5,13},{6,30},{7,15},{8,0},{9,17... | collective-permute-start | bytes 1536008 | tf_op jit(solution)/shard_map/ppermute | solution.py:986
  90.4 13.3 %collective-permute-start.8 = (f32[25,40,128]{2,1,0:T(8,128)S(1)}, f32[25,40,128]{2,1,0:T(8,128)S(1)}, u32[]{:S(2)}, u32[]{:S(2)}) collective-permute-start(f32[25,40,128]{2,1,0:T(8,128)S(1)} %slice.88), channel_id=1, source_target_pairs={{0,2},{1,7},{2,4},{3,1},{4,6},{5,3},{6,0},{7,5},{8,10},{9,15},{10,... | collective-permute-start | bytes 1536008 | tf_op jit(solution)/shard_map/ppermute | solution.py:986
  92.8 10.9 %collective-permute-start.9 = (f32[25,40,128]{2,1,0:T(8,128)S(1)}, f32[25,40,128]{2,1,0:T(8,128)S(1)}, u32[]{:S(2)}, u32[]{:S(2)}) collective-permute-start(f32[25,40,128]{2,1,0:T(8,128)S(1)} %slice.89), channel_id=1, source_target_pairs={{0,6},{1,3},{2,0},{3,5},{4,2},{5,7},{6,4},{7,1},{8,14},{9,11},{10,... | collective-permute-start | bytes 1536008 | tf_op jit(solution)/shard_map/ppermute | solution.py:986
  116.8 17.1 %collective-permute-start.18 = (f32[55,40,128]{2,1,0:T(8,128)}, f32[55,40,128]{2,1,0:T(8,128)S(1)}, u32[]{:S(2)}, u32[]{:S(2)}) collective-permute-start(f32[55,40,128]{2,1,0:T(8,128)} %get-tuple-element.125), channel_id=1, source_target_pairs={{0,8},{1,25},{2,10},{3,27},{4,12},{5,29},{6,14},{7,31},{8,16},{9,1... | collective-permute-start | bytes 3379208 | tf_op jit(solution)/shard_map/ppermute | solution.py:985
  116.9 33.1 %collective-permute-start.22 = (f32[65,40,128]{2,1,0:T(8,128)}, f32[65,40,128]{2,1,0:T(8,128)S(1)}, u32[]{:S(2)}, u32[]{:S(2)}) collective-permute-start(f32[65,40,128]{2,1,0:T(8,128)} %get-tuple-element.128), channel_id=1, source_target_pairs={{0,32},{1,97},{2,34},{3,99},{4,36},{5,101},{6,38},{7,103},{8,40},{... | collective-permute-start | bytes 3993608 | tf_op jit(solution)/shard_map/ppermute | solution.py:985
  117.0 33.0 %collective-permute-start.23 = (f32[65,40,128]{2,1,0:T(8,128)}, f32[65,40,128]{2,1,0:T(8,128)S(1)}, u32[]{:S(2)}, u32[]{:S(2)}) collective-permute-start(f32[65,40,128]{2,1,0:T(8,128)} %get-tuple-element.129), channel_id=1, source_target_pairs={{0,96},{1,33},{2,98},{3,35},{4,100},{5,37},{6,102},{7,39},{8,104},... | collective-permute-start | bytes 3993608 | tf_op jit(solution)/shard_map/ppermute | solution.py:985
  120.9 29.6 %collective-permute-start.14 = (f32[47,48,128]{2,1,0:T(8,128)}, f32[47,48,128]{2,1,0:T(8,128)S(1)}, u32[]{:S(2)}, u32[]{:S(2)}) collective-permute-start(f32[47,48,128]{2,1,0:T(8,128)} %get-tuple-element.122), channel_id=1, source_target_pairs={{0,2},{1,7},{2,4},{3,1},{4,6},{5,3},{6,0},{7,5},{8,10},{9,15},{10,... | collective-permute-start | bytes 3465224 | tf_op jit(solution)/shard_map/ppermute | solution.py:985
  120.9 32.7 %collective-permute-start.15 = (f32[47,48,128]{2,1,0:T(8,128)}, f32[47,48,128]{2,1,0:T(8,128)S(1)}, u32[]{:S(2)}, u32[]{:S(2)}) collective-permute-start(f32[47,48,128]{2,1,0:T(8,128)} %get-tuple-element.123), channel_id=1, source_target_pairs={{0,6},{1,3},{2,0},{3,5},{4,2},{5,7},{6,4},{7,1},{8,14},{9,11},{10,... | collective-permute-start | bytes 3465224 | tf_op jit(solution)/shard_map/ppermute | solution.py:985
  133.9 20.7 %collective-permute-start.19 = (f32[55,40,128]{2,1,0:T(8,128)}, f32[55,40,128]{2,1,0:T(8,128)S(1)}, u32[]{:S(2)}, u32[]{:S(2)}) collective-permute-start(f32[55,40,128]{2,1,0:T(8,128)} %get-tuple-element.126), channel_id=1, source_target_pairs={{0,24},{1,9},{2,26},{3,11},{4,28},{5,13},{6,30},{7,15},{8,0},{9,17... | collective-permute-start | bytes 3379208 | tf_op jit(solution)/shard_map/ppermute | solution.py:985
  150.0 19.8 %collective-permute-start.24 = (f32[33,40,128]{2,1,0:T(8,128)S(1)}, f32[33,40,128]{2,1,0:T(8,128)S(1)}, u32[]{:S(2)}, u32[]{:S(2)}) collective-permute-start(f32[33,40,128]{2,1,0:T(8,128)S(1)} %slice.96), channel_id=1, source_target_pairs={{0,32},{1,97},{2,34},{3,99},{4,36},{5,101},{6,38},{7,103},{8,40},{... | collective-permute-start | bytes 2027528 | tf_op jit(solution)/shard_map/ppermute | solution.py:986
  150.5 19.3 %collective-permute-start.25 = (f32[33,40,128]{2,1,0:T(8,128)S(1)}, f32[33,40,128]{2,1,0:T(8,128)S(1)}, u32[]{:S(2)}, u32[]{:S(2)}) collective-permute-start(f32[33,40,128]{2,1,0:T(8,128)S(1)} %slice.97), channel_id=1, source_target_pairs={{0,96},{1,33},{2,98},{3,35},{4,100},{5,37},{6,102},{7,39},{8,104},... | collective-permute-start | bytes 2027528 | tf_op jit(solution)/shard_map/ppermute | solution.py:986
  153.6 16.2 %collective-permute-start.16 = (f32[25,48,128]{2,1,0:T(8,128)S(1)}, f32[25,48,128]{2,1,0:T(8,128)S(1)}, u32[]{:S(2)}, u32[]{:S(2)}) collective-permute-start(f32[25,48,128]{2,1,0:T(8,128)S(1)} %slice.92), channel_id=1, source_target_pairs={{0,2},{1,7},{2,4},{3,1},{4,6},{5,3},{6,0},{7,5},{8,10},{9,15},{10,... | collective-permute-start | bytes 1843208 | tf_op jit(solution)/shard_map/ppermute | solution.py:986
  154.6 15.2 %collective-permute-start.17 = (f32[25,48,128]{2,1,0:T(8,128)S(1)}, f32[25,48,128]{2,1,0:T(8,128)S(1)}, u32[]{:S(2)}, u32[]{:S(2)}) collective-permute-start(f32[25,48,128]{2,1,0:T(8,128)S(1)} %slice.93), channel_id=1, source_target_pairs={{0,6},{1,3},{2,0},{3,5},{4,2},{5,7},{6,4},{7,1},{8,14},{9,11},{10,... | collective-permute-start | bytes 1843208 | tf_op jit(solution)/shard_map/ppermute | solution.py:986
  181.7 25.2 %collective-permute-start.30 = (f32[51,40,128]{2,1,0:T(8,128)S(1)}, f32[51,40,128]{2,1,0:T(8,128)}, u32[]{:S(2)}, u32[]{:S(2)}) collective-permute-start(f32[51,40,128]{2,1,0:T(8,128)S(1)} %get-tuple-element.134), channel_id=1, source_target_pairs={{0,32},{1,97},{2,34},{3,99},{4,36},{5,101},{6,38},{7,103},{8,40},{... | collective-permute-start | bytes 3133448 | tf_op jit(solution)/shard_map/ppermute | solution.py:985
  182.0 34.1 %collective-permute-start.26 = (f32[55,48,128]{2,1,0:T(8,128)}, f32[55,48,128]{2,1,0:T(8,128)S(1)}, u32[]{:S(2)}, u32[]{:S(2)}) collective-permute-start(f32[55,48,128]{2,1,0:T(8,128)} %get-tuple-element.131), channel_id=1, source_target_pairs={{0,8},{1,25},{2,10},{3,27},{4,12},{5,29},{6,14},{7,31},{8,16},{9,1... | collective-permute-start | bytes 4055048 | tf_op jit(solution)/shard_map/ppermute | solution.py:985
  182.0 34.2 %collective-permute-start.27 = (f32[55,48,128]{2,1,0:T(8,128)}, f32[55,48,128]{2,1,0:T(8,128)S(1)}, u32[]{:S(2)}, u32[]{:S(2)}) collective-permute-start(f32[55,48,128]{2,1,0:T(8,128)} %get-tuple-element.132), channel_id=1, source_target_pairs={{0,24},{1,9},{2,26},{3,11},{4,28},{5,13},{6,30},{7,15},{8,0},{9,17... | collective-permute-start | bytes 4055048 | tf_op jit(solution)/shard_map/ppermute | solution.py:985
  186.2 30.1 %collective-permute-start.31 = (f32[51,40,128]{2,1,0:T(8,128)}, f32[51,40,128]{2,1,0:T(8,128)}, u32[]{:S(2)}, u32[]{:S(2)}) collective-permute-start(f32[51,40,128]{2,1,0:T(8,128)} %get-tuple-element.135), channel_id=1, source_target_pairs={{0,96},{1,33},{2,98},{3,35},{4,100},{5,37},{6,102},{7,39},{8,104},... | collective-permute-start | bytes 3133448 | tf_op jit(solution)/shard_map/ppermute | solution.py:985
  189.3 31.4 %collective-permute-start.34 = (f32[54,40,128]{2,1,0:T(8,128)}, f32[54,40,128]{2,1,0:T(8,128)}, u32[]{:S(2)}, u32[]{:S(2)}) collective-permute-start(f32[54,40,128]{2,1,0:T(8,128)} %get-tuple-element.137), channel_id=1, source_target_pairs={{0,2},{1,7},{2,4},{3,1},{4,6},{5,3},{6,0},{7,5},{8,10},{9,15},{10,... | collective-permute-start | bytes 3317768 | tf_op jit(solution)/shard_map/ppermute | solution.py:985
  206.9 19.4 %collective-permute-start.35 = (f32[54,40,128]{2,1,0:T(8,128)}, f32[54,40,128]{2,1,0:T(8,128)}, u32[]{:S(2)}, u32[]{:S(2)}) collective-permute-start(f32[54,40,128]{2,1,0:T(8,128)} %get-tuple-element.138), channel_id=1, source_target_pairs={{0,6},{1,3},{2,0},{3,5},{4,2},{5,7},{6,4},{7,1},{8,14},{9,11},{10,... | collective-permute-start | bytes 3317768 | tf_op jit(solution)/shard_map/ppermute | solution.py:985
  216.1 14.6 %collective-permute-start.32 = (f32[25,40,128]{2,1,0:T(8,128)S(1)}, f32[25,40,128]{2,1,0:T(8,128)}, u32[]{:S(2)}, u32[]{:S(2)}) collective-permute-start(f32[25,40,128]{2,1,0:T(8,128)S(1)} %slice.100), channel_id=1, source_target_pairs={{0,32},{1,97},{2,34},{3,99},{4,36},{5,101},{6,38},{7,103},{8,40},{... | collective-permute-start | bytes 1536008 | tf_op jit(solution)/shard_map/ppermute | solution.py:986
  216.2 23.7 %collective-permute-start.28 = (f32[25,48,128]{2,1,0:T(8,128)S(1)}, f32[25,48,128]{2,1,0:T(8,128)S(1)}, u32[]{:S(2)}, u32[]{:S(2)}) collective-permute-start(f32[25,48,128]{2,1,0:T(8,128)S(1)} %slice.98), channel_id=1, source_target_pairs={{0,8},{1,25},{2,10},{3,27},{4,12},{5,29},{6,14},{7,31},{8,16},{9,1... | collective-permute-start | bytes 1843208 | tf_op jit(solution)/shard_map/ppermute | solution.py:986
  216.3 23.6 %collective-permute-start.29 = (f32[25,48,128]{2,1,0:T(8,128)S(1)}, f32[25,48,128]{2,1,0:T(8,128)}, u32[]{:S(2)}, u32[]{:S(2)}) collective-permute-start(f32[25,48,128]{2,1,0:T(8,128)S(1)} %slice.99), channel_id=1, source_target_pairs={{0,24},{1,9},{2,26},{3,11},{4,28},{5,13},{6,30},{7,15},{8,0},{9,17... | collective-permute-start | bytes 1843208 | tf_op jit(solution)/shard_map/ppermute | solution.py:986
  226.3 11.8 %collective-permute-start.36 = (f32[25,40,128]{2,1,0:T(8,128)S(1)}, f32[25,40,128]{2,1,0:T(8,128)}, u32[]{:S(2)}, u32[]{:S(2)}) collective-permute-start(f32[25,40,128]{2,1,0:T(8,128)S(1)} %slice.102), channel_id=1, source_target_pairs={{0,2},{1,7},{2,4},{3,1},{4,6},{5,3},{6,0},{7,5},{8,10},{9,15},{10,... | collective-permute-start | bytes 1536008 | tf_op jit(solution)/shard_map/ppermute | solution.py:986
  (33 other events, 296.7 us)
where the time goes:
time: 265 us; the launch traced here: 261 us
  waiting for transfers between devices  101 us (38%)
  Pallas kernels  81.4 us (31%)
  starting transfers between devices  60.5 us (23%)
  local copies, waits for them, and re-layouts  17.5 us (7%)
    ppermute x18, waiting for transfers between devices, by_ring(): came = [lax.ppermute(x, AXES, way) for x, way in zip((one, two), ways)]  69.5 us
    pallas_call x3, Pallas kernels, route(): pl.pallas_call(functools.partial(route_kernel, stage), grid_spec=pltpu.Pr...  33.9 us
    ppermute x18, waiting for transfers between devices, by_ring(): came += [lax.ppermute(x[:on], AXES, way) for x, way in zip(came, ways)]  27.8 us
    ppermute x18, starting transfers between devices, by_ring(): came += [lax.ppermute(x[:on], AXES, way) for x, way in zip(came, ways)]  26.5 us
    ppermute x18, starting transfers between devices, by_ring(): came = [lax.ppermute(x, AXES, way) for x, way in zip((one, two), ways)]  25.2 us
    pallas_call x1, Pallas kernels, main_product(): pl.pallas_call(main_kernel, grid_spec=pltpu.PrefetchScalarGridSpec(num_sc...  18.2 us
    unnamed x48, local copies, waits for them, and re-layouts  12.2 us
    ppermute x1, starting transfers between devices, shards(): lax.ppermute(down, AXES, [((i + 1) % size, i) for i in range(size)])  8.12 us
  transfers between devices with their start and end apart: 41, of which 18 were waited for; matrix products, arithmetic and copies ran while one was open for 2% of the time, Pallas kernels for 8%

commit v1 on v0

--- a/solution.py
+++ b/solution.py
@@ -19,7 +19,9 @@
 VMEM = pltpu.VMEM
 
 
-LEFT, OUT_LEFT, OUT_RIGHT, CODE, PLAN = 64, 128, 192, 256, 384
+LEFT, OUT_LEFT, OUT_RIGHT, CODE, SLOT_A, SLOT_B, PLAN = 64, 128, 192, 256, 320, 352, 384
+HALF = B // 2
+MIDDLE = pl.ds(1, CWIN - 2)
 
 
 def split(x):
@@ -61,26 +63,40 @@
 SLOTS = {0: (0, 1, 2, 3), 1: (1, 2, 3), 2: (1, 2, 3, 4)}
 
 
+def row_copies(plan, c, row, out_a, out_b, out_outer, sems, back=False):
+    pairs = (
+        (row.at[MIDDLE, pl.ds(0, HALF)], out_a.at[plan[SLOT_A + c]]),
+        (row.at[MIDDLE, pl.ds(HALF, HALF)], out_b.at[plan[SLOT_B + c]]),
+        (row.at[0], out_outer.at[2 * c]),
+        (row.at[CWIN - 1], out_outer.at[2 * c + 1]),
+    )
+    return [
+        pltpu.make_async_copy(*((there, here) if back else (here, there)), sems.at[k])
+        for k, (here, there) in enumerate(pairs)
+    ]
+
+
 def main_kernel(
     plan,
     a_ref, p_ref, before_ref, after_ref,
-    out,
+    out_a, out_b, out_outer,
     stage, carry, sems,
 ):
     step = pl.program_id(0)
     steps = pl.num_programs(0) - 1
     buf = lax.rem(step, 2)
 
-    def copy_out(at, which, row):
+    def copies(at, which, row):
         c = 2 * at - 1 + row
-        return pltpu.make_async_copy(stage.at[which, row], out.at[c], sems.at[which, row])
+        return row_copies(plan, c, stage.at[which, row], out_a, out_b, out_outer, sems.at[which, row])
 
     def drain(at):
         which = lax.rem(at, 2)
         for row in range(2):
             @pl.when((2 * at - 1 + row >= 0) & (2 * at - 1 + row < 2 * steps))
             def _():
-                copy_out(at, which, row).wait()
+                for copy in copies(at, which, row):
+                    copy.wait()
 
     @pl.when(step >= 2)
     def _():
@@ -144,7 +160,8 @@
     for row in range(2):
         @pl.when((2 * step - 1 + row >= 0) & (2 * step - 1 + row < 2 * steps))
         def _():
-            copy_out(step, buf, row).start()
+            for copy in copies(step, buf, row):
+                copy.start()
 
     @pl.when(step == steps)
     def _():
@@ -152,7 +169,7 @@
         drain(step)
 
 
-def main_product(plan, a_tiles, p_tiles):
+def main_product(plan, a_tiles, p_tiles, count_y):
     rows = a_tiles.shape[0]
     steps = rows // W
     coarse = rows // 3
@@ -172,14 +189,18 @@
                 spec((1, KP, B, B), lambda s, *_: (jnp.maximum(jnp.minimum(s, last) * W - 1, 0), 0, 0, 0)),
                 spec((1, KP, B, B), lambda s, *_: (jnp.minimum(s * W + W, rows - 1), 0, 0, 0)),
             ],
-            out_specs=pl.BlockSpec(memory_space=pl.ANY),
+            out_specs=[ANYWHERE] * 3,
             scratch_shapes=[
                 VMEM((2, 2, CWIN, B, B), F32),
                 VMEM((2, CWIN, B, B), F32),
-                pltpu.SemaphoreType.DMA((2, 2)),
+                pltpu.SemaphoreType.DMA((2, 2, 4)),
             ],
         ),
-        out_shape=jax.ShapeDtypeStruct((coarse, CWIN, B, B), F32),
+        out_shape=[
+            jax.ShapeDtypeStruct((coarse, CWIN - 2, HALF, B), F32),
+            jax.ShapeDtypeStruct((count_y, CWIN - 2, HALF, B), F32),
+            jax.ShapeDtypeStruct((2 * coarse, B, B), F32),
+        ],
         compiler_params=pltpu.CompilerParams(
             dimension_semantics=("arbitrary",), vmem_limit_bytes=56 << 20
         ),
@@ -192,21 +213,19 @@
 
 def edge_kernel(
     plan,
-    before, after, a_first, a_last, p_first, p_last, in_rows,
-    out_rows,
+    before, after, a_first, a_last, p_first, p_last, in_a, in_b, in_outer,
+    out_a, out_b, out_outer,
     rows_ref, sems,
 ):
-    coarse = out_rows.shape[0]
+    coarse = out_a.shape[0]
     held = (0, 1, coarse - 2, coarse - 1)
 
-    def copy(n, back):
-        there, here = out_rows.at[held[n]], rows_ref.at[n]
-        if back:
-            return pltpu.make_async_copy(here, there, sems.at[n])
-        return pltpu.make_async_copy(there, here, sems.at[n])
+    def copies(n, back):
+        return row_copies(plan, held[n], rows_ref.at[n], out_a, out_b, out_outer, sems.at[n], back)
 
     for n in range(4):
-        copy(n, False).start()
+        for copy in copies(n, True):
+            copy.start()
 
     sums = []
     for side in range(2):
@@ -266,23 +285,25 @@
         sums.append((outer, inner))
 
     for n in range(4):
-        copy(n, False).wait()
+        for copy in copies(n, True):
+            copy.wait()
     for n, target in ((0, sums[0][0]), (1, sums[0][1]), (2, sums[1][1]), (3, sums[1][0])):
         for w, value in target.items():
             rows_ref[n, w] += value
     for n in range(4):
-        copy(n, True).start()
+        for copy in copies(n, False):
+            copy.start()
     for n in range(4):
-        copy(n, True).wait()
-
-
-def edge_product(plan, before, after, up, down, p_tiles, out_rows):
+        for copy in copies(n, False):
+            copy.wait()
+
+
+def edge_product(plan, before, after, up, down, p_tiles, pieces):
     rows = p_tiles.shape[0]
 
     def whole(x):
         return pl.BlockSpec(x.shape, lambda *_: (0,) * x.ndim)
 
-    anywhere = pl.BlockSpec(memory_space=pl.ANY)
     return pl.pallas_call(
         edge_kernel,
         grid_spec=pltpu.PrefetchScalarGridSpec(
@@ -294,22 +315,22 @@
                 pl.BlockSpec((1, B, B), lambda *_: (8, 0, 0)),
                 pl.BlockSpec((1, KP, B, B), lambda *_: (0, 0, 0, 0)),
                 pl.BlockSpec((1, KP, B, B), lambda *_: (rows - 1, 0, 0, 0)),
-                anywhere,
-            ],
-            out_specs=anywhere,
-            scratch_shapes=[VMEM((4, CWIN, B, B), F32), pltpu.SemaphoreType.DMA((4,))],
+            ]
+            + [ANYWHERE] * 3,
+            out_specs=[ANYWHERE] * 3,
+            scratch_shapes=[VMEM((4, CWIN, B, B), F32), pltpu.SemaphoreType.DMA((4, 4))],
         ),
-        out_shape=jax.ShapeDtypeStruct(out_rows.shape, F32),
-        input_output_aliases={7: 0},
+        out_shape=[jax.ShapeDtypeStruct(x.shape, F32) for x in pieces],
+        input_output_aliases={7: 0, 8: 1, 9: 2},
         compiler_params=pltpu.CompilerParams(
-            dimension_semantics=("arbitrary",), vmem_limit_bytes=56 << 20
+            dimension_semantics=("arbitrary",), vmem_limit_bytes=32 << 20
         ),
         cost_estimate=pl.CostEstimate(flops=2_000_000_000, bytes_accessed=10_000_000, transcendentals=0),
         name="edge_rows",
-    )(plan, before, after, down, up, p_tiles, p_tiles, out_rows)
-
-
-def plan_kernel(place, cols, length, a_tiles, p_tiles, aggregate, owners, owners_all, plan, counts, up, down, low, high, near, mine_ref, sem):
+    )(plan, before, after, down, up, p_tiles, p_tiles, *pieces)
+
+
+def plan_kernel(place, cols, length, a_tiles, p_tiles, aggregate, owners, owners_all, plan, counts, up, down, low, high, near, mine_ref, used, sem):
     fine, coarse = length.shape[0], counts.shape[0]
     wide = aggregate.shape[0]
     fine_total = wide * LANES
@@ -407,10 +428,19 @@
         row = place[0] * coarse + c
         mine = mine_ref[0, row & (LANES - 1)]
         spot = jnp.sum(jnp.where((everyone == mine) & (ids < row), 1, 0))
-        tiles = most - least + 1
-        plan[CODE + c] = mine * 1024 + spot * 64 + least * 8 + tiles
+        first_on, last_on = jnp.where(least == 0, 1, 0), jnp.where(most == CWIN - 1, 1, 0)
+        whole = mine * 1024 + spot * 64
+        plan[CODE + 2 * c] = whole + first_on
+        plan[CODE + 2 * c + 1] = whole + (CWIN - 1) * 8 + last_on
+        tiles = first_on + last_on
+        shift = ((mine >> 5) - (place[0] >> 5)) & 3
+        plan[SLOT_A + c] = shift * (coarse // 4) + used[shift]
+        plan[SLOT_B + c] = mine & 31
+        used[shift] = used[shift] + 1
         return jnp.where(ids == row, tiles, carry)
 
+    for k in range(4):
+        used[k] = 0
     tiles = lax.fori_loop(0, coarse, code, jnp.zeros(counts.shape, jnp.int32), unroll=4)
     counts[...] = tiles.astype(F32)
     for k, (here, there, on) in enumerate(sends):
@@ -449,6 +479,7 @@
                 SMEM((fine + 6,), jnp.int32),
                 SMEM((2, LANES), jnp.int32),
                 SMEM((1, LANES), jnp.int32),
+                SMEM((4,), jnp.int32),
                 pltpu.SemaphoreType.DMA((3 + 2 * halo[0],)),
             ],
         ),
@@ -458,18 +489,14 @@
             jax.ShapeDtypeStruct(halo, F32),
             jax.ShapeDtypeStruct(halo, F32),
         ],
-        compiler_params=pltpu.CompilerParams(vmem_limit_bytes=32 << 20),
+        compiler_params=pltpu.CompilerParams(vmem_limit_bytes=60 << 20),
         cost_estimate=pl.CostEstimate(flops=0, bytes_accessed=5_000_000, transcendentals=0),
         name="plan",
     )(place, a_cols.T, a_len, a_tiles, p_tiles, aggregate.reshape(-1, LANES), owners, owners)
 
 
-PARTS = (
-    (0, 48, "xyz", ((37, 14, 48), (46, 24, 48), (54, 24, 48))),
-    (48, 40, "yzx", ((49, 24, 48), (54, 24, 48), (50, 24, 48))),
-    (88, 40, "zxy", ((47, 24, 48), (64, 32, 64), (53, 24, 48))),
-)
-SWAP = 67
+PARTS = ((0, 128, "xyz", ((8, 4, 12), (10, 5, 12), (9, 5, 12))),)
+SWAP = 12
 SHIFT = {"x": 5, "z": 3, "y": 1}
 FRONTS, BACKS = LANES - 2, LANES - 1
 TABLE = pl.ds(8, 16)
@@ -480,12 +507,9 @@
 
 
 def start_tiles(count, source, target, sem):
-    for size in (4, 2, 1):
-        first = count & (8 - 2 * size)
-
-        @pl.when((count & size) != 0)
-        def _():
-            pltpu.make_async_copy(source(first, size), target(first, size), sem).start()
+    @pl.when(count > 0)
+    def _():
+        pltpu.make_async_copy(source(0, 1), target(0, 1), sem).start()
 
 
 def wait_tiles(count, one, sem):
@@ -496,16 +520,13 @@
     lax.fori_loop(0, count, step, 0)
 
 
-class Rows:
-    def __init__(self, codes, ref, first, height):
-        self.codes, self.ref, self.first, self.height = codes, ref, first, height
+class Outer:
+    def __init__(self, codes, ref):
+        self.codes, self.ref = codes, ref
 
     def walk(self, body):
         def step(k, carry):
-            code = self.codes[CODE + k]
-            tile = fields(code)[2]
-            part = pl.ds(self.first, self.height)
-            body(code, lambda at, size: self.ref.at[k, pl.ds(tile + at, size), part])
+            body(self.codes[CODE + k], lambda first, size: self.ref.at[pl.ds(k + first, size)])
             return carry
 
         lax.fori_loop(0, self.ref.shape[0], step, 0)
@@ -552,7 +573,7 @@
     return finish
 
 
-def route_kernel(stage, plan, place, *refs):
+def route_kernel(stage, behind, plan, place, *refs):
     refs = list(refs)
     parts = len(PARTS)
     if stage == 0:
@@ -560,6 +581,7 @@
         counts = refs.pop(0)
     else:
         arrivals = [[refs.pop(0) for _ in range(5)] for _ in range(parts)]
+    del refs[:behind]
     outs_of = [[refs.pop(0) for _ in range(3)] for _ in range(parts)]
     bufs = [refs.pop(0) for _ in range(parts)]
     state, copy_sem, head_sem, out_sem, table_in, table_out, table_sem = [refs.pop(0) for _ in range(7)]
@@ -614,7 +636,7 @@
         shift = SHIFT[order[stage]]
         buf, sem, head, zero = bufs[p], copy_sem.at[p], heads[p], 16 * p
         if stage == 0:
-            sources = [Rows(plan, arrivals[p][0], first_row, height)]
+            sources = [Outer(plan, arrivals[p][0])]
         else:
             sources = [
                 Slots(h, g, back)
@@ -673,7 +695,7 @@
             tiles = code & 7
             slot = state[zero + 7 + way] - tiles
 
-            @pl.when(slot >= state[zero + 4 + way])
+            @pl.when((tiles > 0) & (slot >= state[zero + 4 + way]))
             def _():
                 state[zero + 7 + way] = slot
                 entry = state[zero + 12 + way]
@@ -728,15 +750,15 @@
     return [SMEM((1, LANES), F32)] * count
 
 
-def route(stage, plan, place, got):
+def route(stage, plan, place, got, *behind):
     parts = len(PARTS)
     sizes = [(size[stage], height) for _, height, _, size in PARTS]
     result = pl.pallas_call(
-        functools.partial(route_kernel, stage),
+        functools.partial(route_kernel, stage, len(behind)),
         grid_spec=pltpu.PrefetchScalarGridSpec(
             num_scalar_prefetch=2,
             grid=(1,),
-            in_specs=[ANYWHERE] * len(got),
+            in_specs=[ANYWHERE] * (len(got) + len(behind)),
             out_specs=[ANYWHERE] * (3 * parts),
             scratch_shapes=[VMEM((2 * (send + 1) + stay + 1, height, LANES), F32) for (send, _, stay), height in sizes]
             + [
@@ -757,7 +779,7 @@
         compiler_params=pltpu.CompilerParams(vmem_limit_bytes=48 << 20),
         cost_estimate=pl.CostEstimate(flops=0, bytes_accessed=24_000_000, transcendentals=0),
         name="route",
-    )(plan, place, *got)
+    )(plan, place, *got, *behind)
     return [result[3 * p : 3 * p + 3] for p in range(parts)]
 
 
@@ -843,71 +865,119 @@
     )(place, *inputs)
 
 
-def gather_kernel(firsts, heights, place, *refs):
-    refs = list(refs)
-    parts = len(heights)
-    got = [[refs.pop(0) for _ in range(6)] for _ in range(parts)]
-    out, state, copy_sem, head_sem = [refs.pop(0) for _ in range(4)]
-    heads = [[refs.pop(0) for _ in range(6)] for _ in range(parts)]
-    copies = [
-        pltpu.make_async_copy(got[p][k].at[0, pl.ds(0, 1)], heads[p][k], head_sem.at[6 * p + k])
-        for p in range(parts)
-        for k in range(6)
-    ]
-    for copy in copies:
+def relay(pairs, sems_in, sems_out):
+    inward = [pltpu.make_async_copy(x, y, sems_in.at[k]) for k, (x, y, z) in enumerate(pairs)]
+    outward = [pltpu.make_async_copy(y, z, sems_out.at[k]) for k, (x, y, z) in enumerate(pairs)]
+    for copy in inward:
         copy.start()
+    for come, go in zip(inward, outward):
+        come.wait()
+        go.start()
+    for copy in outward:
+        copy.wait()
+
+
+def move_kernel(source_ref, target_ref, rows_in, rows_out, stage, sems_in, sems_out):
+    relay(
+        [(rows_in.at[source_ref[k]], stage.at[k], rows_out.at[target_ref[k]]) for k in range(stage.shape[0])],
+        sems_in,
+        sems_out,
+    )
+
+
+def move_rows(source, target, rows, places):
+    count = source.shape[0]
+    return pl.pallas_call(
+        move_kernel,
+        grid_spec=pltpu.PrefetchScalarGridSpec(
+            num_scalar_prefetch=2,
+            grid=(1,),
+            in_specs=[ANYWHERE],
+            out_specs=ANYWHERE,
+            scratch_shapes=[
+                VMEM((count,) + rows.shape[1:], F32),
+                pltpu.SemaphoreType.DMA((count,)),
+                pltpu.SemaphoreType.DMA((count,)),
+            ],
+        ),
+        out_shape=jax.ShapeDtypeStruct((places,) + rows.shape[1:], F32),
+        compiler_params=pltpu.CompilerParams(vmem_limit_bytes=56 << 20),
+        cost_estimate=pl.CostEstimate(flops=0, bytes_accessed=8_000_000, transcendentals=0),
+        name="move_rows",
+    )(source, target, rows)
+
+
+def join_kernel(source_a, source_b, place, rows_a, rows_b, *refs):
+    got, refs = refs[:6], refs[6:]
+    out, stage, copied, copy_sem, head_sem, sems_in, sems_out = refs[:7]
+    heads = refs[7:]
+    coarse = out.shape[0]
+    inward, outward = [], []
+    for k in range(coarse):
+        for h, (rows, source) in enumerate(((rows_a, source_a), (rows_b, source_b))):
+            inward.append(
+                pltpu.make_async_copy(
+                    rows.at[source[k]], stage.at[k, MIDDLE, pl.ds(h * HALF, HALF)], sems_in.at[2 * k + h]
+                )
+            )
+        outward.append(pltpu.make_async_copy(stage.at[k], out.at[k], sems_out.at[k]))
+    for copy in inward:
+        copy.start()
 
     def clear(k, carry):
-        out[k] = jnp.zeros(out.shape[1:], F32)
+        stage[k, 0] = jnp.zeros((B, B), F32)
+        stage[k, CWIN - 1] = jnp.zeros((B, B), F32)
         return carry
 
-    lax.fori_loop(0, out.shape[0], clear, 0)
-    for copy in copies:
+    lax.fori_loop(0, coarse, clear, 0)
+    read_headers(list(zip(got, heads)), head_sem)
+    core = place[0] & 1
+    sem = copy_sem.at[0]
+    copied[0] = 0
+
+    def assign(code, source):
+        owner, row, tile, tiles = fields(code)
+
+        @pl.when((owner & 1) == core)
+        def _():
+            start_tiles(tiles, source, lambda at, size: stage.at[row, pl.ds(tile + at, size)], sem)
+            copied[0] = copied[0] + tiles
+
+    for head, ref, back in zip(heads, got, (False, True, True, False, False, False)):
+        Slots(head, ref, back).walk(assign)
+    wait_tiles(copied[0], stage.at[0, 0], sem)
+    for k in range(coarse):
+        inward[2 * k].wait()
+        inward[2 * k + 1].wait()
+        outward[k].start()
+    for copy in outward:
         copy.wait()
-    core = place[0] & 1
-    for p in range(parts):
-        sem = copy_sem.at[p]
-        part = pl.ds(firsts[p], heights[p])
-        state[p] = 0
-
-        def assign(code, source):
-            owner, row, tile, tiles = fields(code)
-
-            @pl.when((owner & 1) == core)
-            def _():
-                start_tiles(tiles, source, lambda at, size: out.at[row, pl.ds(tile + at, size), part], sem)
-                state[p] = state[p] + tiles
-
-        for k, back in enumerate((False, True, True, False, False, False)):
-            Slots(heads[p][k], got[p][k], back).walk(assign)
-    for p in range(parts):
-        wait_tiles(state[p], out.at[0, 0, pl.ds(firsts[p], heights[p])], copy_sem.at[p])
-
-
-def gather_rows(place, got, coarse):
-    firsts = tuple(first for first, _, _, _ in PARTS)
-    heights = tuple(height for _, height, _, _ in PARTS)
-    parts = len(PARTS)
-    inputs = [x for part in got for x in part]
+
+
+def join_rows(source_a, source_b, place, rows_a, rows_b, got):
+    coarse = source_a.shape[0]
     return pl.pallas_call(
-        functools.partial(gather_kernel, firsts, heights),
+        join_kernel,
         grid_spec=pltpu.PrefetchScalarGridSpec(
-            num_scalar_prefetch=1,
+            num_scalar_prefetch=3,
             grid=(1,),
-            in_specs=[ANYWHERE] * len(inputs),
-            out_specs=pl.BlockSpec((coarse, CWIN, B, B), lambda *_: (0, 0, 0, 0)),
+            in_specs=[ANYWHERE] * (2 + len(got)),
+            out_specs=ANYWHERE,
             scratch_shapes=[
-                SMEM((4,), jnp.int32),
-                pltpu.SemaphoreType.DMA((parts,)),
-                pltpu.SemaphoreType.DMA((6 * parts,)),
+                VMEM((coarse, CWIN, B, B), F32),
+                SMEM((1,), jnp.int32),
+                pltpu.SemaphoreType.DMA((1,)),
+                pltpu.SemaphoreType.DMA((len(got),)),
+                pltpu.SemaphoreType.DMA((2 * coarse,)),
+                pltpu.SemaphoreType.DMA((coarse,)),
             ]
-            + head_scratch(6 * parts),
+            + head_scratch(len(got)),
         ),
         out_shape=jax.ShapeDtypeStruct((coarse, CWIN, B, B), F32),
         compiler_params=pltpu.CompilerParams(vmem_limit_bytes=56 << 20),
         cost_estimate=pl.CostEstimate(flops=0, bytes_accessed=16_000_000, transcendentals=0),
-        name="gather_rows",
-    )(place, *inputs)
+        name="join_rows",
+    )(source_a, source_b, place, rows_a, rows_b, *got)
 
 
 def fits_kernel(owner_ref, one_ref, two_ref, out_ref):
@@ -974,10 +1044,10 @@
     return pairs
 
 
-def by_ring(plan, place, rows, counts):
-    got = [[rows, counts]]
+def by_ring(plan, place, outer, counts, waits):
+    got = [[outer, counts]]
     for stage in range(3):
-        sent = route(stage, plan, place, [x for part in got for x in part])
+        sent = route(stage, plan, place, [x for part in got for x in part], *waits[stage])
         got = []
         for (one, two, stay), (_, _, order, sizes) in zip(sent, PARTS):
             on = sizes[stage][1] + 1
@@ -989,27 +1059,70 @@
     pairs = [(i, i ^ 1) for i in range(size)]
     other = swap_out(place, got)
     swapped = [lax.ppermute(x, AXES, pairs) for x in other]
-    return [part + [x] for part, x in zip(got, swapped)], other[0], swapped[0]
+    return got[0] + [swapped[0]], other[0], swapped[0]
 
 
 def shards(a_tiles, a_cols, a_len, p_tiles, aggregate, owner):
-    device = lax.axis_index(AXES)
-    size = lax.axis_size(AXES)
+    count_x, count_y = lax.axis_size("gx"), lax.axis_size("gy")
+    index_x, index_y = lax.axis_index("gx"), lax.axis_index("gy")
+    size = count_x * count_y
+    device = index_x * count_y + index_y
     coarse = a_tiles.shape[0] // 3
+    depth = coarse // count_x
     place = jnp.reshape(device, (1,)).astype(jnp.int32)
     plan, counts, up, down = make_plan(place, a_cols, a_len, aggregate, owner, a_tiles, p_tiles)
     before = lax.ppermute(up, AXES, [(i, (i + 1) % size) for i in range(size)])
     behind = lax.ppermute(down, AXES, [((i + 1) % size, i) for i in range(size)])
-    coarse_rows = main_product(plan, a_tiles, p_tiles)
-    coarse_rows = edge_product(plan, before, behind, up, down, p_tiles, coarse_rows)
-    got, one, two = by_ring(plan, place, coarse_rows, counts)
+    pieces = main_product(plan, a_tiles, p_tiles, count_y)
+    rows_a, rows_b, outer = edge_product(plan, before, behind, up, down, p_tiles, pieces)
+
+    table = owner.reshape(count_x, count_y, coarse)
+    order = jnp.arange(coarse)
+    shift = table[0, 0] // count_y
+    same = shift[None, :] == shift[:, None]
+    rank = jnp.sum((same & (order[None, :] < order[:, None])).astype(jnp.int32), axis=1)
+    slot = (shift * depth + rank).astype(jnp.int32)
+    from_x = (index_x - shift) % count_x
+    column = table[:, index_y] % count_y
+    mid_a_target = jnp.sum(
+        jnp.where(jnp.arange(count_x)[:, None] == from_x[None, :], column, 0), axis=0
+    ).astype(jnp.int32)
+    hit = (table[index_x] % count_y) == index_y
+    mid_b_source = jnp.sum(jnp.where(hit, jnp.arange(count_y)[:, None], 0), axis=0).astype(jnp.int32)
+    found = table.reshape(size, coarse) == device
+    sender = jnp.sum(jnp.where(found, jnp.arange(size)[:, None], 0), axis=0)
+    ids = sender * coarse + order
+    spot = jnp.sum((ids[None, :] < ids[:, None]).astype(jnp.int32), axis=1)
+    at = spot[None, :] == order[:, None]
+    last_a = jnp.sum(jnp.where(at, (sender % count_y)[None, :], 0), axis=1).astype(jnp.int32)
+    last_b = jnp.sum(jnp.where(at, slot[None, :], 0), axis=1).astype(jnp.int32)
+
+    def over_y(x):
+        return lax.all_to_all(x, "gy", split_axis=0, concat_axis=0, tiled=True)
+
+    def along_x(x):
+        parts = [x[:depth]]
+        for k in range(1, count_x):
+            pairs = [(i, (i + k) % count_x) for i in range(count_x)]
+            parts.append(lax.ppermute(x[k * depth : (k + 1) * depth], "gx", pairs))
+        return jnp.concatenate(parts, axis=0)
+
+    got_b = over_y(rows_b)
+    got_a = along_x(rows_a)
+    ring, one, two = by_ring(plan, place, outer, counts, ((got_a,), (), (got_b,)))
     fits = ring_fits(owner, one, two)
+    end_a = over_y(move_rows(slot, mid_a_target, got_a, count_y))
+    end_b = along_x(move_rows(mid_b_source, slot, got_b, coarse))
+
+    def slow(*_):
+        mine = table[index_x, index_y]
+        slots = ((mine // count_y - index_x) % count_x) * depth + rank
+        middle = jnp.concatenate([rows_a[slots], rows_b[mine % count_y]], axis=2)
+        sides = outer.reshape(coarse, 2, B, B)
+        return by_slots(jnp.concatenate([sides[:, :1], middle, sides[:, 1:]], axis=1), owner, device)
+
     return lax.cond(
-        fits,
-        lambda kept, parts: gather_rows(place, parts, coarse),
-        lambda kept, parts: by_slots(kept, owner, device),
-        coarse_rows,
-        got,
+        fits, lambda x, y, z: join_rows(last_a, last_b, place, x, y, z), slow, end_a, end_b, ring
     )
 
 

time: 265 us -> 289 us (1.091)
  waiting for transfers between devices: 101 us -> 173 us
  Pallas kernels: 81.4 us -> 57.6 us
  starting transfers between devices: 60.5 us -> 45.2 us
  local copies, waits for them, and re-layouts: 17.5 us -> 4.22 us
  other arithmetic: 0 us -> 6.64 us
    ppermute x0 -> x6, waiting for transfers between devices: none -> 57.5 us  [along_x(): parts.append(lax.ppermute(x[k * depth:(k + 1) * depth], 'gx', pairs))]
    all_to_all x0 -> x2, waiting for transfers between devices: none -> 27.4 us  [over_y(): return lax.all_to_all(x, 'gy', split_axis=0, concat_axis=0, tiled=True)]
    pallas_call x4 -> x6, Pallas kernels: 41.7 us -> 23.9 us  [the longest x3 10 us: route(): pl.pallas_call(functools.partial(route_kernel, stage, len(behind)), grid_...]
    ppermute x18 -> x6, starting transfers between devices: 26.5 us -> 10.1 us  [by_ring(): came += [lax.ppermute(x[:on], AXES, way) for x, way in zip(came, ways)]]
    ppermute x18 -> x6, starting transfers between devices: 25.2 us -> 9.91 us  [by_ring(): came = [lax.ppermute(x, AXES, way) for x, way in zip((one, two), ways)]]
    unnamed x48 -> x32, local copies, waits for them, and re-layouts: 12.2 us -> 1.3 us
    all_to_all x0 -> x2, starting transfers between devices: none -> 9.9 us  [over_y(): return lax.all_to_all(x, 'gy', split_axis=0, concat_axis=0, tiled=True)]
    ppermute x0 -> x6, starting transfers between devices: none -> 6.8 us  [along_x(): parts.append(lax.ppermute(x[k * depth:(k + 1) * depth], 'gx', pairs))]
  transfers between devices with their start and end apart: 41 -> 23, of which waited for: 18 -> 11; matrix products, arithmetic and copies ran while one was open for 2% -> 3% of each run, Pallas kernels for 8% -> 13%
where the time goes in v1:
time: 289 us; the launch traced here: 288 us
  waiting for transfers between devices  173 us (60%)
  Pallas kernels  57.6 us (20%)
  starting transfers between devices  45.2 us (16%)
  other arithmetic  6.64 us (2%)
  local copies, waits for them, and re-layouts  4.22 us (1%)
    ppermute x6, waiting for transfers between devices, by_ring(): came = [lax.ppermute(x, AXES, way) for x, way in zip((one, two), ways)]  67.3 us
    ppermute x6, waiting for transfers between devices, along_x(): parts.append(lax.ppermute(x[k * depth:(k + 1) * depth], 'gx', pairs))  57.5 us
    all_to_all x2, waiting for transfers between devices, over_y(): return lax.all_to_all(x, 'gy', split_axis=0, concat_axis=0, tiled=True)  27.4 us
    ppermute x6, waiting for transfers between devices, by_ring(): came += [lax.ppermute(x[:on], AXES, way) for x, way in zip(came, ways)]  21.1 us
    pallas_call x1, Pallas kernels, main_product(): pl.pallas_call(main_kernel, grid_spec=pltpu.PrefetchScalarGridSpec(num_sc...  18.5 us
    ppermute x6, starting transfers between devices, by_ring(): came += [lax.ppermute(x[:on], AXES, way) for x, way in zip(came, ways)]  10.1 us
    pallas_call x3, Pallas kernels, route(): pl.pallas_call(functools.partial(route_kernel, stage, len(behind)), grid_...  10 us
    ppermute x6, starting transfers between devices, by_ring(): came = [lax.ppermute(x, AXES, way) for x, way in zip((one, two), ways)]  9.91 us
  transfers between devices with their start and end apart: 23, of which 11 were waited for; matrix products, arithmetic and copies ran while one was open for 3% of the time, Pallas kernels for 13%

profile of v1, /device:TPU:0, one launch (start us, length us, event | category | flops | bytes accessed | tf_op | source)
XLA Modules:
  0.0 288.2 jit_solution(13456650675646092662)
XLA Ops:
  0.0 6.1 %plan.1 = (s32[384]{0:T(512)}, f32[16,128]{1,0:T(8,128)}, f32[17,128,128]{2,1,0:T(8,128)}, f32[17,128,128]{2,1,0:T(8,128)}) custom-call(s32[1]{0:T(128)} %bitcast.18.place, s32[3,48]{1,0:T(4,128)} %bitcast.84, s32[48]{0:T(128)} %length.1, f32[48,3,128,128]{3,2,1,0:T(8,128)} %a_ref.1, f32[48,2,128,128]{3,2,1,0:T(8,128)} %p_last.1, s32[48,128]{1,0:T(8,128)} %bitcast.81, ...), custom_call_target="tpu_custom_call" | custom-call | bytes 5000000 | tf_op jit(solution)/shard_map/plan/pallas_call | solution.py:465
  6.2 8.3 %collective-permute-start.1 = (f32[17,128,128]{2,1,0:T(8,128)}, f32[17,128,128]{2,1,0:T(8,128)}, u32[]{:S(2)}, u32[]{:S(2)}) collective-permute-start(f32[17,128,128]{2,1,0:T(8,128)} %get-tuple-element.180.a_first), channel_id=1, source_target_pairs={{1,0},{2,1},{3,2},{4,3},{5,4},{6,5},{7,6},{8,7},{9,8},{10,9},{11,1... | collective-permute-start | bytes 3342344 | tf_op jit(solution)/shard_map/ppermute | solution.py:1075
  14.4 18.5 %triple_product.1 = (f32[16,5,64,128]{3,2,1,0:T(8,128)}, f32[32,5,64,128]{3,2,1,0:T(8,128)}, f32[32,128,128]{2,1,0:T(8,128)}) custom-call(s32[384]{0:T(512)} %get-tuple-element.178.plan, f32[48,3,128,128]{3,2,1,0:T(8,128)} %a_ref.1, f32[48,2,128,128]{3,2,1,0:T(8,128)} %p_last.1, f32[48,2,128,128]{3,2,1,0:T(8,128)} %p_last.1, f32[48,2,128,128]{3,2,1,0:T(8,128)} %p_last.1), custom_call_target="tpu_custom_call" | custom-call | flops 16000000000 | bytes 24000000 | tf_op jit(solution)/shard_map/triple_product/pallas_call | solution.py:181
  34.3 6.0 %edge_rows.1 = (f32[16,5,64,128]{3,2,1,0:T(8,128)}, f32[32,5,64,128]{3,2,1,0:T(8,128)}, f32[32,128,128]{2,1,0:T(8,128)}) custom-call(s32[384]{0:T(512)S(1)} %copy-done.3, f32[17,128,128]{2,1,0:T(8,128)} %collective-permute-done.before, f32[17,128,128]{2,1,0:T(8,128)} %collective-permute-done.1.after, ...), custom_call_target="tpu_custom_call", output_to_operand_aliasing={{0}: (7, {}), {1}: (8, {}), {2}: (9, {})} | custom-call | flops 2000000000 | bytes 10000000 | tf_op jit(solution)/shard_map/edge_rows/pallas_call | solution.py:307
  40.4 5.0 %all-to-all-start.2 = ((f32[32,5,64,128]{3,2,1,0:T(8,128)}), f32[32,5,64,128]{3,2,1,0:T(8,128)}, u32[]{:S(2)}, u32[]{:S(2)}) async-start(f32[32,5,64,128]{3,2,1,0:T(8,128)} %get-tuple-element.193), calls=%async_computation.2 | async-start | bytes 10485760 | tf_op jit(solution)/shard_map/all_to_all | solution.py:1101
  45.8 2.3 collective-permute-start.3
  50.6 27.2 %collective-permute-done.2 = f32[4,5,64,128]{3,2,1,0:T(8,128)S(1)} collective-permute-done((f32[4,5,64,128]{3,2,1,0:T(8,128)S(1)}, f32[4,5,64,128]{3,2,1,0:T(8,128)S(1)}, u32[]{:S(2)}, u32[]{:S(2)}) %collective-permute-start.2) | collective-permute-done | bytes 655392 | tf_op jit(solution)/shard_map/ppermute | solution.py:1107
  78.4 1.9 pad_maximum_fusion.1.refs_2_.rows_in
  80.3 3.5 %move_rows.2 = f32[32,5,64,128]{3,2,1,0:T(8,128)} custom-call(s32[16]{0:T(128)} %multiply_add_fusion.2.source_ref.target_ref, s32[16]{0:T(128)} %fusion.22.target_ref, f32[16,5,64,128]{3,2,1,0:T(8,128)} %pad_maximum_fusion.1.refs_2_.rows_in), custom_call_target="tpu_custom_call" | custom-call | bytes 8000000 | tf_op jit(solution)/shard_map/move_rows/pallas_call | solution.py:890
  83.8 27.4 %all-to-all-done.2.refs_5_.rows_in = f32[32,5,64,128]{3,2,1,0:T(8,128)} async-done(((f32[32,5,64,128]{3,2,1,0:T(8,128)}), f32[32,5,64,128]{3,2,1,0:T(8,128)}, u32[]{:S(2)}, u32[]{:S(2)}) %all-to-all-start.2) | async-done | bytes 5242912 | tf_op jit(solution)/shard_map/all_to_all | solution.py:1101
  111.2 4.9 %all-to-all-start.3 = ((f32[32,5,64,128]{3,2,1,0:T(8,128)}), f32[32,5,64,128]{3,2,1,0:T(8,128)}, u32[]{:S(2)}, u32[]{:S(2)}) async-start(f32[32,5,64,128]{3,2,1,0:T(8,128)} %move_rows.2), calls=%async_computation.3 | async-start | bytes 10485760 | tf_op jit(solution)/shard_map/all_to_all | solution.py:1101
  116.1 4.1 %route.3 = (f32[9,128,128]{2,1,0:T(8,128)S(1)}, f32[9,128,128]{2,1,0:T(8,128)S(1)}, f32[13,128,128]{2,1,0:T(8,128)S(1)}) custom-call(s32[384]{0:T(512)S(1)} %copy-done.3, s32[1]{0:T(128)} %bitcast.18.place, f32[32,128,128]{2,1,0:T(8,128)} %get-tuple-element.184.refs_0_, f32[16,128]{1,0:T(8,128)S(1)} %copy-done.4, f32[16,5,64,128]{3,2,1,0:T(8,128)S(1)} %copy-done), custom_call_target="tpu_custom_call" | custom-call | bytes 24000000 | tf_op jit(solution)/shard_map/route/pallas_call | solution.py:756
  120.2 3.2 %collective-permute-start.6 = (f32[9,128,128]{2,1,0:T(8,128)S(1)}, f32[9,128,128]{2,1,0:T(8,128)S(1)}, u32[]{:S(2)}, u32[]{:S(2)}) collective-permute-start(f32[9,128,128]{2,1,0:T(8,128)S(1)} %get-tuple-element.189), channel_id=1, source_target_pairs={{0,96},{1,33},{2,98},{3,35},{4,100},{5,37},{6,102},{7,39},{8,104},... | collective-permute-start | bytes 1769480 | tf_op jit(solution)/shard_map/ppermute | solution.py:1055
  123.5 13.9 %collective-permute-done.5.refs_1_ = f32[9,128,128]{2,1,0:T(8,128)S(1)} collective-permute-done((f32[9,128,128]{2,1,0:T(8,128)S(1)}, f32[9,128,128]{2,1,0:T(8,128)S(1)}, u32[]{:S(2)}, u32[]{:S(2)}) %collective-permute-start.5) | collective-permute-done | bytes 589856 | tf_op jit(solution)/shard_map/ppermute | solution.py:1055
  137.5 3.3 %collective-permute-start.8 = (f32[5,128,128]{2,1,0:T(8,128)S(1)}, f32[5,128,128]{2,1,0:T(8,128)S(1)}, u32[]{:S(2)}, u32[]{:S(2)}) collective-permute-start(f32[5,128,128]{2,1,0:T(8,128)S(1)} %slice.87), channel_id=1, source_target_pairs={{0,96},{1,33},{2,98},{3,35},{4,100},{5,37},{6,102},{7,39},{8,104},... | collective-permute-start | bytes 983048 | tf_op jit(solution)/shard_map/ppermute | solution.py:1056
  140.8 7.4 %collective-permute-done.7.refs_3_ = f32[5,128,128]{2,1,0:T(8,128)S(1)} collective-permute-done((f32[5,128,128]{2,1,0:T(8,128)S(1)}, f32[5,128,128]{2,1,0:T(8,128)S(1)}, u32[]{:S(2)}, u32[]{:S(2)}) %collective-permute-start.7) | collective-permute-done | bytes 327712 | tf_op jit(solution)/shard_map/ppermute | solution.py:1056
  148.1 3.0 %route.4 = (f32[11,128,128]{2,1,0:T(8,128)S(1)}, f32[11,128,128]{2,1,0:T(8,128)S(1)}, f32[13,128,128]{2,1,0:T(8,128)S(1)}) custom-call(s32[384]{0:T(512)S(1)} %copy-done.3, s32[1]{0:T(128)} %bitcast.18.place, f32[13,128,128]{2,1,0:T(8,128)S(1)} %get-tuple-element.187.refs_0_, f32[9,128,128]{2,1,0:T(8,128)S(1)} %collective-permute-done.5.refs_1_, ...), custom_call_target="tpu_custom_call" | custom-call | bytes 24000000 | tf_op jit(solution)/shard_map/route/pallas_call | solution.py:756
  154.4 38.2 %collective-permute-done.9.refs_1_ = f32[11,128,128]{2,1,0:T(8,128)S(1)} collective-permute-done((f32[11,128,128]{2,1,0:T(8,128)S(1)}, f32[11,128,128]{2,1,0:T(8,128)S(1)}, u32[]{:S(2)}, u32[]{:S(2)}) %collective-permute-start.9) | collective-permute-done | bytes 720928 | tf_op jit(solution)/shard_map/ppermute | solution.py:1055
  193.5 2.8 collective-permute-start.12
  196.3 9.8 %collective-permute-done.11.refs_3_ = f32[6,128,128]{2,1,0:T(8,128)S(1)} collective-permute-done((f32[6,128,128]{2,1,0:T(8,128)S(1)}, f32[6,128,128]{2,1,0:T(8,128)S(1)}, u32[]{:S(2)}, u32[]{:S(2)}) %collective-permute-start.11) | collective-permute-done | bytes 393248 | tf_op jit(solution)/shard_map/ppermute | solution.py:1056
  206.0 2.9 %route.5 = (f32[10,128,128]{2,1,0:T(8,128)S(1)}, f32[10,128,128]{2,1,0:T(8,128)S(1)}, f32[13,128,128]{2,1,0:T(8,128)S(1)}) custom-call(s32[384]{0:T(512)S(1)} %copy-done.3, s32[1]{0:T(128)} %bitcast.18.place, f32[13,128,128]{2,1,0:T(8,128)S(1)} %get-tuple-element.190.refs_0_, f32[11,128,128]{2,1,0:T(8,128)S(1)} %collective-permute-done.9.refs_1_, ...), custom_call_target="tpu_custom_call" | custom-call | bytes 24000000 | tf_op jit(solution)/shard_map/route/pallas_call | solution.py:756
  209.4 2.9 %collective-permute-start.14 = (f32[10,128,128]{2,1,0:T(8,128)S(1)}, f32[10,128,128]{2,1,0:T(8,128)S(1)}, u32[]{:S(2)}, u32[]{:S(2)}) collective-permute-start(f32[10,128,128]{2,1,0:T(8,128)S(1)} %get-tuple-element.196), channel_id=1, source_target_pairs={{0,24},{1,9},{2,26},{3,11},{4,28},{5,13},{6,30},{7,15},{8,0},{9,17... | collective-permute-start | bytes 1966088 | tf_op jit(solution)/shard_map/ppermute | solution.py:1055
  212.3 15.2 %collective-permute-done.13.refs_1_ = f32[10,128,128]{2,1,0:T(8,128)S(1)} collective-permute-done((f32[10,128,128]{2,1,0:T(8,128)S(1)}, f32[10,128,128]{2,1,0:T(8,128)S(1)}, u32[]{:S(2)}, u32[]{:S(2)}) %collective-permute-start.13) | collective-permute-done | bytes 655392 | tf_op jit(solution)/shard_map/ppermute | solution.py:1055
  229.1 3.2 %collective-permute-start.16 = (f32[6,128,128]{2,1,0:T(8,128)}, f32[6,128,128]{2,1,0:T(8,128)S(1)}, u32[]{:S(2)}, u32[]{:S(2)}) collective-permute-start(f32[6,128,128]{2,1,0:T(8,128)} %slice.91), channel_id=1, source_target_pairs={{0,24},{1,9},{2,26},{3,11},{4,28},{5,13},{6,30},{7,15},{8,0},{9,17... | collective-permute-start | bytes 1179656 | tf_op jit(solution)/shard_map/ppermute | solution.py:1056
  233.1 3.5 %move_rows.3 = f32[16,5,64,128]{3,2,1,0:T(8,128)} custom-call(s32[16]{0:T(128)} %select_reduce_fusion.7.source_ref, s32[16]{0:T(128)} %multiply_add_fusion.2.source_ref.target_ref, f32[32,5,64,128]{3,2,1,0:T(8,128)} %all-to-all-done.2.refs_5_.rows_in), custom_call_target="tpu_custom_call" | custom-call | bytes 8000000 | tf_op jit(solution)/shard_map/move_rows/pallas_call | solution.py:890
  236.6 3.9 %collective-permute-done.15.refs_3_ = f32[6,128,128]{2,1,0:T(8,128)S(1)} collective-permute-done((f32[6,128,128]{2,1,0:T(8,128)}, f32[6,128,128]{2,1,0:T(8,128)S(1)}, u32[]{:S(2)}, u32[]{:S(2)}) %collective-permute-start.15) | collective-permute-done | bytes 393248 | tf_op jit(solution)/shard_map/ppermute | solution.py:1056
  240.6 2.1 swap_out.1.one_ref
  243.2 2.1 collective-permute-start.19
  246.5 29.1 %collective-permute-done.18 = f32[4,5,64,128]{3,2,1,0:T(8,128)S(1)} collective-permute-done((f32[4,5,64,128]{3,2,1,0:T(8,128)S(1)}, f32[4,5,64,128]{3,2,1,0:T(8,128)S(1)}, u32[]{:S(2)}, u32[]{:S(2)}) %collective-permute-start.18) | collective-permute-done | bytes 655392 | tf_op jit(solution)/shard_map/ppermute | solution.py:1107
  276.2 1.9 pad_maximum_fusion.2
  280.3 7.8 %conditional.1 = (f32[16,7,128,128]{3,2,1,0:T(8,128)}) conditional(s32[]{:T(128)} %bitcast.22, (f32[32,128,128]{2,1,0:T(8,128)}, s32[]{:T(128)}, s32[]{:T(128)}, s32[4,32,16]{2,1,0:T(8,128)S(1)}, s32[16]{0:T(128)S(1)}, /*index=5*/f32[16,5,64,128]{3,2,1,0:T(8,128)S(1)}, f32[32,5,64,128]{3,2,1,0:T(8,128)}, s32[2048]{0:T(1024)S(1)}, ...), branch_computations={%region_4.12_spmd, %region_12.16_spmd} | conditional | flops 5524079 | bytes 164684224 | solution.py:1124
  281.1 6.9 %join_rows.1 = f32[16,7,128,128]{3,2,1,0:T(8,128)} custom-call(s32[16]{0:T(128)} %get-tuple-element.206.source_a, s32[16]{0:T(128)} %get-tuple-element.205.source_b, s32[1]{0:T(128)} %get-tuple-element.150.place, f32[32,5,64,128]{3,2,1,0:T(8,128)} %get-tuple-element.151.rows_a, f32[16,5,64,128]{3,2,1,0:T(8,128)} %get-tuple-element.152.rows_b, ...), custom_call_target="tpu_custom_call" | custom-call | bytes 16000000 | tf_op jit(solution)/shard_map/cond/branch_1_fun/join_rows/pallas_call | solution.py:959
  (88 shorter events, 16.5 us)
Async XLA Ops:
  6.1 26.9 %collective-permute-start = (f32[17,128,128]{2,1,0:T(8,128)}, f32[17,128,128]{2,1,0:T(8,128)}, u32[]{:S(2)}, u32[]{:S(2)}) collective-permute-start(f32[17,128,128]{2,1,0:T(8,128)} %get-tuple-element.179.a_last), channel_id=1, source_target_pairs={{0,1},{1,2},{2,3},{3,4},{4,5},{5,6},{6,7},{7,8},{8,9},{9,10},{10,1... | collective-permute-start | bytes 3342344 | tf_op jit(solution)/shard_map/ppermute | solution.py:1074
  6.2 26.9 %collective-permute-start.1 = (f32[17,128,128]{2,1,0:T(8,128)}, f32[17,128,128]{2,1,0:T(8,128)}, u32[]{:S(2)}, u32[]{:S(2)}) collective-permute-start(f32[17,128,128]{2,1,0:T(8,128)} %get-tuple-element.180.a_first), channel_id=1, source_target_pairs={{1,0},{2,1},{3,2},{4,3},{5,4},{6,5},{7,6},{8,7},{9,8},{10,9},{11,1... | collective-permute-start | bytes 3342344 | tf_op jit(solution)/shard_map/ppermute | solution.py:1075
  14.4 18.6 %slice-start = ((s8[6291456]{0:T(1024)(128)(4,1)}), s8[4194304]{0:T(1024)(128)(4,1)S(1)}, s32[]{:S(2)}) async-start(s8[6291456]{0:T(1024)(128)(4,1)} %bitcast.75), calls=%async_computation.4 | async-start | bytes 8388608
  14.4 18.6 %slice-start.1 = ((s8[6291456]{0:T(1024)(128)(4,1)}), s8[2097152]{0:T(1024)(128)(4,1)S(1)}, s32[]{:S(2)}) async-start(s8[6291456]{0:T(1024)(128)(4,1)} %bitcast.75), calls=%async_computation.5 | async-start | bytes 4194304
  14.4 18.6 %copy-start.1 = (f32[17,128,128]{2,1,0:T(8,128)S(1)}, f32[17,128,128]{2,1,0:T(8,128)}, u32[]{:S(2)}) copy-start(f32[17,128,128]{2,1,0:T(8,128)} %get-tuple-element.179.a_last) | copy-start | bytes 3342340
  14.4 18.6 %copy-start.3 = (s32[384]{0:T(512)S(1)}, s32[384]{0:T(512)}, u32[]{:S(2)}) copy-start(s32[384]{0:T(512)} %get-tuple-element.178.plan) | copy-start | bytes 4612
  40.4 70.8 %all-to-all-start.2 = ((f32[32,5,64,128]{3,2,1,0:T(8,128)}), f32[32,5,64,128]{3,2,1,0:T(8,128)}, u32[]{:S(2)}, u32[]{:S(2)}) async-start(f32[32,5,64,128]{3,2,1,0:T(8,128)} %get-tuple-element.193), calls=%async_computation.2 | async-start | bytes 10485760 | tf_op jit(solution)/shard_map/all_to_all | solution.py:1101
  45.7 32.1 %collective-permute-start.2 = (f32[4,5,64,128]{3,2,1,0:T(8,128)S(1)}, f32[4,5,64,128]{3,2,1,0:T(8,128)S(1)}, u32[]{:S(2)}, u32[]{:S(2)}) collective-permute-start(f32[4,5,64,128]{3,2,1,0:T(8,128)S(1)} %get-tuple-element.227), channel_id=1, source_target_pairs={{0,32},{32,64},{64,96},{96,0},{1,33},{33,65},{65,97},{97,1},{2,34}... | collective-permute-start | bytes 1966088 | tf_op jit(solution)/shard_map/ppermute | solution.py:1107
  45.8 32.0 %collective-permute-start.3 = (f32[4,5,64,128]{3,2,1,0:T(8,128)S(1)}, f32[4,5,64,128]{3,2,1,0:T(8,128)S(1)}, u32[]{:S(2)}, u32[]{:S(2)}) collective-permute-start(f32[4,5,64,128]{3,2,1,0:T(8,128)S(1)} %get-tuple-element.226), channel_id=1, source_target_pairs={{0,64},{32,96},{64,0},{96,32},{1,65},{33,97},{65,1},{97,33},{2,66}... | collective-permute-start | bytes 1966088 | tf_op jit(solution)/shard_map/ppermute | solution.py:1107
  48.1 30.3 %collective-permute-start.4 = (f32[4,5,64,128]{3,2,1,0:T(8,128)S(1)}, f32[4,5,64,128]{3,2,1,0:T(8,128)S(1)}, u32[]{:S(2)}, u32[]{:S(2)}) collective-permute-start(f32[4,5,64,128]{3,2,1,0:T(8,128)S(1)} %get-tuple-element.225), channel_id=1, source_target_pairs={{0,96},{32,0},{64,32},{96,64},{1,97},{33,1},{65,33},{97,65},{2,98}... | collective-permute-start | bytes 1966088 | tf_op jit(solution)/shard_map/ppermute | solution.py:1107
  83.8 32.3 %copy-start = (f32[16,5,64,128]{3,2,1,0:T(8,128)S(1)}, f32[16,5,64,128]{3,2,1,0:T(8,128)}, u32[]{:S(2)}) copy-start(f32[16,5,64,128]{3,2,1,0:T(8,128)} %pad_maximum_fusion.1.refs_2_.rows_in) | copy-start | bytes 7864324
  83.8 32.3 %copy-start.4 = (f32[16,128]{1,0:T(8,128)S(1)}, f32[16,128]{1,0:T(8,128)}, u32[]{:S(2)}) copy-start(f32[16,128]{1,0:T(8,128)} %get-tuple-element.185.refs_1_) | copy-start | bytes 24580
  111.2 169.1 %all-to-all-start.3 = ((f32[32,5,64,128]{3,2,1,0:T(8,128)}), f32[32,5,64,128]{3,2,1,0:T(8,128)}, u32[]{:S(2)}, u32[]{:S(2)}) async-start(f32[32,5,64,128]{3,2,1,0:T(8,128)} %move_rows.2), calls=%async_computation.3 | async-start | bytes 10485760 | tf_op jit(solution)/shard_map/all_to_all | solution.py:1101
  120.2 17.2 %collective-permute-start.5 = (f32[9,128,128]{2,1,0:T(8,128)S(1)}, f32[9,128,128]{2,1,0:T(8,128)S(1)}, u32[]{:S(2)}, u32[]{:S(2)}) collective-permute-start(f32[9,128,128]{2,1,0:T(8,128)S(1)} %get-tuple-element.188), channel_id=1, source_target_pairs={{0,32},{1,97},{2,34},{3,99},{4,36},{5,101},{6,38},{7,103},{8,40},{... | collective-permute-start | bytes 1769480 | tf_op jit(solution)/shard_map/ppermute | solution.py:1055
  120.2 17.2 %collective-permute-start.6 = (f32[9,128,128]{2,1,0:T(8,128)S(1)}, f32[9,128,128]{2,1,0:T(8,128)S(1)}, u32[]{:S(2)}, u32[]{:S(2)}) collective-permute-start(f32[9,128,128]{2,1,0:T(8,128)S(1)} %get-tuple-element.189), channel_id=1, source_target_pairs={{0,96},{1,33},{2,98},{3,35},{4,100},{5,37},{6,102},{7,39},{8,104},... | collective-permute-start | bytes 1769480 | tf_op jit(solution)/shard_map/ppermute | solution.py:1055
  137.4 10.8 %collective-permute-start.7 = (f32[5,128,128]{2,1,0:T(8,128)S(1)}, f32[5,128,128]{2,1,0:T(8,128)S(1)}, u32[]{:S(2)}, u32[]{:S(2)}) collective-permute-start(f32[5,128,128]{2,1,0:T(8,128)S(1)} %slice.86), channel_id=1, source_target_pairs={{0,32},{1,97},{2,34},{3,99},{4,36},{5,101},{6,38},{7,103},{8,40},{... | collective-permute-start | bytes 983048 | tf_op jit(solution)/shard_map/ppermute | solution.py:1056
  137.5 10.7 %collective-permute-start.8 = (f32[5,128,128]{2,1,0:T(8,128)S(1)}, f32[5,128,128]{2,1,0:T(8,128)S(1)}, u32[]{:S(2)}, u32[]{:S(2)}) collective-permute-start(f32[5,128,128]{2,1,0:T(8,128)S(1)} %slice.87), channel_id=1, source_target_pairs={{0,96},{1,33},{2,98},{3,35},{4,100},{5,37},{6,102},{7,39},{8,104},... | collective-permute-start | bytes 983048 | tf_op jit(solution)/shard_map/ppermute | solution.py:1056
  151.1 41.5 %collective-permute-start.9 = (f32[11,128,128]{2,1,0:T(8,128)S(1)}, f32[11,128,128]{2,1,0:T(8,128)S(1)}, u32[]{:S(2)}, u32[]{:S(2)}) collective-permute-start(f32[11,128,128]{2,1,0:T(8,128)S(1)} %get-tuple-element.191), channel_id=1, source_target_pairs={{0,2},{1,7},{2,4},{3,1},{4,6},{5,3},{6,0},{7,5},{8,10},{9,15},{10,... | collective-permute-start | bytes 2162696 | tf_op jit(solution)/shard_map/ppermute | solution.py:1055
  152.7 40.7 %collective-permute-start.10 = (f32[11,128,128]{2,1,0:T(8,128)S(1)}, f32[11,128,128]{2,1,0:T(8,128)S(1)}, u32[]{:S(2)}, u32[]{:S(2)}) collective-permute-start(f32[11,128,128]{2,1,0:T(8,128)S(1)} %get-tuple-element.192), channel_id=1, source_target_pairs={{0,6},{1,3},{2,0},{3,5},{4,2},{5,7},{6,4},{7,1},{8,14},{9,11},{10,... | collective-permute-start | bytes 2162696 | tf_op jit(solution)/shard_map/ppermute | solution.py:1055
  192.7 13.3 %collective-permute-start.11 = (f32[6,128,128]{2,1,0:T(8,128)S(1)}, f32[6,128,128]{2,1,0:T(8,128)S(1)}, u32[]{:S(2)}, u32[]{:S(2)}) collective-permute-start(f32[6,128,128]{2,1,0:T(8,128)S(1)} %slice.88), channel_id=1, source_target_pairs={{0,2},{1,7},{2,4},{3,1},{4,6},{5,3},{6,0},{7,5},{8,10},{9,15},{10,... | collective-permute-start | bytes 1179656 | tf_op jit(solution)/shard_map/ppermute | solution.py:1056
  193.5 12.5 %collective-permute-start.12 = (f32[6,128,128]{2,1,0:T(8,128)S(1)}, f32[6,128,128]{2,1,0:T(8,128)S(1)}, u32[]{:S(2)}, u32[]{:S(2)}) collective-permute-start(f32[6,128,128]{2,1,0:T(8,128)S(1)} %slice.89), channel_id=1, source_target_pairs={{0,6},{1,3},{2,0},{3,5},{4,2},{5,7},{6,4},{7,1},{8,14},{9,11},{10,... | collective-permute-start | bytes 1179656 | tf_op jit(solution)/shard_map/ppermute | solution.py:1056
  209.0 31.6 %copy-start.11 = (f32[13,128,128]{2,1,0:T(8,128)}, f32[13,128,128]{2,1,0:T(8,128)S(1)}, u32[]{:S(2)}) copy-start(f32[13,128,128]{2,1,0:T(8,128)S(1)} %get-tuple-element.194.refs_0_) | copy-start | bytes 2555908
  209.0 18.5 %collective-permute-start.13 = (f32[10,128,128]{2,1,0:T(8,128)S(1)}, f32[10,128,128]{2,1,0:T(8,128)S(1)}, u32[]{:S(2)}, u32[]{:S(2)}) collective-permute-start(f32[10,128,128]{2,1,0:T(8,128)S(1)} %get-tuple-element.195), channel_id=1, source_target_pairs={{0,8},{1,25},{2,10},{3,27},{4,12},{5,29},{6,14},{7,31},{8,16},{9,1... | collective-permute-start | bytes 1966088 | tf_op jit(solution)/shard_map/ppermute | solution.py:1055
  209.4 18.9 %collective-permute-start.14 = (f32[10,128,128]{2,1,0:T(8,128)S(1)}, f32[10,128,128]{2,1,0:T(8,128)S(1)}, u32[]{:S(2)}, u32[]{:S(2)}) collective-permute-start(f32[10,128,128]{2,1,0:T(8,128)S(1)} %get-tuple-element.196), channel_id=1, source_target_pairs={{0,24},{1,9},{2,26},{3,11},{4,28},{5,13},{6,30},{7,15},{8,0},{9,17... | collective-permute-start | bytes 1966088 | tf_op jit(solution)/shard_map/ppermute | solution.py:1055
  228.3 12.3 %collective-permute-start.15 = (f32[6,128,128]{2,1,0:T(8,128)}, f32[6,128,128]{2,1,0:T(8,128)S(1)}, u32[]{:S(2)}, u32[]{:S(2)}) collective-permute-start(f32[6,128,128]{2,1,0:T(8,128)} %slice.90), channel_id=1, source_target_pairs={{0,8},{1,25},{2,10},{3,27},{4,12},{5,29},{6,14},{7,31},{8,16},{9,1... | collective-permute-start | bytes 1179656 | tf_op jit(solution)/shard_map/ppermute | solution.py:1056
  228.3 12.3 %copy-start.9 = (f32[10,128,128]{2,1,0:T(8,128)}, f32[10,128,128]{2,1,0:T(8,128)S(1)}, u32[]{:S(2)}) copy-start(f32[10,128,128]{2,1,0:T(8,128)S(1)} %collective-permute-done.14.refs_2_) | copy-start | bytes 1966084
  229.1 11.4 %collective-permute-start.16 = (f32[6,128,128]{2,1,0:T(8,128)}, f32[6,128,128]{2,1,0:T(8,128)S(1)}, u32[]{:S(2)}, u32[]{:S(2)}) collective-permute-start(f32[6,128,128]{2,1,0:T(8,128)} %slice.91), channel_id=1, source_target_pairs={{0,24},{1,9},{2,26},{3,11},{4,28},{5,13},{6,30},{7,15},{8,0},{9,17... | collective-permute-start | bytes 1179656 | tf_op jit(solution)/shard_map/ppermute | solution.py:1056
  236.6 6.1 %copy-start.7 = (f32[16,5,64,128]{3,2,1,0:T(8,128)S(1)}, f32[16,5,64,128]{3,2,1,0:T(8,128)}, u32[]{:S(2)}) copy-start(f32[16,5,64,128]{3,2,1,0:T(8,128)} %move_rows.3) | copy-start | bytes 7864324
  242.7 35.4 %collective-permute-start.17 = (f32[13,128,128]{2,1,0:T(8,128)S(1)}, f32[13,128,128]{2,1,0:T(8,128)S(1)}, u32[]{:S(2)}, u32[]{:S(2)}) collective-permute-start(f32[13,128,128]{2,1,0:T(8,128)S(1)} %swap_out.1.one_ref), channel_id=1, source_target_pairs={{0,1},{1,0},{2,3},{3,2},{4,5},{5,4},{6,7},{7,6},{8,9},{9,8},{10,11... | collective-permute-start | bytes 2555912 | tf_op jit(solution)/shard_map/ppermute | solution.py:1061
  243.1 32.4 %collective-permute-start.18 = (f32[4,5,64,128]{3,2,1,0:T(8,128)S(1)}, f32[4,5,64,128]{3,2,1,0:T(8,128)S(1)}, u32[]{:S(2)}, u32[]{:S(2)}) collective-permute-start(f32[4,5,64,128]{3,2,1,0:T(8,128)S(1)} %get-tuple-element.223), channel_id=1, source_target_pairs={{0,32},{32,64},{64,96},{96,0},{1,33},{33,65},{65,97},{97,1},{2,34}... | collective-permute-start | bytes 1966088 | tf_op jit(solution)/shard_map/ppermute | solution.py:1107
  243.2 32.4 %collective-permute-start.19 = (f32[4,5,64,128]{3,2,1,0:T(8,128)S(1)}, f32[4,5,64,128]{3,2,1,0:T(8,128)S(1)}, u32[]{:S(2)}, u32[]{:S(2)}) collective-permute-start(f32[4,5,64,128]{3,2,1,0:T(8,128)S(1)} %get-tuple-element.222), channel_id=1, source_target_pairs={{0,64},{32,96},{64,0},{96,32},{1,65},{33,97},{65,1},{97,33},{2,66}... | collective-permute-start | bytes 1966088 | tf_op jit(solution)/shard_map/ppermute | solution.py:1107
  245.3 30.9 %collective-permute-start.20 = (f32[4,5,64,128]{3,2,1,0:T(8,128)S(1)}, f32[4,5,64,128]{3,2,1,0:T(8,128)S(1)}, u32[]{:S(2)}, u32[]{:S(2)}) collective-permute-start(f32[4,5,64,128]{3,2,1,0:T(8,128)S(1)} %get-tuple-element.221), channel_id=1, source_target_pairs={{0,96},{32,0},{64,32},{96,64},{1,97},{33,1},{65,33},{97,65},{2,98}... | collective-permute-start | bytes 1966088 | tf_op jit(solution)/shard_map/ppermute | solution.py:1107
  (7 other events, 22.1 us)

commit v2 on v1

v2 whole, which is shorter than its diff:
```python
import functools

import jax
import jax.numpy as jnp
from jax import lax
from jax.experimental import pallas as pl
from jax.experimental.pallas import tpu as pltpu
from jax.sharding import PartitionSpec as P

B = 128
KP = 2
LANES = 128
CWIN = 7
W = 6
BF = jnp.bfloat16
F32 = jnp.float32
SMEM = pltpu.SMEM
ANYWHERE = pl.BlockSpec(memory_space=pl.ANY)
VMEM = pltpu.VMEM


LEFT, OUT_LEFT, OUT_RIGHT, CODE, SLOT_A, SLOT_B, PLAN = 64, 128, 192, 256, 320, 352, 384
HALF = B // 2
MIDDLE = pl.ds(1, CWIN - 2)


def split(x):
    high = x.astype(BF)
    return high, (x - high.astype(F32)).astype(BF)


def left_operand(x):
    high, low = split(x)
    return jnp.concatenate([high, low, high], axis=1)


def right_operand(x):
    high, low = split(x)
    return jnp.concatenate([high, high, low], axis=0)


def matmul(left, right):
    return jnp.dot(left, right, preferred_element_type=F32)


def spread(total, flag, base, pair, slots):
    first, second = pair
    values = {
        base - 1: jnp.where(flag, first, 0.0),
        base: jnp.where(flag, second, first),
        base + 1: jnp.where(flag, 0.0, second),
    }
    for s, value in values.items():
        if s in slots:
            total[s] = value if total.get(s) is None else total[s] + value


def row_product(p_pair, tiles):
    turned = jnp.concatenate([p_pair[0].T, p_pair[1].T], axis=0)
    return matmul(left_operand(turned), right_operand(jnp.concatenate(tiles, axis=1)))


SLOTS = {0: (0, 1, 2, 3), 1: (1, 2, 3), 2: (1, 2, 3, 4)}


def row_copies(plan, c, row, out_a, out_b, out_outer, sems, back=False):
    pairs = (
        (row.at[MIDDLE, pl.ds(0, HALF)], out_a.at[plan[SLOT_A + c]]),
        (row.at[MIDDLE, pl.ds(HALF, HALF)], out_b.at[plan[SLOT_B + c]]),
        (row.at[0], out_outer.at[2 * c]),
        (row.at[CWIN - 1], out_outer.at[2 * c + 1]),
    )
    return [
        pltpu.make_async_copy(*((there, here) if back else (here, there)), sems.at[k])
        for k, (here, there) in enumerate(pairs)
    ]


def main_kernel(
    plan,
    a_ref, p_ref, before_ref, after_ref, behind_ref,
    out_a, out_b, out_outer,
    stage, carry, sems,
):
    step = pl.program_id(0)
    steps = pl.num_programs(0) - 1
    buf = lax.rem(step, 2)

    def copies(at, which, row):
        c = 2 * at - 1 + row
        return row_copies(plan, c, stage.at[which, row], out_a, out_b, out_outer, sems.at[which, row])

    def drain(at):
        which = lax.rem(at, 2)
        for row in range(2):
            @pl.when((2 * at - 1 + row >= 0) & (2 * at - 1 + row < 2 * steps))
            def _():
                for copy in copies(at, which, row):
                    copy.wait()

    @pl.when(step >= 2)
    def _():
        drain(step - 2)

    @pl.when(step == 0)
    def _():
        carry[...] = jnp.zeros_like(carry)

    stage[buf, 0] = carry[0]
    stage[buf, 1] = carry[1]

    @pl.when(step < steps)
    def _():
        carry[...] = jnp.zeros_like(carry)
        first = step * W
        flags = {q: plan[first + q + 4] > 0 for q in range(-1, W + 1)}

        def p_tile(q, m):
            if q < 0:
                return before_ref[0, m]
            if q >= W:
                return after_ref[0, m]
            return p_ref[q, m]

        lefts = {}
        for r in range(W):
            tiles = {
                0: jnp.where(plan[OUT_LEFT + first + r] > 0, a_ref[r, plan[LEFT + first + r]], 0.0),
                1: a_ref[r, 0],
                2: jnp.where(plan[OUT_RIGHT + first + r] > 0, a_ref[r, 3 - plan[LEFT + first + r]], 0.0),
            }
            for k in range(3):
                lefts[r, r + k - 1] = left_operand(tiles[k])
        total = {r: {} for r in range(W)}
        for q in range(-1, W + 1):
            rows = [r for r in (q - 1, q, q + 1) if 0 <= r < W]
            right = right_operand(jnp.concatenate([p_tile(q, 0), p_tile(q, 1)], axis=1))
            product = matmul(jnp.concatenate([lefts[r, q] for r in rows], axis=0), right)
            for n, r in enumerate(rows):
                pair = (product[n * B : (n + 1) * B, :B], product[n * B : (n + 1) * B, B:])
                spread(total[r], flags[q], q // 3 - r // 3 + 2, pair, SLOTS[r % 3])
        for r in range(W):
            slots = SLOTS[r % 3]
            product = row_product((p_ref[r, 0], p_ref[r, 1]), [total[r][s] for s in slots])
            g = r // 3
            for n, s in enumerate(slots):
                one = product[:B, n * B : (n + 1) * B]
                two = product[B:, n * B : (n + 1) * B]
                for delta, value in (
                    (-1, jnp.where(flags[r], one, 0.0)),
                    (0, jnp.where(flags[r], two, one)),
                    (1, jnp.where(flags[r], 0.0, two)),
                ):
                    place = g + delta + 1
                    if place < 2:
                        stage[buf, place, s + 1 - delta] += value
                    else:
                        carry[place - 2, s + 1 - delta] += value

    for row in range(2):
        @pl.when((2 * step - 1 + row >= 0) & (2 * step - 1 + row < 2 * steps))
        def _():
            for copy in copies(step, buf, row):
                copy.start()

    @pl.when(step == steps)
    def _():
        drain(step - 1)
        drain(step)


def main_product(plan, a_tiles, p_tiles, count_y, behind):
    rows = a_tiles.shape[0]
    steps = rows // W
    coarse = rows // 3
    last = steps - 1

    def spec(shape, index):
        return pl.BlockSpec(shape, index)

    return pl.pallas_call(
        main_kernel,
        grid_spec=pltpu.PrefetchScalarGridSpec(
            num_scalar_prefetch=1,
            grid=(steps + 1,),
            in_specs=[
                spec((W, 3, B, B), lambda s, *_: (jnp.minimum(s, last), 0, 0, 0)),
                spec((W, KP, B, B), lambda s, *_: (jnp.minimum(s, last), 0, 0, 0)),
                spec((1, KP, B, B), lambda s, *_: (jnp.maximum(jnp.minimum(s, last) * W - 1, 0), 0, 0, 0)),
                spec((1, KP, B, B), lambda s, *_: (jnp.minimum(s * W + W, rows - 1), 0, 0, 0)),
                ANYWHERE,
            ],
            out_specs=[ANYWHERE] * 3,
            scratch_shapes=[
                VMEM((2, 2, CWIN, B, B), F32),
                VMEM((2, CWIN, B, B), F32),
                pltpu.SemaphoreType.DMA((2, 2, 4)),
            ],
        ),
        out_shape=[
            jax.ShapeDtypeStruct((coarse, CWIN - 2, HALF, B), F32),
            jax.ShapeDtypeStruct((count_y, CWIN - 2, HALF, B), F32),
            jax.ShapeDtypeStruct((2 * coarse, B, B), F32),
        ],
        compiler_params=pltpu.CompilerParams(
            dimension_semantics=("arbitrary",), vmem_limit_bytes=56 << 20
        ),
        cost_estimate=pl.CostEstimate(
            flops=16_000_000_000, bytes_accessed=24_000_000, transcendentals=0
        ),
        name="triple_product",
    )(plan, a_tiles, p_tiles, p_tiles, p_tiles, behind)


def edge_kernel(
    plan,
    before, after, a_first, a_last, p_first, p_last, in_a, in_b, in_outer,
    out_a, out_b, out_outer,
    rows_ref, sems,
):
    coarse = out_a.shape[0]
    held = (0, 1, coarse - 2, coarse - 1)

    def copies(n, back):
        return row_copies(plan, held[n], rows_ref.at[n], out_a, out_b, out_outer, sems.at[n], back)

    for n in range(4):
        for copy in copies(n, True):
            copy.start()

    sums = []
    for side in range(2):
        halo = (before, after)[side]
        a_edge = (a_first, a_last)[side]
        own_p = (p_first, p_last)[side]
        own_flag = plan[(4, 3 * coarse + 3)[side]] > 0
        flags, tiles, p_at = {}, {}, {}
        for n in range(4):
            q = n - 1 if side == 0 else n
            flags[q] = plan[(0, 3 * coarse + 4)[side] + n] > 0
            p_at[q] = (halo[9 + 2 * n], halo[10 + 2 * n])
        near = 3 if side == 0 else -1
        flags[near] = own_flag
        p_at[near] = (own_p[0, 0], own_p[0, 1])
        total = {r: {} for r in range(3)}
        total[near] = {}
        for q in range(-1, 4):
            rows = [r for r in (q - 1, q, q + 1) if 0 <= r < 3]
            lefts = [left_operand(halo[3 * r + q - r + 1]) for r in rows]
            if q == (2 if side == 0 else 0):
                rows.append(near)
                lefts.append(left_operand(a_edge[0]))
            right = right_operand(jnp.concatenate(p_at[q], axis=1))
            product = matmul(jnp.concatenate(lefts, axis=0), right)
            for n, r in enumerate(rows):
                pair = (product[n * B : (n + 1) * B, :B], product[n * B : (n + 1) * B, B:])
                base = q // 3 - r // 3 + 2
                slots = SLOTS[r % 3] if r != near else (base - 1, base, base + 1)
                spread(total[r], flags[q], base, pair, slots)
        outer, inner = {}, {}

        def put(target, w, value):
            target[w] = value if w not in target else target[w] + value

        for r in range(3):
            slots = sorted(total[r])
            pick = 1 if side == 0 else 0
            turned = left_operand(p_at[r][pick].T)
            product = matmul(turned, right_operand(jnp.concatenate([total[r][s] for s in slots], axis=1)))
            for n, s in enumerate(slots):
                value = product[:, n * B : (n + 1) * B]
                if side == 0:
                    put(outer, s, jnp.where(flags[r], 0.0, value))
                else:
                    put(outer, s + 2, jnp.where(flags[r], value, 0.0))
        slots = sorted(total[near])
        product = row_product(p_at[near], [total[near][s] for s in slots])
        for n, s in enumerate(slots):
            one = product[:B, n * B : (n + 1) * B]
            two = product[B:, n * B : (n + 1) * B]
            put(outer, s + 1, jnp.where(own_flag, two, one))
            if side == 0:
                put(inner, s, jnp.where(own_flag, 0.0, two))
            else:
                put(inner, s + 2, jnp.where(own_flag, one, 0.0))
        sums.append((outer, inner))

    for n in range(4):
        for copy in copies(n, True):
            copy.wait()
    for n, target in ((0, sums[0][0]), (1, sums[0][1]), (2, sums[1][1]), (3, sums[1][0])):
        for w, value in target.items():
            rows_ref[n, w] += value
    for n in range(4):
        for copy in copies(n, False):
            copy.start()
    for n in range(4):
        for copy in copies(n, False):
            copy.wait()


def edge_product(plan, before, after, up, down, p_tiles, pieces):
    rows = p_tiles.shape[0]

    def whole(x):
        return pl.BlockSpec(x.shape, lambda *_: (0,) * x.ndim)

    return pl.pallas_call(
        edge_kernel,
        grid_spec=pltpu.PrefetchScalarGridSpec(
            num_scalar_prefetch=1,
            grid=(1,),
            in_specs=[whole(before), whole(after)]
            + [
                pl.BlockSpec((1, B, B), lambda *_: (0, 0, 0)),
                pl.BlockSpec((1, B, B), lambda *_: (8, 0, 0)),
                pl.BlockSpec((1, KP, B, B), lambda *_: (0, 0, 0, 0)),
                pl.BlockSpec((1, KP, B, B), lambda *_: (rows - 1, 0, 0, 0)),
            ]
            + [ANYWHERE] * 3,
            out_specs=[ANYWHERE] * 3,
            scratch_shapes=[VMEM((4, CWIN, B, B), F32), pltpu.SemaphoreType.DMA((4, 4))],
        ),
        out_shape=[jax.ShapeDtypeStruct(x.shape, F32) for x in pieces],
        input_output_aliases={7: 0, 8: 1, 9: 2},
        compiler_params=pltpu.CompilerParams(
            dimension_semantics=("arbitrary",), vmem_limit_bytes=32 << 20
        ),
        cost_estimate=pl.CostEstimate(flops=2_000_000_000, bytes_accessed=10_000_000, transcendentals=0),
        name="edge_rows",
    )(plan, before, after, down, up, p_tiles, p_tiles, *pieces)


def plan_kernel(place, cols, length, a_tiles, p_tiles, aggregate, owners, owners_all, plan, counts, up, down, near, mine_ref, spots, used, sem):
    fine = length.shape[0]
    coarse = fine // 3
    coarse_total = owners.shape[0] * LANES
    wide = aggregate.shape[0]
    fine_total = wide * LANES
    first = place[0] * fine
    line = jnp.where(first < 4, wide - 1, (first - 4) >> 7)
    begin = jnp.where(first < 4, LANES - 4, (first - 4) & (LANES - 1))
    lines = (line, jnp.where(line == wide - 1, 0, line + 1))
    index_loads = [
        pltpu.make_async_copy(aggregate.at[pl.ds(at, 1)], near.at[pl.ds(n, 1)], sem.at[n]) for n, at in enumerate(lines)
    ]
    row_before = (place[0] * coarse - 1) & (coarse_total - 1)
    line = row_before >> 7
    for n, at in enumerate((line, (line + 1) & (owners.shape[0] - 1))):
        index_loads.append(pltpu.make_async_copy(owners.at[pl.ds(at, 1)], mine_ref.at[pl.ds(n, 1)], sem.at[2 + n]))
    for load in index_loads:
        load.start()

    def entry(i):
        before = first + i - 1
        before = jnp.where(before < 0, fine_total - 1, before)
        left = jnp.where(cols[1, i] == before, 1, 2)
        return left, length[i] > left, length[i] > 3 - left

    sends = []
    for out, row, p_row in ((up, fine - 3, fine - 4), (down, 0, 0)):
        for r in range(3):
            left, on_left, on_right = entry(row + r)
            for k, slot, on in ((0, left, on_left), (2, 3 - left, on_right)):
                sends.append((a_tiles.at[row + r, slot], out.at[3 * r + k], on))
            sends.append((a_tiles.at[row + r, 0], out.at[3 * r + 1], None))
        for n in range(4):
            for m in range(KP):
                sends.append((p_tiles.at[p_row + n, m], out.at[9 + 2 * n + m], None))
    for k, (here, there, on) in enumerate(sends):
        if on is None:
            pltpu.make_async_copy(here, there, sem.at[4 + k]).start()
        else:

            @pl.when(on)
            def _():
                pltpu.make_async_copy(here, there, sem.at[4 + k]).start()

            @pl.when(jnp.logical_not(on))
            def _():
                there[...] = jnp.zeros(there.shape, F32)

    def flag(k, carry):
        row = first + k - 4
        row = jnp.where(row < 0, row + fine_total, jnp.where(row >= fine_total, row - fine_total, row))
        at = begin + k
        plan[k] = jnp.where(near[at >> 7, at & (LANES - 1)] != lax.div(row, 3), 1, 0)
        return carry

    for load in index_loads:
        load.wait()
    lax.fori_loop(0, fine + 8, flag, 0, unroll=8)

    def group(g, carry):
        for mod in range(3):
            i = 3 * g + mod
            left, on_left, on_right = entry(i)
            plan[LEFT + i] = left
            plan[OUT_LEFT + i] = jnp.where(on_left & (i > 0), 1, 0)
            plan[OUT_RIGHT + i] = jnp.where(on_right & (i < fine - 1), 1, 0)
            if mod == 0:
                plan[CODE + 2 * g] = jnp.where(on_left & (plan[i + 4] == 0) & (plan[i + 3] == 1), 1, 0)
            if mod == 2:
                plan[CODE + 2 * g + 1] = jnp.where(on_right & (plan[i + 4] == 1) & (plan[i + 5] == 0), 1, 0)
        return carry

    lax.fori_loop(0, coarse, group, 0, unroll=4)
    everyone = owners_all[...]
    ids = lax.broadcasted_iota(jnp.int32, everyone.shape, 0) * LANES + lax.broadcasted_iota(
        jnp.int32, everyone.shape, 1
    )

    def owner_of(k):
        at = (row_before & (LANES - 1)) + k
        return mine_ref[at >> 7, at & (LANES - 1)]

    def spot(k, carry):
        row = (row_before + k) & (coarse_total - 1)
        spots[k] = jnp.sum(jnp.where((everyone == owner_of(k)) & (ids < row), 1, 0))
        return carry

    lax.fori_loop(0, coarse + 2, spot, 0, unroll=6)
    for k in range(4):
        used[k] = 0
    cells = lax.broadcasted_iota(jnp.int32, counts.shape, 0) * LANES + lax.broadcasted_iota(
        jnp.int32, counts.shape, 1
    )

    def code(g, carry):
        for side, k in ((0, g + 2), (1, g)):
            on = plan[CODE + 2 * g + side]
            plan[CODE + 2 * g + side] = owner_of(k) * 1024 + spots[k] * 64 + side * (CWIN - 1) * 8 + on
            cell = side * coarse_total + ((row_before + k) & (coarse_total - 1))
            carry = jnp.where(cells == cell, on, carry)
        mine = owner_of(g + 1)
        shift = ((mine >> 5) - (place[0] >> 5)) & 3
        plan[SLOT_A + g] = shift * (coarse // 4) + used[shift]
        plan[SLOT_B + g] = mine & 31
        used[shift] = used[shift] + 1
        return carry

    ones = lax.fori_loop(0, coarse, code, jnp.zeros(counts.shape, jnp.int32), unroll=4)
    counts[...] = ones.astype(F32)
    for k, (here, there, on) in enumerate(sends):
        if on is None:
            pltpu.make_async_copy(here, there, sem.at[4 + k]).wait()
        else:

            @pl.when(on)
            def _():
                pltpu.make_async_copy(here, there, sem.at[4 + k]).wait()


def make_plan(place, a_cols, a_len, aggregate, owner, a_tiles, p_tiles):
    fine = a_len.shape[0]
    coarse = fine // 3
    owners = owner.reshape(-1, LANES)

    def whole(shape):
        return pl.BlockSpec(shape, lambda *_: (0,) * len(shape))

    halo = (9 + 4 * KP, B, B)
    return pl.pallas_call(
        plan_kernel,
        grid_spec=pltpu.PrefetchScalarGridSpec(
            num_scalar_prefetch=3,
            grid=(1,),
            in_specs=[ANYWHERE] * 4 + [whole(owners.shape)],
            out_specs=[
                pl.BlockSpec(memory_space=SMEM),
                whole((2 * coarse, LANES)),
                whole(halo),
                whole(halo),
            ],
            scratch_shapes=[
                SMEM((2, LANES), jnp.int32),
                SMEM((2, LANES), jnp.int32),
                SMEM((coarse + 2,), jnp.int32),
                SMEM((4,), jnp.int32),
                pltpu.SemaphoreType.DMA((4 + 2 * halo[0],)),
            ],
        ),
        out_shape=[
            jax.ShapeDtypeStruct((PLAN,), jnp.int32),
            jax.ShapeDtypeStruct((2 * coarse, LANES), F32),
            jax.ShapeDtypeStruct(halo, F32),
            jax.ShapeDtypeStruct(halo, F32),
        ],
        compiler_params=pltpu.CompilerParams(vmem_limit_bytes=60 << 20),
        cost_estimate=pl.CostEstimate(flops=0, bytes_accessed=5_000_000, transcendentals=0),
        name="plan",
    )(place, a_cols.T, a_len, a_tiles, p_tiles, aggregate.reshape(-1, LANES), owners, owners)


ORDER = "yzx"
SEND, STAY, SWAP = 8, 10, 11
SHIFT = {"x": 5, "z": 3, "y": 1}
COUNT = LANES - 1
TABLE = pl.ds(8, 32)


def corner_kernel(plan, a_tiles, p_tiles, left, right, out, a_buf, p_buf, result, sems, out_sem):
    fine, count = a_tiles.shape[0], out.shape[0]

    def loads(k):
        side = k & 1
        i = 3 * (k >> 1) + 2 * side
        j = i - 1 + 2 * side
        slot = jnp.where(side == 0, plan[LEFT + i], 3 - plan[LEFT + i])
        inside = (j >= 0) & (j < fine)
        near = jnp.where(inside, j, i)
        return side, inside, (
            pltpu.make_async_copy(a_tiles.at[i, slot], a_buf.at[k], sems.at[k, 0]),
            pltpu.make_async_copy(p_tiles.at[i, 1 - side], p_buf.at[k, 0], sems.at[k, 1]),
            pltpu.make_async_copy(p_tiles.at[near, side], p_buf.at[k, 1], sems.at[k, 2]),
        )

    def active(k):
        return (plan[CODE + k] & 7) > 0

    def back(k):
        return pltpu.make_async_copy(result.at[k], out.at[k], out_sem.at[k])

    def start(k, carry):
        @pl.when(active(k))
        def _():
            for copy in loads(k)[2]:
                copy.start()

        return carry

    def work(k, carry):
        @pl.when(active(k))
        def _():
            side, inside, copies = loads(k)
            for copy in copies:
                copy.wait()
            outside = jnp.where(side == 0, left[...], right[...])
            column = jnp.where(inside, p_buf[k, 1], outside)
            product = matmul(left_operand(a_buf[k]), right_operand(column))
            result[k] = matmul(left_operand(p_buf[k, 0].T), right_operand(product))
            back(k).start()

        return carry

    def finish(k, carry):
        @pl.when(active(k))
        def _():
            back(k).wait()

        return carry

    for step in (start, work, finish):
        lax.fori_loop(0, count, step, 0)


def corner_tiles(plan, a_tiles, p_tiles, left, right):
    count = 2 * (a_tiles.shape[0] // 3)
    tile = pl.BlockSpec((B, B), lambda *_: (0, 0))
    return pl.pallas_call(
        corner_kernel,
        grid_spec=pltpu.PrefetchScalarGridSpec(
            num_scalar_prefetch=1,
            grid=(1,),
            in_specs=[ANYWHERE, ANYWHERE, tile, tile],
            out_specs=ANYWHERE,
            scratch_shapes=[
                VMEM((count, B, B), F32),
                VMEM((count, 2, B, B), F32),
                VMEM((count, B, B), F32),
                pltpu.SemaphoreType.DMA((count, 3)),
                pltpu.SemaphoreType.DMA((count,)),
            ],
        ),
        out_shape=jax.ShapeDtypeStruct((count, B, B), F32),
        compiler_params=pltpu.CompilerParams(vmem_limit_bytes=60 << 20),
        cost_estimate=pl.CostEstimate(flops=100_000_000, bytes_accessed=4_000_000, transcendentals=0),
        name="corner_tiles",
    )(plan, a_tiles, p_tiles, left, right)


def fields(code):
    return code >> 10, (code >> 6) & 15, (code >> 3) & 7, code & 7


def read_headers(refs, heads, table_in, sem):
    copies = [pltpu.make_async_copy(x.at[0, pl.ds(0, 1)], heads.at[pl.ds(k, 1)], sem.at[k]) for k, x in enumerate(refs)]
    copies += [
        pltpu.make_async_copy(x.at[0, TABLE], table_in.at[k], sem.at[len(refs) + k]) for k, x in enumerate(refs)
    ]
    for copy in copies:
        copy.start()
    for copy in copies:
        copy.wait()
    table = table_in[0]
    for k in range(1, len(refs)):
        table = jnp.maximum(table, table_in[k])
    return table


def walk(refs, heads, body):
    for k, ref in enumerate(refs):

        def step(n, carry):
            body(heads[k, n].astype(jnp.int32), ref.at[1 + n])
            return carry

        lax.fori_loop(0, heads[k, COUNT].astype(jnp.int32), step, 0)


def sort_out(outs, sizes, feed, pick, buf, state, heads, table_out, copy_sem, out_sem):
    kinds = len(outs)
    bases = [sum(sizes[:k]) for k in range(kinds)]
    for k in range(kinds + 1):
        state[k] = 0

    def body(code, tile):
        where, wanted = pick(code)
        base, size = jnp.int32(bases[0]), jnp.int32(sizes[0])
        for k in range(1, kinds):
            base, size = jnp.where(where == k, bases[k], base), jnp.where(where == k, sizes[k], size)
        slot = state[where]

        @pl.when(wanted & (slot < size))
        def _():
            state[where] = slot + 1
            state[kinds] = state[kinds] + 1
            heads[where, slot] = code.astype(F32)
            pltpu.make_async_copy(tile, buf.at[base + slot], copy_sem.at[0]).start()

    feed(body)

    def wait(_, carry):
        pltpu.make_async_copy(buf.at[0], buf.at[0], copy_sem.at[0]).wait()
        return carry

    lax.fori_loop(0, state[kinds], wait, 0)
    always, maybe, n = [], [], 0
    for k, out in enumerate(outs):
        heads[k, COUNT] = state[k].astype(F32)
        always.append(pltpu.make_async_copy(heads.at[pl.ds(k, 1)], out.at[0, pl.ds(0, 1)], out_sem.at[n]))
        always.append(pltpu.make_async_copy(table_out, out.at[0, TABLE], out_sem.at[n + 1]))
        n += 2
        for slot in range(sizes[k]):
            copy = pltpu.make_async_copy(buf.at[bases[k] + slot], out.at[1 + slot], out_sem.at[n])
            maybe.append((state[k] > slot, copy))
            n += 1
    for copy in always:
        copy.start()
    for used, copy in maybe:
        pl.when(used)(copy.start)
    for used, copy in maybe:
        pl.when(used)(copy.wait)
    for copy in always:
        copy.wait()


SIZES = (STAY, SEND, SEND, SEND)


def sort_scratch(sizes):
    return [
        VMEM((sum(sizes), B, B), F32),
        SMEM((8,), jnp.int32),
        SMEM((4, LANES), F32),
        SMEM((4, LANES), F32),
        VMEM((4, 32, LANES), F32),
        VMEM((32, LANES), F32),
        pltpu.SemaphoreType.DMA((1,)),
        pltpu.SemaphoreType.DMA((8,)),
        pltpu.SemaphoreType.DMA((sum(sizes) + 2 * len(sizes),)),
    ]


def route_kernel(stage, behind, through, plan, place, *refs):
    refs = list(refs)
    came = [refs.pop(0) for _ in range(2 if stage == 0 else 4)]
    del refs[: behind + through]
    outs = [refs.pop(0) for _ in range(4)]
    del refs[:through]
    buf, state, heads_in, heads, table_in, table_out, copy_sem, head_sem, out_sem = refs
    if stage == 0:
        load = pltpu.make_async_copy(came[1], table_out, head_sem.at[0])
        load.start()
        load.wait()

        def feed(body):
            def step(k, carry):
                body(plan[CODE + k], came[0].at[k])
                return carry

            lax.fori_loop(0, came[0].shape[0], step, 0)
    else:
        table_out[...] = read_headers(came, heads_in, table_in, head_sem)

        def feed(body):
            walk(came, heads_in, body)

    shift = SHIFT[ORDER[stage]]
    mine = (place[0] >> shift) & 3
    odd = (place[0] & 1) == 1

    def pick(code):
        by = (code >> (10 + shift)) - mine
        return jnp.where(odd, -by, by) & 3, (code & 7) > 0

    sort_out(outs, SIZES, feed, pick, buf, state, heads, table_out, copy_sem, out_sem)


def route(stage, plan, place, came, behind=(), through=()):
    outs = [jax.ShapeDtypeStruct((size + 1, B, B), F32) for size in SIZES]
    first = 2 + len(came) + len(behind)
    result = pl.pallas_call(
        functools.partial(route_kernel, stage, len(behind), len(through)),
        grid_spec=pltpu.PrefetchScalarGridSpec(
            num_scalar_prefetch=2,
            grid=(1,),
            in_specs=[ANYWHERE] * (len(came) + len(behind) + len(through)),
            out_specs=[ANYWHERE] * (4 + len(through)),
            scratch_shapes=sort_scratch(SIZES),
        ),
        out_shape=outs + [jax.ShapeDtypeStruct(x.shape, x.dtype) for x in through],
        input_output_aliases={first + k: 4 + k for k in range(len(through))},
        compiler_params=pltpu.CompilerParams(vmem_limit_bytes=24 << 20),
        cost_estimate=pl.CostEstimate(flops=0, bytes_accessed=2_000_000, transcendentals=0),
        name="route",
    )(plan, place, *came, *behind, *through)
    return result[:4], result[4:]


def swap_kernel(place, *refs):
    came, out, scratch = refs[:4], refs[4], refs[5:]
    buf, state, heads_in, heads, table_in, table_out, copy_sem, head_sem, out_sem = scratch
    table_out[...] = read_headers(came, heads_in, table_in, head_sem)

    def pick(code):
        return jnp.int32(0), ((code >> 10) & 1) != (place[0] & 1)

    def feed(body):
        walk(came, heads_in, body)

    sort_out([out], (SWAP,), feed, pick, buf, state, heads, table_out, copy_sem, out_sem)


def swap_out(place, came):
    return pl.pallas_call(
        swap_kernel,
        grid_spec=pltpu.PrefetchScalarGridSpec(
            num_scalar_prefetch=1,
            grid=(1,),
            in_specs=[ANYWHERE] * 4,
            out_specs=ANYWHERE,
            scratch_shapes=sort_scratch((SWAP,)),
        ),
        out_shape=jax.ShapeDtypeStruct((SWAP + 1, B, B), F32),
        compiler_params=pltpu.CompilerParams(vmem_limit_bytes=24 << 20),
        cost_estimate=pl.CostEstimate(flops=0, bytes_accessed=2_000_000, transcendentals=0),
        name="swap_out",
    )(place, *came)


def relay(pairs, sems_in, sems_out):
    inward = [pltpu.make_async_copy(x, y, sems_in.at[k]) for k, (x, y, z) in enumerate(pairs)]
    outward = [pltpu.make_async_copy(y, z, sems_out.at[k]) for k, (x, y, z) in enumerate(pairs)]
    for copy in inward:
        copy.start()
    for come, go in zip(inward, outward):
        come.wait()
        go.start()
    for copy in outward:
        copy.wait()


def move_kernel(source_ref, target_ref, rows_in, rows_out, stage, sems_in, sems_out):
    relay(
        [(rows_in.at[source_ref[k]], stage.at[k], rows_out.at[target_ref[k]]) for k in range(stage.shape[0])],
        sems_in,
        sems_out,
    )


def move_rows(source, target, rows, places):
    count = source.shape[0]
    return pl.pallas_call(
        move_kernel,
        grid_spec=pltpu.PrefetchScalarGridSpec(
            num_scalar_prefetch=2,
            grid=(1,),
            in_specs=[ANYWHERE],
            out_specs=ANYWHERE,
            scratch_shapes=[
                VMEM((count,) + rows.shape[1:], F32),
                pltpu.SemaphoreType.DMA((count,)),
                pltpu.SemaphoreType.DMA((count,)),
            ],
        ),
        out_shape=jax.ShapeDtypeStruct((places,) + rows.shape[1:], F32),
        compiler_params=pltpu.CompilerParams(vmem_limit_bytes=56 << 20),
        cost_estimate=pl.CostEstimate(flops=0, bytes_accessed=8_000_000, transcendentals=0),
        name="move_rows",
    )(source, target, rows)


def join_kernel(source_a, source_b, place, rows_a, rows_b, *refs):
    got, refs = refs[:5], refs[5:]
    out, stage, copied, heads, table_in, copy_sem, head_sem, sems_in, sems_out = refs
    coarse = out.shape[0]
    inward, outward = [], []
    for k in range(coarse):
        for h, (rows, source) in enumerate(((rows_a, source_a), (rows_b, source_b))):
            inward.append(
                pltpu.make_async_copy(
                    rows.at[source[k]], stage.at[k, MIDDLE, pl.ds(h * HALF, HALF)], sems_in.at[2 * k + h]
                )
            )
        outward.append(pltpu.make_async_copy(stage.at[k], out.at[k], sems_out.at[k]))
    for copy in inward:
        copy.start()

    def clear(k, carry):
        stage[k, 0] = jnp.zeros((B, B), F32)
        stage[k, CWIN - 1] = jnp.zeros((B, B), F32)
        return carry

    lax.fori_loop(0, coarse, clear, 0)
    read_headers(got, heads, table_in, head_sem)
    core = place[0] & 1
    sem = copy_sem.at[0]
    copied[0] = 0

    def assign(code, tile):
        owner, row, column, _ = fields(code)

        @pl.when((owner & 1) == core)
        def _():
            pltpu.make_async_copy(tile, stage.at[row, column], sem).start()
            copied[0] = copied[0] + 1

    walk(got, heads, assign)

    def wait(_, carry):
        pltpu.make_async_copy(stage.at[0, 0], stage.at[0, 0], sem).wait()
        return carry

    lax.fori_loop(0, copied[0], wait, 0)
    for k in range(coarse):
        inward[2 * k].wait()
        inward[2 * k + 1].wait()
        outward[k].start()
    for copy in outward:
        copy.wait()


def join_rows(source_a, source_b, place, rows_a, rows_b, got):
    coarse = source_a.shape[0]
    return pl.pallas_call(
        join_kernel,
        grid_spec=pltpu.PrefetchScalarGridSpec(
            num_scalar_prefetch=3,
            grid=(1,),
            in_specs=[ANYWHERE] * (2 + len(got)),
            out_specs=ANYWHERE,
            scratch_shapes=[
                VMEM((coarse, CWIN, B, B), F32),
                SMEM((1,), jnp.int32),
                SMEM((len(got), LANES), F32),
                VMEM((len(got), 32, LANES), F32),
                pltpu.SemaphoreType.DMA((1,)),
                pltpu.SemaphoreType.DMA((2 * len(got),)),
                pltpu.SemaphoreType.DMA((2 * coarse,)),
                pltpu.SemaphoreType.DMA((coarse,)),
            ],
        ),
        out_shape=jax.ShapeDtypeStruct((coarse, CWIN, B, B), F32),
        compiler_params=pltpu.CompilerParams(vmem_limit_bytes=56 << 20),
        cost_estimate=pl.CostEstimate(flops=0, bytes_accessed=16_000_000, transcendentals=0),
        name="join_rows",
    )(source_a, source_b, place, rows_a, rows_b, *got)


def fits_kernel(owner_ref, one_ref, two_ref, out_ref):
    total = owner_ref.shape[1]
    devices, units = LANES, 2 * total
    owner = jnp.concatenate([owner_ref[...]] * 2, axis=1)
    table = jnp.maximum(one_ref[0, TABLE], two_ref[0, TABLE])
    tiles = jnp.concatenate([table[r : r + 1] for r in range(units // LANES)], axis=1)
    unit = lax.broadcasted_iota(jnp.int32, (1, units), 1)
    source = ((unit + jnp.where(unit < total, -1, 1)) & (total - 1)) // (total // devices)
    index = lax.broadcasted_iota(jnp.int32, (devices, units), 0)
    kinds = lax.broadcasted_iota(jnp.int32, (8, units), 0)

    def tally(holder, kind):
        left = jnp.where(holder == index, 1.0, 0.0).astype(BF)
        right = jnp.where(kinds == kind, tiles, 0.0).astype(BF)
        return lax.dot_general(left, right, (((1,), (1,)), ((), ())), preferred_element_type=F32)

    excess = jnp.full((devices, 1), -1.0, F32)
    holder = source
    for axis in ORDER:
        shift = SHIFT[axis]
        by = ((owner >> shift) - (holder >> shift)) & 3
        counts = tally(holder, by)
        for k, size in enumerate(SIZES):
            excess = jnp.maximum(excess, counts[:, k : k + 1] - float(size))
        holder = holder + ((((owner >> shift) & 3) - ((holder >> shift) & 3)) << shift)
    counts = tally(holder, (owner ^ holder) & 1)
    excess = jnp.maximum(excess, counts[:, 1:2] - float(SWAP))
    out_ref[...] = jnp.broadcast_to(jnp.max(excess, axis=0, keepdims=True), out_ref.shape)


def ring_fits(owner, one, two):
    turned = owner.reshape(1, -1)
    head = pl.BlockSpec((1,) + one.shape[1:], lambda *_: (0, 0, 0))
    return pl.pallas_call(
        fits_kernel,
        grid=(1,),
        in_specs=[pl.BlockSpec(turned.shape, lambda *_: (0, 0)), head, head],
        out_specs=pl.BlockSpec((8, LANES), lambda *_: (0, 0)),
        out_shape=jax.ShapeDtypeStruct((8, LANES), F32),
        compiler_params=pltpu.CompilerParams(vmem_limit_bytes=32 << 20),
        cost_estimate=pl.CostEstimate(flops=100_000_000, bytes_accessed=100_000, transcendentals=0),
        name="ring_fits",
    )(turned, one, two)[0, 0] <= 0.0


AXES = ("gx", "gy")


def neighbours(axis, way):
    shift, size = SHIFT[axis], lax.axis_size(AXES)
    pairs = []
    for i in range(size):
        by = way if i % 2 == 0 else -way
        pairs.append((i, (i & ~(3 << shift)) | ((((i >> shift) + by) & 3) << shift)))
    return pairs


def step(stage, sent):
    stay, one, across, two = sent
    shift, size = SHIFT[ORDER[stage]], lax.axis_size(AXES)
    far = [(i, i ^ (2 << shift)) for i in range(size)]
    return [
        stay,
        lax.ppermute(one, AXES, neighbours(ORDER[stage], 1)),
        lax.ppermute(across, AXES, far),
        lax.ppermute(two, AXES, neighbours(ORDER[stage], -1)),
    ]


def shards(a_tiles, a_cols, a_len, p_tiles, aggregate, owner):
    count_x, count_y = lax.axis_size("gx"), lax.axis_size("gy")
    index_x, index_y = lax.axis_index("gx"), lax.axis_index("gy")
    size = count_x * count_y
    device = index_x * count_y + index_y
    coarse = a_tiles.shape[0] // 3
    depth = coarse // count_x
    place = jnp.reshape(device, (1,)).astype(jnp.int32)
    above = [(i, (i + 1) % size) for i in range(size)]
    below = [(j, i) for i, j in above]
    left = lax.ppermute(p_tiles[-1, 0], AXES, above)
    right = lax.ppermute(p_tiles[0, 1], AXES, below)
    plan, counts, up, down = make_plan(place, a_cols, a_len, aggregate, owner, a_tiles, p_tiles)
    before = lax.ppermute(up, AXES, above)
    behind = lax.ppermute(down, AXES, below)
    corners = corner_tiles(plan, a_tiles, p_tiles, left, right)
    sent, _ = route(0, plan, place, [corners, counts])
    came = step(0, sent)
    pieces = main_product(plan, a_tiles, p_tiles, count_y, sent[0])
    rows_a, rows_b, outer = edge_product(plan, before, behind, up, down, p_tiles, pieces)
    sent, (rows_b,) = route(1, plan, place, came, through=(rows_b,))
    came = step(1, sent)

    table = owner.reshape(count_x, count_y, coarse)
    order = jnp.arange(coarse)
    shift = table[0, 0] // count_y
    same = shift[None, :] == shift[:, None]
    rank = jnp.sum((same & (order[None, :] < order[:, None])).astype(jnp.int32), axis=1)
    slot = (shift * depth + rank).astype(jnp.int32)
    from_x = (index_x - shift) % count_x
    column = table[:, index_y] % count_y
    mid_a_target = jnp.sum(
        jnp.where(jnp.arange(count_x)[:, None] == from_x[None, :], column, 0), axis=0
    ).astype(jnp.int32)
    hit = (table[index_x] % count_y) == index_y
    mid_b_source = jnp.sum(jnp.where(hit, jnp.arange(count_y)[:, None], 0), axis=0).astype(jnp.int32)
    found = table.reshape(size, coarse) == device
    sender = jnp.sum(jnp.where(found, jnp.arange(size)[:, None], 0), axis=0)
    ids = sender * coarse + order
    spot = jnp.sum((ids[None, :] < ids[:, None]).astype(jnp.int32), axis=1)
    at = spot[None, :] == order[:, None]
    last_a = jnp.sum(jnp.where(at, (sender % count_y)[None, :], 0), axis=1).astype(jnp.int32)
    last_b = jnp.sum(jnp.where(at, slot[None, :], 0), axis=1).astype(jnp.int32)

    def over_y(x):
        return lax.all_to_all(x, "gy", split_axis=0, concat_axis=0, tiled=True)

    def along_x(x):
        parts = [x[:depth]]
        for k in range(1, count_x):
            pairs = [(i, (i + k) % count_x) for i in range(count_x)]
            parts.append(lax.ppermute(x[k * depth : (k + 1) * depth], "gx", pairs))
        return jnp.concatenate(parts, axis=0)

    got_b = over_y(rows_b)
    got_a = along_x(rows_a)
    sent, _ = route(2, plan, place, came, behind=(got_a,))
    came = step(2, sent)
    one = swap_out(place, came)
    two = lax.ppermute(one, AXES, [(i, i ^ 1) for i in range(size)])
    fits = ring_fits(owner, one, two)
    ring = came + [two]
    end_a = over_y(move_rows(slot, mid_a_target, got_a, count_y))
    end_b = along_x(move_rows(mid_b_source, slot, got_b, coarse))

    def slow(*_):
        mine = table[index_x, index_y]
        slots = ((mine // count_y - index_x) % count_x) * depth + rank
        middle = jnp.concatenate([rows_a[slots], rows_b[mine % count_y]], axis=2)
        sides = outer.reshape(coarse, 2, B, B)
        return by_slots(jnp.concatenate([sides[:, :1], middle, sides[:, 1:]], axis=1), owner, device)

    return lax.cond(
        fits, lambda x, y, z: join_rows(last_a, last_b, place, x, y, z), slow, end_a, end_b, ring
    )


def by_slots(complete, owner, device):
    count_x, count_y = lax.axis_size("gx"), lax.axis_size("gy")
    index_x, index_y = device // count_y, device % count_y
    coarse = complete.shape[0]
    depth = coarse // count_x
    table = owner.reshape(count_x, count_y, coarse)
    order = jnp.arange(coarse)
    shift = table[0, 0] // count_y
    same = shift[None, :] == shift[:, None]
    rank = jnp.sum((same & (order[None, :] < order[:, None])).astype(jnp.int32), axis=1)
    mine = table[index_x, index_y]
    slot = (mine // count_y) * depth + rank
    hits = slot[None, :] == order[:, None]
    packed = complete[jnp.sum(jnp.where(hits, order[None, :], 0), axis=1)]
    moved = lax.all_to_all(packed, "gx", split_axis=0, concat_axis=0, tiled=True)
    from_x = (index_x - shift) % count_x
    column = table[:, index_y] % count_y
    target = jnp.sum(jnp.where(jnp.arange(count_x)[:, None] == from_x[None, :], column, 0), axis=0)
    hits = target[None, :] == jnp.arange(count_y)[:, None]
    packed = moved[jnp.sum(jnp.where(hits, (from_x * depth + rank)[None, :], 0), axis=1)]
    moved = lax.all_to_all(packed, "gy", split_axis=0, concat_axis=0, tiled=True)
    found = table.reshape(-1, coarse) == device
    sender = jnp.sum(jnp.where(found, jnp.arange(count_x * count_y)[:, None], 0), axis=0)
    ids = sender * coarse + order
    spot = jnp.sum((ids[None, :] < ids[:, None]).astype(jnp.int32), axis=1)
    hits = spot[None, :] == order[:, None]
    return moved[jnp.sum(jnp.where(hits, (sender % count_y)[None, :], 0), axis=1)]


def solution(mesh):
    in_specs = (
        P(("gx", "gy"), None, None, None),
        P(("gx", "gy"), None),
        P(("gx", "gy")),
        P(("gx", "gy"), None, None, None),
        P(),
        P(),
    )
    out_specs = P(("gx", "gy"), None, None, None)
    return jax.shard_map(shards, mesh=mesh, in_specs=in_specs, out_specs=out_specs, check_vma=False)
```

time: 289 us -> 319 us (1.10)
  waiting for transfers between devices: 173 us -> 185 us
  local copies, waits for them, and re-layouts: 4.22 us -> 13.3 us
  Pallas kernels: 57.6 us -> 62.4 us
    ppermute x15 -> x14, waiting for transfers between devices: 88.4 us -> 103 us  [the longest x3 98.3 us: step(): lax.ppermute(one, AXES, neighbours(ORDER[stage], 1))]
    unnamed x32 -> x48, local copies, waits for them, and re-layouts: 1.3 us -> 9.57 us
    pallas_call x3 -> x4, Pallas kernels: 10 us -> 14.3 us  [the longest x3 8.24 us: route(): pl.pallas_call(functools.partial(route_kernel, stage, len(behind), len(th...]
    ppermute x15 -> x14, starting transfers between devices: 28.5 us -> 29.4 us  [the longest x1 8.27 us: shards(): right = lax.ppermute(p_tiles[0, 1], AXES, below)]
  transfers between devices with their start and end apart: 23 -> 22, of which waited for: 11 -> 9; matrix products, arithmetic and copies ran while one was open for 3% -> 3% of each run, Pallas kernels for 13% -> 17%
where the time goes in v2:
time: 319 us; the launch traced here: 315 us
  waiting for transfers between devices  185 us (58%)
  Pallas kernels  62.4 us (20%)
  starting transfers between devices  47.2 us (15%)
  local copies, waits for them, and re-layouts  13.3 us (4%)
  other arithmetic  6.63 us (2%)
    ppermute x3, waiting for transfers between devices, step(): lax.ppermute(one, AXES, neighbours(ORDER[stage], 1))  98.3 us
    ppermute x6, waiting for transfers between devices, along_x(): parts.append(lax.ppermute(x[k * depth:(k + 1) * depth], 'gx', pairs))  54.7 us
    all_to_all x2, waiting for transfers between devices, over_y(): return lax.all_to_all(x, 'gy', split_axis=0, concat_axis=0, tiled=True)  27.3 us
    pallas_call x1, Pallas kernels, main_product(): pl.pallas_call(main_kernel, grid_spec=pltpu.PrefetchScalarGridSpec(num_sc...  18.6 us
    all_to_all x2, starting transfers between devices, over_y(): return lax.all_to_all(x, 'gy', split_axis=0, concat_axis=0, tiled=True)  10.5 us
    unnamed x48, local copies, waits for them, and re-layouts  9.57 us
    ppermute x1, starting transfers between devices, shards(): right = lax.ppermute(p_tiles[0, 1], AXES, below)  8.27 us
    pallas_call x3, Pallas kernels, route(): pl.pallas_call(functools.partial(route_kernel, stage, len(behind), len(th...  8.24 us
  transfers between devices with their start and end apart: 22, of which 9 were waited for; matrix products, arithmetic and copies ran while one was open for 3% of the time, Pallas kernels for 17%

profile of v2, /device:TPU:0, one launch (start us, length us, event | category | flops | bytes accessed | tf_op | source)
XLA Modules:
  0.0 315.3 jit_solution(8698058547907567749)
XLA Ops:
  1.0 8.3 %collective-permute-start.1 = (f32[128,128]{1,0:T(8,128)S(1)}, f32[128,128]{1,0:T(8,128)S(1)}, u32[]{:S(2)}, u32[]{:S(2)}) collective-permute-start(f32[128,128]{1,0:T(8,128)S(1)} %get-tuple-element.225), channel_id=1, source_target_pairs={{1,0},{2,1},{3,2},{4,3},{5,4},{6,5},{7,6},{8,7},{9,8},{10,9},{11,1... | collective-permute-start | bytes 196616 | tf_op jit(solution)/shard_map/ppermute | solution.py:961
  9.2 5.7 %plan.1 = (s32[384]{0:T(512)}, f32[32,128]{1,0:T(8,128)}, f32[17,128,128]{2,1,0:T(8,128)}, f32[17,128,128]{2,1,0:T(8,128)}) custom-call(s32[1]{0:T(128)} %bitcast.18.place, s32[3,48]{1,0:T(4,128)} %bitcast.88, s32[48]{0:T(128)} %length.1, f32[48,3,128,128]{3,2,1,0:T(8,128)} %a_ref.1, f32[48,2,128,128]{3,2,1,0:T(8,128)} %p_last.1, s32[48,128]{1,0:T(8,128)} %bitcast.85, ...), custom_call_target="tpu_custom_call" | custom-call | bytes 5000000 | tf_op jit(solution)/shard_map/plan/pallas_call | solution.py:463
  15.0 7.2 %collective-permute-start.6 = (f32[17,128,128]{2,1,0:T(8,128)}, f32[17,128,128]{2,1,0:T(8,128)}, u32[]{:S(2)}, u32[]{:S(2)}) collective-permute-start(f32[17,128,128]{2,1,0:T(8,128)} %get-tuple-element.186.a_first), channel_id=1, source_target_pairs={{1,0},{2,1},{3,2},{4,3},{5,4},{6,5},{7,6},{8,7},{9,8},{10,9},{11,1... | collective-permute-start | bytes 3342344 | tf_op jit(solution)/shard_map/ppermute | solution.py:964
  22.8 6.0 %corner_tiles.1.refs_0_ = f32[32,128,128]{2,1,0:T(8,128)} custom-call(s32[384]{0:T(512)} %get-tuple-element.179.plan, f32[48,3,128,128]{3,2,1,0:T(8,128)} %a_ref.1, f32[48,2,128,128]{3,2,1,0:T(8,128)} %p_last.1, f32[128,128]{1,0:T(8,128)} %copy-done.21, f32[128,128]{1,0:T(8,128)} %copy-done.22), custom_call_target="tpu_custom_call" | custom-call | flops 100000000 | bytes 4000000 | tf_op jit(solution)/shard_map/corner_tiles/pallas_call | solution.py:560
  30.5 3.0 route.3
  34.3 3.2 %collective-permute-start.4 = (f32[9,128,128]{2,1,0:T(8,128)}, f32[9,128,128]{2,1,0:T(8,128)}, u32[]{:S(2)}, u32[]{:S(2)}) collective-permute-start(f32[9,128,128]{2,1,0:T(8,128)} %get-tuple-element.184), channel_id=1, source_target_pairs={{0,6},{1,3},{2,0},{3,5},{4,2},{5,7},{6,4},{7,1},{8,14},{9,11},{10,... | collective-permute-start | bytes 1769480 | tf_op jit(solution)/shard_map/ppermute | solution.py:946
  37.6 18.6 %triple_product.1 = (f32[16,5,64,128]{3,2,1,0:T(8,128)}, f32[32,5,64,128]{3,2,1,0:T(8,128)}, f32[32,128,128]{2,1,0:T(8,128)}) custom-call(s32[384]{0:T(512)} %get-tuple-element.179.plan, f32[48,3,128,128]{3,2,1,0:T(8,128)} %a_ref.1, f32[48,2,128,128]{3,2,1,0:T(8,128)} %p_last.1, f32[48,2,128,128]{3,2,1,0:T(8,128)} %p_last.1, f32[48,2,128,128]{3,2,1,0:T(8,128)} %p_last.1, ...), custom_call_target="tpu_custom_call" | custom-call | flops 16000000000 | bytes 24000000 | tf_op jit(solution)/shard_map/triple_product/pallas_call | solution.py:181
  57.5 6.1 %edge_rows.1 = (f32[16,5,64,128]{3,2,1,0:T(8,128)}, f32[32,5,64,128]{3,2,1,0:T(8,128)}, f32[32,128,128]{2,1,0:T(8,128)}) custom-call(s32[384]{0:T(512)S(1)} %copy-done.9, f32[17,128,128]{2,1,0:T(8,128)} %collective-permute-done.5.before, f32[17,128,128]{2,1,0:T(8,128)} %collective-permute-done.6.after, ...), custom_call_target="tpu_custom_call", output_to_operand_aliasing={{0}: (7, {}), {1}: (8, {}), {2}: (9, {})} | custom-call | flops 2000000000 | bytes 10000000 | tf_op jit(solution)/shard_map/edge_rows/pallas_call | solution.py:308
  65.5 2.8 route.4
  70.8 5.6 %all-to-all-start.3 = ((f32[32,5,64,128]{3,2,1,0:T(8,128)}), f32[32,5,64,128]{3,2,1,0:T(8,128)}, u32[]{:S(2)}, u32[]{:S(2)}) async-start(f32[32,5,64,128]{3,2,1,0:T(8,128)} %get-tuple-element.201), calls=%async_computation.3 | async-start | bytes 10485760 | tf_op jit(solution)/shard_map/all_to_all | solution.py:995
  76.9 2.1 collective-permute-start.11
  78.9 1.9 collective-permute-start.12
  82.2 26.8 %collective-permute-done.10 = f32[4,5,64,128]{3,2,1,0:T(8,128)S(1)} collective-permute-done((f32[4,5,64,128]{3,2,1,0:T(8,128)S(1)}, f32[4,5,64,128]{3,2,1,0:T(8,128)S(1)}, u32[]{:S(2)}, u32[]{:S(2)}) %collective-permute-start.10) | collective-permute-done | bytes 655392 | tf_op jit(solution)/shard_map/ppermute | solution.py:1001
  109.6 1.9 pad_maximum_fusion.1.refs_4_.rows_in
  111.5 3.5 %move_rows.2 = f32[32,5,64,128]{3,2,1,0:T(8,128)} custom-call(s32[16]{0:T(128)} %multiply_add_fusion.2.source_ref.target_ref, s32[16]{0:T(128)} %fusion.22.target_ref, f32[16,5,64,128]{3,2,1,0:T(8,128)} %pad_maximum_fusion.1.refs_4_.rows_in), custom_call_target="tpu_custom_call" | custom-call | bytes 8000000 | tf_op jit(solution)/shard_map/move_rows/pallas_call | solution.py:784
  115.0 27.3 %all-to-all-done.3.rows_in = f32[32,5,64,128]{3,2,1,0:T(8,128)} async-done(((f32[32,5,64,128]{3,2,1,0:T(8,128)}), f32[32,5,64,128]{3,2,1,0:T(8,128)}, u32[]{:S(2)}, u32[]{:S(2)}) %all-to-all-start.3) | async-done | bytes 5242912 | tf_op jit(solution)/shard_map/all_to_all | solution.py:995
  142.2 4.9 %all-to-all-start.2 = ((f32[32,5,64,128]{3,2,1,0:T(8,128)}), f32[32,5,64,128]{3,2,1,0:T(8,128)}, u32[]{:S(2)}, u32[]{:S(2)}) async-start(f32[32,5,64,128]{3,2,1,0:T(8,128)} %move_rows.2), calls=%async_computation.2 | async-start | bytes 10485760 | tf_op jit(solution)/shard_map/all_to_all | solution.py:995
  148.8 2.8 collective-permute-start.8
  153.0 78.3 %collective-permute-done.7.refs_1_ = f32[9,128,128]{2,1,0:T(8,128)S(1)} collective-permute-done((f32[9,128,128]{2,1,0:T(8,128)}, f32[9,128,128]{2,1,0:T(8,128)S(1)}, u32[]{:S(2)}, u32[]{:S(2)}) %collective-permute-start.7) | collective-permute-done | bytes 589856 | tf_op jit(solution)/shard_map/ppermute | solution.py:944
  231.4 2.0 collective-permute-done.8.refs_2_
  233.3 2.4 route.5
  235.9 2.8 collective-permute-start.14
  241.1 20.0 %collective-permute-done.13.refs_1_ = f32[9,128,128]{2,1,0:T(8,128)S(1)} collective-permute-done((f32[9,128,128]{2,1,0:T(8,128)}, f32[9,128,128]{2,1,0:T(8,128)S(1)}, u32[]{:S(2)}, u32[]{:S(2)}) %collective-permute-start.13) | collective-permute-done | bytes 589856 | tf_op jit(solution)/shard_map/ppermute | solution.py:944
  261.1 2.4 collective-permute-done.14.refs_2_
  263.5 1.9 swap_out.1.one_ref
  265.4 3.5 %move_rows.3 = f32[16,5,64,128]{3,2,1,0:T(8,128)} custom-call(s32[16]{0:T(128)} %select_reduce_fusion.7.source_ref, s32[16]{0:T(128)} %multiply_add_fusion.2.source_ref.target_ref, f32[32,5,64,128]{3,2,1,0:T(8,128)} %all-to-all-done.3.rows_in), custom_call_target="tpu_custom_call" | custom-call | bytes 8000000 | tf_op jit(solution)/shard_map/move_rows/pallas_call | solution.py:784
  269.0 2.0 fusion.25
  271.0 2.0 collective-permute-start.18
  276.8 26.6 %collective-permute-done.17 = f32[4,5,64,128]{3,2,1,0:T(8,128)S(1)} collective-permute-done((f32[4,5,64,128]{3,2,1,0:T(8,128)S(1)}, f32[4,5,64,128]{3,2,1,0:T(8,128)S(1)}, u32[]{:S(2)}, u32[]{:S(2)}) %collective-permute-start.17) | collective-permute-done | bytes 655392 | tf_op jit(solution)/shard_map/ppermute | solution.py:1001
  304.0 1.8 pad_maximum_fusion.2
  306.7 8.4 %conditional.1 = (f32[16,7,128,128]{3,2,1,0:T(8,128)}) conditional(s32[]{:T(128)} %bitcast.24, (f32[32,128,128]{2,1,0:T(8,128)}, s32[]{:T(128)}, s32[]{:T(128)}, s32[4,32,16]{2,1,0:T(8,128)S(1)}, s32[16]{0:T(128)S(1)}, /*index=5*/f32[16,5,64,128]{3,2,1,0:T(8,128)S(1)}, f32[32,5,64,128]{3,2,1,0:T(8,128)}, s32[2048]{0:T(1024)S(1)}, ...), branch_computations={%region_4.12_spmd, %region_12.16_spmd} | conditional | flops 5524079 | bytes 164684224 | solution.py:1022
  307.5 7.5 %join_rows.1 = f32[16,7,128,128]{3,2,1,0:T(8,128)} custom-call(s32[16]{0:T(128)} %get-tuple-element.211.source_a, s32[16]{0:T(128)} %get-tuple-element.210.source_b, s32[1]{0:T(128)} %get-tuple-element.148.place, f32[32,5,64,128]{3,2,1,0:T(8,128)} %get-tuple-element.149.rows_a, f32[16,5,64,128]{3,2,1,0:T(8,128)} %get-tuple-element.150.rows_b, ...), custom_call_target="tpu_custom_call" | custom-call | bytes 16000000 | tf_op jit(solution)/shard_map/cond/branch_1_fun/join_rows/pallas_call | solution.py:856
  (98 shorter events, 23.4 us)
Async XLA Ops:
  0.9 21.3 %collective-permute-start = (f32[128,128]{1,0:T(8,128)S(1)}, f32[128,128]{1,0:T(8,128)S(1)}, u32[]{:S(2)}, u32[]{:S(2)}) collective-permute-start(f32[128,128]{1,0:T(8,128)S(1)} %get-tuple-element.226), channel_id=1, source_target_pairs={{0,1},{1,2},{2,3},{3,4},{4,5},{5,6},{6,7},{7,8},{8,9},{9,10},{10,1... | collective-permute-start | bytes 196616 | tf_op jit(solution)/shard_map/ppermute | solution.py:960
  1.0 21.2 %collective-permute-start.1 = (f32[128,128]{1,0:T(8,128)S(1)}, f32[128,128]{1,0:T(8,128)S(1)}, u32[]{:S(2)}, u32[]{:S(2)}) collective-permute-start(f32[128,128]{1,0:T(8,128)S(1)} %get-tuple-element.225), channel_id=1, source_target_pairs={{1,0},{2,1},{3,2},{4,3},{5,4},{6,5},{7,6},{8,7},{9,8},{10,9},{11,1... | collective-permute-start | bytes 196616 | tf_op jit(solution)/shard_map/ppermute | solution.py:961
  14.9 41.3 %collective-permute-start.5 = (f32[17,128,128]{2,1,0:T(8,128)}, f32[17,128,128]{2,1,0:T(8,128)}, u32[]{:S(2)}, u32[]{:S(2)}) collective-permute-start(f32[17,128,128]{2,1,0:T(8,128)} %get-tuple-element.185.a_last), channel_id=1, source_target_pairs={{0,1},{1,2},{2,3},{3,4},{4,5},{5,6},{6,7},{7,8},{8,9},{9,10},{10,1... | collective-permute-start | bytes 3342344 | tf_op jit(solution)/shard_map/ppermute | solution.py:963
  15.0 41.2 %collective-permute-start.6 = (f32[17,128,128]{2,1,0:T(8,128)}, f32[17,128,128]{2,1,0:T(8,128)}, u32[]{:S(2)}, u32[]{:S(2)}) collective-permute-start(f32[17,128,128]{2,1,0:T(8,128)} %get-tuple-element.186.a_first), channel_id=1, source_target_pairs={{1,0},{2,1},{3,2},{4,3},{5,4},{6,5},{7,6},{8,7},{9,8},{10,9},{11,1... | collective-permute-start | bytes 3342344 | tf_op jit(solution)/shard_map/ppermute | solution.py:964
  22.8 6.0 %copy-start.8 = (s32[384]{0:T(512)S(1)}, s32[384]{0:T(512)}, u32[]{:S(2)}) copy-start(s32[384]{0:T(512)} %get-tuple-element.179.plan) | copy-start | bytes 4612
  22.8 6.1 %copy-start.10 = (f32[32,128]{1,0:T(8,128)S(1)}, f32[32,128]{1,0:T(8,128)}, u32[]{:S(2)}) copy-start(f32[32,128]{1,0:T(8,128)} %get-tuple-element.180.refs_1_) | copy-start | bytes 49156
  34.3 29.3 %collective-permute-start.2 = (f32[9,128,128]{2,1,0:T(8,128)}, f32[9,128,128]{2,1,0:T(8,128)S(1)}, u32[]{:S(2)}, u32[]{:S(2)}) collective-permute-start(f32[9,128,128]{2,1,0:T(8,128)} %get-tuple-element.182), channel_id=1, source_target_pairs={{0,2},{1,7},{2,4},{3,1},{4,6},{5,3},{6,0},{7,5},{8,10},{9,15},{10,... | collective-permute-start | bytes 1769480 | tf_op jit(solution)/shard_map/ppermute | solution.py:944
  34.3 30.1 %collective-permute-start.3 = (f32[9,128,128]{2,1,0:T(8,128)}, f32[9,128,128]{2,1,0:T(8,128)}, u32[]{:S(2)}, u32[]{:S(2)}) collective-permute-start(f32[9,128,128]{2,1,0:T(8,128)} %get-tuple-element.183), channel_id=1, source_target_pairs={{0,4},{1,5},{2,6},{3,7},{4,0},{5,1},{6,2},{7,3},{8,12},{9,13},{10,... | collective-permute-start | bytes 1769480 | tf_op jit(solution)/shard_map/ppermute | solution.py:945
  34.3 30.1 %collective-permute-start.4 = (f32[9,128,128]{2,1,0:T(8,128)}, f32[9,128,128]{2,1,0:T(8,128)}, u32[]{:S(2)}, u32[]{:S(2)}) collective-permute-start(f32[9,128,128]{2,1,0:T(8,128)} %get-tuple-element.184), channel_id=1, source_target_pairs={{0,6},{1,3},{2,0},{3,5},{4,2},{5,7},{6,4},{7,1},{8,14},{9,11},{10,... | collective-permute-start | bytes 1769480 | tf_op jit(solution)/shard_map/ppermute | solution.py:946
  37.6 18.6 %slice-start = ((s8[6291456]{0:T(1024)(128)(4,1)}), s8[4194304]{0:T(1024)(128)(4,1)S(1)}, s32[]{:S(2)}) async-start(s8[6291456]{0:T(1024)(128)(4,1)} %bitcast.79), calls=%async_computation.4 | async-start | bytes 8388608
  37.6 18.6 %slice-start.1 = ((s8[6291456]{0:T(1024)(128)(4,1)}), s8[2097152]{0:T(1024)(128)(4,1)S(1)}, s32[]{:S(2)}) async-start(s8[6291456]{0:T(1024)(128)(4,1)} %bitcast.79), calls=%async_computation.5 | async-start | bytes 4194304
  37.6 18.6 %copy-start.2 = (f32[17,128,128]{2,1,0:T(8,128)S(1)}, f32[17,128,128]{2,1,0:T(8,128)}, u32[]{:S(2)}) copy-start(f32[17,128,128]{2,1,0:T(8,128)} %get-tuple-element.185.a_last) | copy-start | bytes 3342340
  37.6 18.7 %copy-start.9 = (s32[384]{0:T(512)S(1)}, s32[384]{0:T(512)}, u32[]{:S(2)}) copy-start(s32[384]{0:T(512)} %get-tuple-element.179.plan) | copy-start | bytes 4612
  57.5 7.0 %copy-start.5 = (f32[11,128,128]{2,1,0:T(8,128)S(1)}, f32[11,128,128]{2,1,0:T(8,128)}, u32[]{:S(2)}) copy-start(f32[11,128,128]{2,1,0:T(8,128)} %copy-done.4) | copy-start | bytes 2162692
  70.8 5.8 %copy-start.14 = (f32[16,5,64,128]{3,2,1,0:T(8,128)S(1)}, f32[16,5,64,128]{3,2,1,0:T(8,128)}, u32[]{:S(2)}) copy-start(f32[16,5,64,128]{3,2,1,0:T(8,128)} %get-tuple-element.195) | copy-start | bytes 7864324
  70.8 71.4 %all-to-all-start.3 = ((f32[32,5,64,128]{3,2,1,0:T(8,128)}), f32[32,5,64,128]{3,2,1,0:T(8,128)}, u32[]{:S(2)}, u32[]{:S(2)}) async-start(f32[32,5,64,128]{3,2,1,0:T(8,128)} %get-tuple-element.201), calls=%async_computation.3 | async-start | bytes 10485760 | tf_op jit(solution)/shard_map/all_to_all | solution.py:995
  76.8 32.2 %collective-permute-start.10 = (f32[4,5,64,128]{3,2,1,0:T(8,128)S(1)}, f32[4,5,64,128]{3,2,1,0:T(8,128)S(1)}, u32[]{:S(2)}, u32[]{:S(2)}) collective-permute-start(f32[4,5,64,128]{3,2,1,0:T(8,128)S(1)} %get-tuple-element.234), channel_id=1, source_target_pairs={{0,32},{32,64},{64,96},{96,0},{1,33},{33,65},{65,97},{97,1},{2,34}... | collective-permute-start | bytes 1966088 | tf_op jit(solution)/shard_map/ppermute | solution.py:1001
  76.9 32.1 %collective-permute-start.11 = (f32[4,5,64,128]{3,2,1,0:T(8,128)S(1)}, f32[4,5,64,128]{3,2,1,0:T(8,128)S(1)}, u32[]{:S(2)}, u32[]{:S(2)}) collective-permute-start(f32[4,5,64,128]{3,2,1,0:T(8,128)S(1)} %get-tuple-element.233), channel_id=1, source_target_pairs={{0,64},{32,96},{64,0},{96,32},{1,65},{33,97},{65,1},{97,33},{2,66}... | collective-permute-start | bytes 1966088 | tf_op jit(solution)/shard_map/ppermute | solution.py:1001
  78.9 30.7 %collective-permute-start.12 = (f32[4,5,64,128]{3,2,1,0:T(8,128)S(1)}, f32[4,5,64,128]{3,2,1,0:T(8,128)S(1)}, u32[]{:S(2)}, u32[]{:S(2)}) collective-permute-start(f32[4,5,64,128]{3,2,1,0:T(8,128)S(1)} %get-tuple-element.232), channel_id=1, source_target_pairs={{0,96},{32,0},{64,32},{96,64},{1,97},{33,1},{65,33},{97,65},{2,98}... | collective-permute-start | bytes 1966088 | tf_op jit(solution)/shard_map/ppermute | solution.py:1001
  115.0 118.4 %copy-start = (f32[16,5,64,128]{3,2,1,0:T(8,128)S(1)}, f32[16,5,64,128]{3,2,1,0:T(8,128)}, u32[]{:S(2)}) copy-start(f32[16,5,64,128]{3,2,1,0:T(8,128)} %pad_maximum_fusion.1.refs_4_.rows_in) | copy-start | bytes 7864324
  142.2 163.6 %all-to-all-start.2 = ((f32[32,5,64,128]{3,2,1,0:T(8,128)}), f32[32,5,64,128]{3,2,1,0:T(8,128)}, u32[]{:S(2)}, u32[]{:S(2)}) async-start(f32[32,5,64,128]{3,2,1,0:T(8,128)} %move_rows.2), calls=%async_computation.2 | async-start | bytes 10485760 | tf_op jit(solution)/shard_map/all_to_all | solution.py:995
  147.1 84.3 %collective-permute-start.7 = (f32[9,128,128]{2,1,0:T(8,128)}, f32[9,128,128]{2,1,0:T(8,128)S(1)}, u32[]{:S(2)}, u32[]{:S(2)}) collective-permute-start(f32[9,128,128]{2,1,0:T(8,128)} %copy-done.13), channel_id=1, source_target_pairs={{0,8},{1,25},{2,10},{3,27},{4,12},{5,29},{6,14},{7,31},{8,16},{9,1... | collective-permute-start | bytes 1769480 | tf_op jit(solution)/shard_map/ppermute | solution.py:944
  148.8 84.5 %collective-permute-start.8 = (f32[9,128,128]{2,1,0:T(8,128)}, f32[9,128,128]{2,1,0:T(8,128)S(1)}, u32[]{:S(2)}, u32[]{:S(2)}) collective-permute-start(f32[9,128,128]{2,1,0:T(8,128)} %copy-done.12), channel_id=1, source_target_pairs={{0,16},{1,17},{2,18},{3,19},{4,20},{5,21},{6,22},{7,23},{8,24},{9,... | collective-permute-start | bytes 1769480 | tf_op jit(solution)/shard_map/ppermute | solution.py:945
  151.6 81.7 %collective-permute-start.9 = (f32[9,128,128]{2,1,0:T(8,128)}, f32[9,128,128]{2,1,0:T(8,128)S(1)}, u32[]{:S(2)}, u32[]{:S(2)}) collective-permute-start(f32[9,128,128]{2,1,0:T(8,128)} %copy-done.11), channel_id=1, source_target_pairs={{0,24},{1,9},{2,26},{3,11},{4,28},{5,13},{6,30},{7,15},{8,0},{9,17... | collective-permute-start | bytes 1769480 | tf_op jit(solution)/shard_map/ppermute | solution.py:946
  235.8 25.3 %collective-permute-start.13 = (f32[9,128,128]{2,1,0:T(8,128)}, f32[9,128,128]{2,1,0:T(8,128)S(1)}, u32[]{:S(2)}, u32[]{:S(2)}) collective-permute-start(f32[9,128,128]{2,1,0:T(8,128)} %get-tuple-element.197), channel_id=1, source_target_pairs={{0,32},{1,97},{2,34},{3,99},{4,36},{5,101},{6,38},{7,103},{8,40},{... | collective-permute-start | bytes 1769480 | tf_op jit(solution)/shard_map/ppermute | solution.py:944
  235.9 27.6 %collective-permute-start.14 = (f32[9,128,128]{2,1,0:T(8,128)}, f32[9,128,128]{2,1,0:T(8,128)S(1)}, u32[]{:S(2)}, u32[]{:S(2)}) collective-permute-start(f32[9,128,128]{2,1,0:T(8,128)} %get-tuple-element.198), channel_id=1, source_target_pairs={{0,64},{1,65},{2,66},{3,67},{4,68},{5,69},{6,70},{7,71},{8,72},{9,... | collective-permute-start | bytes 1769480 | tf_op jit(solution)/shard_map/ppermute | solution.py:945
  238.6 24.8 %collective-permute-start.15 = (f32[9,128,128]{2,1,0:T(8,128)}, f32[9,128,128]{2,1,0:T(8,128)S(1)}, u32[]{:S(2)}, u32[]{:S(2)}) collective-permute-start(f32[9,128,128]{2,1,0:T(8,128)} %get-tuple-element.199), channel_id=1, source_target_pairs={{0,96},{1,33},{2,98},{3,35},{4,100},{5,37},{6,102},{7,39},{8,104},... | collective-permute-start | bytes 1769480 | tf_op jit(solution)/shard_map/ppermute | solution.py:946
  261.1 7.9 %copy-start.17 = (f32[9,128,128]{2,1,0:T(8,128)}, f32[9,128,128]{2,1,0:T(8,128)S(1)}, u32[]{:S(2)}) copy-start(f32[9,128,128]{2,1,0:T(8,128)S(1)} %collective-permute-done.13.refs_1_) | copy-start | bytes 1769476
  265.3 9.0 %collective-permute-start.16 = (f32[12,128,128]{2,1,0:T(8,128)S(1)}, f32[12,128,128]{2,1,0:T(8,128)S(1)}, u32[]{:S(2)}, u32[]{:S(2)}) collective-permute-start(f32[12,128,128]{2,1,0:T(8,128)S(1)} %swap_out.1.one_ref), channel_id=1, source_target_pairs={{0,1},{1,0},{2,3},{3,2},{4,5},{5,4},{6,7},{7,6},{8,9},{9,8},{10,11... | collective-permute-start | bytes 2359304 | tf_op jit(solution)/shard_map/ppermute | solution.py:1009
  270.9 32.5 %collective-permute-start.17 = (f32[4,5,64,128]{3,2,1,0:T(8,128)S(1)}, f32[4,5,64,128]{3,2,1,0:T(8,128)S(1)}, u32[]{:S(2)}, u32[]{:S(2)}) collective-permute-start(f32[4,5,64,128]{3,2,1,0:T(8,128)S(1)} %get-tuple-element.230), channel_id=1, source_target_pairs={{0,32},{32,64},{64,96},{96,0},{1,33},{33,65},{65,97},{97,1},{2,34}... | collective-permute-start | bytes 1966088 | tf_op jit(solution)/shard_map/ppermute | solution.py:1001
  271.0 32.4 %collective-permute-start.18 = (f32[4,5,64,128]{3,2,1,0:T(8,128)S(1)}, f32[4,5,64,128]{3,2,1,0:T(8,128)S(1)}, u32[]{:S(2)}, u32[]{:S(2)}) collective-permute-start(f32[4,5,64,128]{3,2,1,0:T(8,128)S(1)} %get-tuple-element.229), channel_id=1, source_target_pairs={{0,64},{32,96},{64,0},{96,32},{1,65},{33,97},{65,1},{97,33},{2,66}... | collective-permute-start | bytes 1966088 | tf_op jit(solution)/shard_map/ppermute | solution.py:1001
  273.0 31.0 %collective-permute-start.19 = (f32[4,5,64,128]{3,2,1,0:T(8,128)S(1)}, f32[4,5,64,128]{3,2,1,0:T(8,128)S(1)}, u32[]{:S(2)}, u32[]{:S(2)}) collective-permute-start(f32[4,5,64,128]{3,2,1,0:T(8,128)S(1)} %get-tuple-element.228), channel_id=1, source_target_pairs={{0,96},{32,0},{64,32},{96,64},{1,97},{33,1},{65,33},{97,65},{2,98}... | collective-permute-start | bytes 1966088 | tf_op jit(solution)/shard_map/ppermute | solution.py:1001
  (14 other events, 28.7 us)
